TPU v7x, 32 devices: a whole 2x2x4 slice. The times are simulated.
32 devices in a mesh: dp: 8 (over y, x, core), tensor: 4 (over z).
Axes of the slice: x: 2, y: 2, z: 4, core: 2. Of those that a mesh axis runs over, the one named last changes fastest.
Arguments:
- activations: bfloat16 [4096, 4096], P(('dp', 'tensor')), may hold values from -6 to 6
- value_weight: bfloat16 [4096, 512], P('tensor'), may hold values from -0.09375 to 0.09375
- value_cotangent: bfloat16 [4096, 512], P(('dp', 'tensor')), may hold values from -6 to 6
Outputs:
- value_proj: bfloat16 [4096, 512], P(('dp', 'tensor'))
- input_grad: bfloat16 [4096, 4096], P(('dp', 'tensor'))
- weight_grad: float32 [4096, 512], P(('tensor', 'dp'))
All inputs are finite; a program needn't handle non-finite values.
Results may differ from a plain program's by a relative error of at most 0.001.
Values may be sent and summed in bfloat16 or wider, within the bound.
No kernel may reach another device: no remote copies, remote signals or barrier semaphores. Data moves between devices by JAX's collectives and lax.ppermute only.
A program may use at most 64 MiB of HBM per device.

v0:
```python
import jax
import jax.numpy as jnp
from jax import lax
from jax.sharding import PartitionSpec as P


def per_device(activations, value_weight, value_cotangent):
    tok_rows = activations.shape[0]
    full_weight = lax.all_gather(value_weight, "tensor", axis=0, tiled=True)
    out_sum = jnp.dot(activations, full_weight, preferred_element_type=jnp.float32)
    grad_cols = lax.dot_general(
        value_cotangent, full_weight, (((1,), (1,)), ((), ())), preferred_element_type=jnp.float32
    )
    value_proj = out_sum.astype(jnp.bfloat16)
    input_grad = grad_cols.astype(jnp.bfloat16)
    own_columns = lax.all_to_all(activations, "tensor", split_axis=1, concat_axis=0, tiled=True)
    group_term = lax.dot_general(
        own_columns,
        lax.all_gather(value_cotangent, "tensor", axis=0, tiled=True),
        (((0,), (0,)), ((), ())),
        preferred_element_type=jnp.float32,
    )
    summed = lax.psum_scatter(group_term, "dp", scatter_dimension=0, tiled=True)
    total_tokens = tok_rows * lax.axis_size("dp") * lax.axis_size("tensor")
    weight_grad = summed / jnp.sqrt(jnp.float32(total_tokens))
    return (value_proj, input_grad, weight_grad)


def solution(mesh):
    placed = (P(("dp", "tensor"), None), P("tensor", None), P(("dp", "tensor"), None))
    return jax.shard_map(
        per_device,
        mesh=mesh,
        in_specs=placed,
        out_specs=(P(("dp", "tensor"), None), P(("dp", "tensor"), None), P(("tensor", "dp"), None)),
        check_vma=False,
    )
```

profile of v0, /device:TPU:0, one launch (start us, length us, event | category | flops | bytes accessed | tf_op | source)
XLA Modules:
  0.0 152.6 jit_solution(17244997506182844089)
XLA Ops:
  8.0 0.0 copy-start.2
  8.0 2.3 %copy.6 = bf16[128,4096]{0,1:T(8,128)(2,1)} copy(bf16[128,4096]{1,0:T(8,128)(2,1)} %param.3) | data formatting | bytes 2097152 | tf_op args[0]
  10.3 6.3 %all-to-all-start = ((bf16[128,4,1024]{0,2,1:T(8,128)(2,1)}), bf16[128,4,1024]{0,2,1:T(8,128)(2,1)S(1)}, u32[]{:S(2)}, u32[]{:S(2)}) async-start(bf16[128,4,1024]{0,2,1:T(8,128)(2,1)} %bitcast), calls=%async_computation | async-start | bytes 2097152 | tf_op jit(solution)/shard_map/all_to_all | solution.py:16
  16.6 0.0 reduce-scatter.2.cloned.1.call-start
  16.6 0.0 copy-done.2
  16.6 36.1 %all_gather.7 = bf16[512,512]{1,0:T(8,128)(2,1)S(1)} all-gather(bf16[128,512]{1,0:T(8,128)(2,1)S(1)} %copy-done.2), channel_id=1, replica_groups=mesh['dp'=8,'tensor'=4] {'tensor'}, dimensions={0}, use_global_device_ids=true | all-gather | bytes 655360 | tf_op jit(solution)/shard_map/all_gather | solution.py:19
  52.7 0.0 all-to-all-done
  52.7 0.5 copy.7
  53.2 0.0 copy-start.1
  53.2 2.1 %fusion = f32[1024,512]{1,0:T(8,128)} fusion(bf16[512,1024]{1,0:T(8,128)(2,1)S(1)} %bitcast.9, bf16[512,512]{1,0:T(8,128)(2,1)S(1)} %all_gather.7), kind=kOutput, calls=%fused_computation.3 | convolution fusion | flops 536870912 | bytes 3670016 | tf_op jit(solution)/shard_map/dot_general | solution.py:17
  55.3 0.0 reduce-scatter.2.cloned.1.call-update
  55.3 0.0 all-gather.2.cloned.1.call-start
  55.4 0.5 all-gather.2.cloned.1.call-update
  55.9 41.8 %reduce-scatter.2.cloned.1.call-done = f32[128,512]{1,0:T(8,128)} async-done(((f32[1024,512]{1,0:T(8,128)}), f32[128,512]{1,0:T(8,128)}) %reduce-scatter.2.cloned.1.call-update) | async-done | bytes 262160 | tf_op jit(solution)/shard_map/reduce_scatter | solution.py:23
  97.7 1.7 %broadcast_multiply_fusion = f32[128,512]{1,0:T(8,128)} fusion(f32[128,512]{1,0:T(8,128)} %reduce-scatter.2.cloned.1.call-done), kind=kLoop, calls=%fused_computation.2 | loop fusion | flops 65536 | bytes 524288 | tf_op jit(solution)/shard_map/div | solution.py:25
  99.4 39.6 %all-gather.2.cloned.1.call-done = bf16[4096,512]{1,0:T(8,128)(2,1)} async-done(((bf16[1024,512]{1,0:T(8,128)(2,1)}), bf16[4096,512]{1,0:T(8,128)(2,1)}) %all-gather.2.cloned.1.call-update) | async-done | bytes 4194320 | tf_op jit(solution)/shard_map/all_gather | solution.py:9
  139.0 0.0 copy-done.1
  139.0 0.0 copy-start
  139.0 3.7 %convolution_convert_fusion.1 = bf16[128,512]{1,0:T(8,128)(2,1)} fusion(bf16[128,4096]{1,0:T(8,128)(2,1)S(1)} %copy-done.1, bf16[4096,512]{1,0:T(8,128)(2,1)} %all-gather.2.cloned.1.call-done), kind=kOutput, calls=%fused_computation.1 | convolution fusion | flops 536936448 | bytes 5373952 | tf_op jit(solution)/shard_map/dot_general | solution.py:10
  142.7 0.0 copy-done
  142.7 2.4 %convolution_convert_fusion = bf16[128,4096]{1,0:T(8,128)(2,1)} fusion(bf16[128,512]{1,0:T(8,128)(2,1)S(1)} %copy-done.2, bf16[4096,512]{1,0:T(8,128)(2,1)S(1)} %copy-done), kind=kOutput, calls=%fused_computation | convolution fusion | flops 537395200 | bytes 5373952 | tf_op jit(solution)/shard_map/dot_general | solution.py:11
Async XLA Ops:
  8.0 8.6 %copy-start.2 = (bf16[128,512]{1,0:T(8,128)(2,1)S(1)}, bf16[128,512]{1,0:T(8,128)(2,1)}, u32[]{:S(2)}) copy-start(bf16[128,512]{1,0:T(8,128)(2,1)} %param.5) | copy-start | bytes 393220
  10.3 42.4 %all-to-all-start = ((bf16[128,4,1024]{0,2,1:T(8,128)(2,1)}), bf16[128,4,1024]{0,2,1:T(8,128)(2,1)S(1)}, u32[]{:S(2)}, u32[]{:S(2)}) async-start(bf16[128,4,1024]{0,2,1:T(8,128)(2,1)} %bitcast), calls=%async_computation | async-start | bytes 2097152 | tf_op jit(solution)/shard_map/all_to_all | solution.py:16
  16.6 81.1 %reduce-scatter.2.cloned.1.call-start = ((), (), s32[]{:S(2)}) async-start(), calls=%async_computation.3 | async-start | bytes 2359296 | tf_op jit(solution)/shard_map/reduce_scatter | solution.py:23
  53.2 85.8 %copy-start.1 = (bf16[128,4096]{1,0:T(8,128)(2,1)S(1)}, bf16[128,4096]{1,0:T(8,128)(2,1)}, u32[]{:S(2)}) copy-start(bf16[128,4096]{1,0:T(8,128)(2,1)} %param.3) | copy-start | bytes 3145732
  55.3 83.7 %all-gather.2.cloned.1.call-start = ((), (), s32[]{:S(2)}) async-start(), calls=%async_computation.2 | async-start | bytes 5242880 | tf_op jit(solution)/shard_map/all_gather | solution.py:9
  139.0 3.7 %copy-start = (bf16[4096,512]{1,0:T(8,128)(2,1)S(1)}, bf16[4096,512]{1,0:T(8,128)(2,1)}, u32[]{:S(2)}) copy-start(bf16[4096,512]{1,0:T(8,128)(2,1)} %all-gather.2.cloned.1.call-done) | copy-start | bytes 12582916
Sparse Core Ops, SparseCore 0:
  55.5 42.1 reduce-scatter.1
Sparse Core Ops, SparseCore 1:
  57.4 81.6 all-gather.1
where the time goes:
time: 153 us
  waiting for transfers between devices  81.9 us (54%)
  blocking collectives  36.1 us (24%)
  between operations  15.5 us (10%)
  matrix products  8.22 us (5%)
  starting transfers between devices  6.36 us (4%)
  local copies, waits for them, and re-layouts  2.84 us (2%)
  other arithmetic  1.67 us (1%)
    reduce_scatter x1, waiting for transfers between devices, per_device(): summed = lax.psum_scatter(group_term, 'dp', scatter_dimension=0, tiled=True)  41.8 us
    all_gather x1, waiting for transfers between devices, per_device(): full_weight = lax.all_gather(value_weight, 'tensor', axis=0, tiled=True)  39.6 us
    all_gather x1, blocking collectives, per_device(): lax.all_gather(value_cotangent, 'tensor', axis=0, tiled=True)  36.1 us
    all_to_all x1, starting transfers between devices, per_device(): lax.all_to_all(activations, 'tensor', split_axis=1, concat_axis=0, tiled=...  6.32 us
    dot_general x1, matrix products, per_device(): jnp.dot(activations, full_weight, preferred_element_type=jnp.float32)  3.71 us
  transfers between devices with their start and end apart: 3, of which 2 were waited for; matrix products, arithmetic and copies ran while one was open for 1% of the time, Pallas kernels for 0%

commit v1 on v0

v1 whole, which is shorter than its diff:
```python
import functools

import jax
import jax.numpy as jnp
from jax import lax
from jax.experimental import pallas as pl
from jax.experimental.pallas import tpu as pltpu
from jax.sharding import PartitionSpec as P

LANES = 128
AXES = ("dp", "tensor")


def contract(a, b, dim_a, dim_b):
    return lax.dot_general(a, b, (((dim_a,), (dim_b,)), ((), ())), preferred_element_type=jnp.float32)


def gathered_form(activations, value_weight, value_cotangent):
    tok_rows = activations.shape[0]
    full_weight = lax.all_gather(value_weight, "tensor", axis=0, tiled=True)
    value_proj = contract(activations, full_weight, 1, 0).astype(jnp.bfloat16)
    input_grad = contract(value_cotangent, full_weight, 1, 1).astype(jnp.bfloat16)
    own_columns = lax.all_to_all(activations, "tensor", split_axis=1, concat_axis=0, tiled=True)
    group_term = contract(own_columns, lax.all_gather(value_cotangent, "tensor", axis=0, tiled=True), 0, 0)
    summed = lax.psum_scatter(group_term, "dp", scatter_dimension=0, tiled=True)
    total_tokens = tok_rows * lax.axis_size("dp") * lax.axis_size("tensor")
    return value_proj, input_grad, summed / jnp.sqrt(jnp.float32(total_tokens))


def exchange(x, n_dp, n_tensor, dp_xor, tensor_xor):
    pairs = [(d * n_tensor + t, (d ^ dp_xor) * n_tensor + (t ^ tensor_xor)) for d in range(n_dp) for t in range(n_tensor)]
    return lax.ppermute(x, AXES, pairs)


def kernel_call(body, out_shapes, args, in_specs=None, name=None, flops=0):
    size = sum(a.size * a.dtype.itemsize for a in args) + sum(o.size * o.dtype.itemsize for o in out_shapes)
    whole = pl.BlockSpec(memory_space=pltpu.VMEM)
    return pl.pallas_call(
        body,
        out_shape=out_shapes,
        in_specs=in_specs or [whole] * len(args),
        out_specs=[whole] * len(out_shapes),
        compiler_params=pltpu.CompilerParams(vmem_limit_bytes=32 * 1024 * 1024),
        cost_estimate=pl.CostEstimate(flops=flops, bytes_accessed=size, transcendentals=0),
        name=name,
    )(*args)


def paired_form(n_dp, n_tensor, activations, value_weight, value_cotangent):
    tok, depth = activations.shape
    vdim = value_cotangent.shape[1]
    blk = depth // (n_dp * n_tensor)
    chips = n_dp // 2
    swap = functools.partial(exchange, n_dp=n_dp, n_tensor=n_tensor)
    bf16, f32 = jnp.bfloat16, jnp.float32

    def column(quarter, chip, core=0):
        return pl.multiple_of(((quarter * chips + chip) * 2 + core) * blk, LANES)

    def place():
        d = lax.axis_index("dp")
        return d // 2, d % 2, lax.axis_index("tensor")

    far = list(range(n_tensor // 2, n_tensor))
    near = list(range(n_tensor // 2))

    def pack(js, with_cot):
        def body(act, cot, *outs):
            p, _, t = place()
            for q, out in enumerate(outs, 1):
                for i, j in enumerate(js):
                    out[:, i * 2 * blk : (i + 1) * 2 * blk] = act[:, pl.ds(column(t ^ j, p ^ q), 2 * blk)]
                if with_cot:
                    out[:, len(js) * 2 * blk :] = cot[...]

        width = len(js) * 2 * blk + (vdim if with_cot else 0)
        shapes = [jax.ShapeDtypeStruct((tok, width), bf16)] * (chips - 1)
        return kernel_call(body, shapes, [activations, value_cotangent], name="pack")

    def partial_sums(js, strips, cots):
        n = chips - 1

        def body(act, cot, *refs):
            strip_refs, cot_refs, (keep, send) = refs[:n], refs[n : 2 * n], refs[2 * n :]
            p, c, t = place()
            all_cots = jnp.concatenate([cot[...]] + [r[:, far_width:] for r in cot_refs], axis=0)
            for i, j in enumerate(js):
                for out, core in ((send, 1 - c), (keep, c)):
                    start = pl.multiple_of(i * 2 * blk + core * blk, LANES)
                    parts = [act[:, pl.ds(column(t ^ j, p, core), blk)]] + [r[:, pl.ds(start, blk)] for r in strip_refs]
                    out[i * blk : (i + 1) * blk, :] = contract(jnp.concatenate(parts, axis=0), all_cots, 0, 0)

        shape = jax.ShapeDtypeStruct((len(js) * blk, vdim), f32)
        flops = 4 * len(js) * blk * vdim * tok * chips
        return kernel_call(body, [shape, shape], [activations, value_cotangent, *strips, *cots], name="partial_sums", flops=flops)

    far_width = len(far) * 2 * blk

    own_slice = lax.dynamic_slice_in_dim(value_weight, lax.axis_index("dp") * blk, blk, 0)
    slices = [swap(own_slice, dp_xor=0, tensor_xor=j) for j in range(1, n_tensor)]
    far_got = [swap(x, dp_xor=2 * q, tensor_xor=0) for q, x in enumerate(pack(far, True), 1)]
    near_got = [swap(x, dp_xor=2 * q, tensor_xor=0) for q, x in enumerate(pack(near, False), 1)]
    mine = jnp.concatenate(slices, axis=0)
    weight_got = [mine] + [swap(mine, dp_xor=2 * q, tensor_xor=0) for q in range(1, chips)]
    weight_twin = [swap(x, dp_xor=1, tensor_xor=0) for x in weight_got]

    far_keep, far_send = partial_sums(far, far_got, far_got)
    far_sum = far_keep + swap(far_send, dp_xor=1, tensor_xor=0)
    terms = [swap(far_sum[i * blk : (i + 1) * blk], dp_xor=0, tensor_xor=j) for i, j in enumerate(far)]
    near_keep, near_send = partial_sums(near, near_got, far_got)
    near_sum = near_keep + swap(near_send, dp_xor=1, tensor_xor=0)
    terms += [swap(near_sum[i * blk : (i + 1) * blk], dp_xor=0, tensor_xor=j) for i, j in enumerate(near) if j]
    summed = near_sum[:blk]
    for term in terms:
        summed = summed + term
    weight_grad = summed / jnp.sqrt(f32(tok * n_dp * n_tensor))

    quarter = depth // n_tensor

    def quarter_body(act, cot, w, acc, grad):
        _, _, t = place()
        acc[...] = contract(act[:, pl.ds(pl.multiple_of(t * quarter, LANES), quarter)], w[...], 1, 0)
        grad[...] = contract(cot[...], w[...], 1, 1).astype(bf16)

    acc, quarter_grad = kernel_call(
        quarter_body,
        [jax.ShapeDtypeStruct((tok, vdim), f32), jax.ShapeDtypeStruct((tok, quarter), bf16)],
        [activations, value_cotangent, value_weight],
        name="own_quarter",
        flops=4 * tok * vdim * quarter,
    )

    def rest_body(act, cot, acc, quarter_grad, *refs):
        got, twin, (proj, grad) = refs[:chips], refs[chips : 2 * chips], refs[2 * chips :]
        p, c, t = place()
        grad[:, pl.ds(pl.multiple_of(t * quarter, LANES), quarter)] = quarter_grad[...]
        total = acc[...]
        for q in range(chips):
            for j in range(1, n_tensor):
                for ref, core in ((got[q], c), (twin[q], 1 - c)):
                    w = ref[(j - 1) * blk : j * blk, :]
                    cols = pl.ds(column(t ^ j, p ^ q, core), blk)
                    total += contract(act[:, cols], w, 1, 0)
                    grad[:, cols] = contract(cot[...], w, 1, 1).astype(bf16)
        proj[...] = total.astype(bf16)

    value_proj, input_grad = kernel_call(
        rest_body,
        [jax.ShapeDtypeStruct((tok, vdim), bf16), jax.ShapeDtypeStruct((tok, depth), bf16)],
        [activations, value_cotangent, acc, quarter_grad, *weight_got, *weight_twin],
        name="other_quarters",
        flops=4 * tok * vdim * (depth - quarter),
    )
    return value_proj, input_grad, weight_grad


def solution(mesh):
    n_dp, n_tensor = mesh.shape["dp"], mesh.shape["tensor"]

    def per_device(activations, value_weight, value_cotangent):
        tok, depth = activations.shape
        powers = all(n > 1 and n & (n - 1) == 0 for n in (n_dp, n_tensor))
        if powers and depth % (n_dp * n_tensor * LANES) == 0 and tok % LANES == 0:
            return paired_form(n_dp, n_tensor, activations, value_weight, value_cotangent)
        return gathered_form(activations, value_weight, value_cotangent)

    return jax.shard_map(
        per_device,
        mesh=mesh,
        in_specs=(P(AXES, None), P("tensor", None), P(AXES, None)),
        out_specs=(P(AXES, None), P(AXES, None), P(("tensor", "dp"), None)),
        check_vma=False,
    )
```

time: 153 us -> 77.6 us (0.51)
  waiting for transfers between devices: 81.9 us -> 44.9 us
  blocking collectives: 36.1 us -> 0 us
  starting transfers between devices: 6.36 us -> 24 us
  between operations: 15.5 us -> 0.79 us
  matrix products: 8.22 us -> 0 us
  Pallas kernels: 0 us -> 4.54 us
    ppermute x0 -> x21, waiting for transfers between devices: none -> 44.9 us  [exchange(): return lax.ppermute(x, AXES, pairs)]
    reduce_scatter x1 -> x0, waiting for transfers between devices: 41.8 us -> none  [per_device(): summed = lax.psum_scatter(group_term, 'dp', scatter_dimension=0, tiled=True)]
    all_gather x1 -> x0, waiting for transfers between devices: 39.6 us -> none  [per_device(): full_weight = lax.all_gather(value_weight, 'tensor', axis=0, tiled=True)]
    all_gather x1 -> x0, blocking collectives: 36.1 us -> none  [per_device(): lax.all_gather(value_cotangent, 'tensor', axis=0, tiled=True)]
    ppermute x0 -> x21, starting transfers between devices: none -> 24 us  [exchange(): return lax.ppermute(x, AXES, pairs)]
    dot_general x3 -> x0, matrix products: 8.22 us -> none  [the longest x1 3.71 us: per_device(): jnp.dot(activations, full_weight, preferred_element_type=jnp.float32)]
    all_to_all x1 -> x0, starting transfers between devices: 6.32 us -> none  [per_device(): lax.all_to_all(activations, 'tensor', split_axis=1, concat_axis=0, tiled=...]
    pallas_call x0 -> x6, Pallas kernels: none -> 4.54 us  [kernel_call(): pl.pallas_call(body, out_shape=out_shapes, in_specs=in_specs or [whole] *...]
  transfers between devices with their start and end apart: 3 -> 21, of which waited for: 2 -> 7; matrix products, arithmetic and copies ran while one was open for 1% -> 0% of each run, Pallas kernels for 0% -> 6%
where the time goes in v1:
time: 77.6 us; the launch traced here: 77.4 us
  waiting for transfers between devices  44.9 us (58%)
  starting transfers between devices  24 us (31%)
  Pallas kernels  4.54 us (6%)
  local copies, waits for them, and re-layouts  2.27 us (3%)
  other arithmetic  0.95 us (1%)
  between operations  0.79 us (1%)
    ppermute x21, waiting for transfers between devices, exchange(): return lax.ppermute(x, AXES, pairs)  44.9 us
    ppermute x21, starting transfers between devices, exchange(): return lax.ppermute(x, AXES, pairs)  24 us
    pallas_call x6, Pallas kernels, kernel_call(): pl.pallas_call(body, out_shape=out_shapes, in_specs=in_specs or [whole] *...  4.54 us
  transfers between devices with their start and end apart: 21, of which 7 were waited for; matrix products, arithmetic and copies ran while one was open for 0% of the time, Pallas kernels for 6%

profile of v1, /device:TPU:0, one launch (start us, length us, event | category | flops | bytes accessed | tf_op | source)
XLA Modules:
  0.0 77.4 jit_solution(4174615379414108377)
XLA Ops:
  0.6 1.0 %constant_dynamic-slice_fusion = bf16[128,512]{1,0:T(8,128)(2,1)S(1)} fusion(bf16[1024,512]{1,0:T(8,128)(2,1)} %w.1, s32[]{:T(128)S(6)} %select_n.3), kind=kLoop, calls=%fused_computation.7 | loop fusion | bytes 262148 | tf_op jit(solution)/shard_map/dynamic_slice | solution.py:99
  1.6 3.1 %collective-permute-start = (bf16[128,512]{1,0:T(8,128)(2,1)S(1)}, bf16[128,512]{1,0:T(8,128)(2,1)S(1)}, u32[]{:S(2)}, u32[]{:S(2)}) collective-permute-start(bf16[128,512]{1,0:T(8,128)(2,1)S(1)} %constant_dynamic-slice_fusion), channel_id=1, source_target_pairs={{0,1},{1,0},{2,3},{3,2},{4,5},{5,4},{6,7},{7,6},{8,9},{9,8},{10,11... | collective-permute-start | bytes 393224 | tf_op jit(solution)/shard_map/ppermute | solution.py:32
  4.7 2.6 %collective-permute-start.1 = (bf16[128,512]{1,0:T(8,128)(2,1)S(1)}, bf16[128,512]{1,0:T(8,128)(2,1)S(1)}, u32[]{:S(2)}, u32[]{:S(2)}) collective-permute-start(bf16[128,512]{1,0:T(8,128)(2,1)S(1)} %constant_dynamic-slice_fusion), channel_id=1, source_target_pairs={{0,2},{1,3},{2,0},{3,1},{4,6},{5,7},{6,4},{7,5},{8,10},{9,11},{10,... | collective-permute-start | bytes 393224 | tf_op jit(solution)/shard_map/ppermute | solution.py:32
  7.3 1.2 %copy-done = bf16[128,4096]{1,0:T(8,128)(2,1)S(1)} copy-done((bf16[128,4096]{1,0:T(8,128)(2,1)S(1)}, bf16[128,4096]{1,0:T(8,128)(2,1)}, u32[]{:S(2)}) %copy-start) | copy-done | bytes 1048600
  8.6 1.8 %collective-permute-start.10 = (bf16[128,512]{1,0:T(8,128)(2,1)S(1)}, bf16[128,512]{1,0:T(8,128)(2,1)S(1)}, u32[]{:S(2)}, u32[]{:S(2)}) collective-permute-start(bf16[128,512]{1,0:T(8,128)(2,1)S(1)} %get-tuple-element.21), channel_id=1, source_target_pairs={{0,8},{1,9},{2,10},{3,11},{4,12},{5,13},{6,14},{7,15},{8,0},{9,1},... | collective-permute-start | bytes 393224 | tf_op jit(solution)/shard_map/ppermute | solution.py:32
  10.8 1.7 %collective-permute-start.14 = (bf16[128,1024]{1,0:T(8,128)(2,1)S(1)}, bf16[128,1024]{1,0:T(8,128)(2,1)S(1)}, u32[]{:S(2)}, u32[]{:S(2)}) collective-permute-start(bf16[128,1024]{1,0:T(8,128)(2,1)S(1)} %get-tuple-element.25), channel_id=1, source_target_pairs={{0,16},{1,17},{2,18},{3,19},{4,20},{5,21},{6,22},{7,23},{8,24},{9,... | collective-permute-start | bytes 786440 | tf_op jit(solution)/shard_map/ppermute | solution.py:32
  12.6 5.1 %collective-permute-done.1 = bf16[128,512]{1,0:T(8,128)(2,1)S(1)} collective-permute-done((bf16[128,512]{1,0:T(8,128)(2,1)S(1)}, bf16[128,512]{1,0:T(8,128)(2,1)S(1)}, u32[]{:S(2)}, u32[]{:S(2)}) %collective-permute-start.1) | collective-permute-done | bytes 131104 | tf_op jit(solution)/shard_map/ppermute | solution.py:32
  17.6 2.4 %collective-permute-start.15 = (bf16[128,1024]{1,0:T(8,128)(2,1)S(1)}, bf16[128,1024]{1,0:T(8,128)(2,1)S(1)}, u32[]{:S(2)}, u32[]{:S(2)}) collective-permute-start(bf16[128,1024]{1,0:T(8,128)(2,1)S(1)} %get-tuple-element.26), channel_id=1, source_target_pairs={{0,24},{1,25},{2,26},{3,27},{4,28},{5,29},{6,30},{7,31},{8,16},{9,... | collective-permute-start | bytes 786440 | tf_op jit(solution)/shard_map/ppermute | solution.py:32
  20.1 0.6 collective-permute-start.11
  20.7 1.5 %collective-permute-start.12 = (bf16[128,512]{1,0:T(8,128)(2,1)S(1)}, bf16[128,512]{1,0:T(8,128)(2,1)S(1)}, u32[]{:S(2)}, u32[]{:S(2)}) collective-permute-start(bf16[128,512]{1,0:T(8,128)(2,1)S(1)} %get-tuple-element.23), channel_id=1, source_target_pairs={{0,24},{1,25},{2,26},{3,27},{4,28},{5,29},{6,30},{7,31},{8,16},{9,... | collective-permute-start | bytes 393224 | tf_op jit(solution)/shard_map/ppermute | solution.py:32
  22.2 8.4 %collective-permute-done.11.refs_1_ = bf16[128,512]{1,0:T(8,128)(2,1)S(1)} collective-permute-done((bf16[128,512]{1,0:T(8,128)(2,1)S(1)}, bf16[128,512]{1,0:T(8,128)(2,1)S(1)}, u32[]{:S(2)}, u32[]{:S(2)}) %collective-permute-start.11) | collective-permute-done | bytes 131104 | tf_op jit(solution)/shard_map/ppermute | solution.py:32
  30.6 1.5 %collective-permute-start.3 = (bf16[384,512]{1,0:T(8,128)(2,1)S(1)}, bf16[384,512]{1,0:T(8,128)(2,1)S(1)}, u32[]{:S(2)}, u32[]{:S(2)}) collective-permute-start(bf16[384,512]{1,0:T(8,128)(2,1)S(1)} %constant_dynamic-update-slice_fusion.refs_0_), channel_id=1, source_target_pairs={{0,8},{1,9},{2,10},{3,11},{4,12},{5,13},{6,14},{7,15},{8,0},{9,1},... | collective-permute-start | bytes 1179656 | tf_op jit(solution)/shard_map/ppermute | solution.py:32
  33.2 0.6 collective-permute-start.17
  33.7 2.0 %collective-permute-start.5 = (bf16[384,512]{1,0:T(8,128)(2,1)S(1)}, bf16[384,512]{1,0:T(8,128)(2,1)S(1)}, u32[]{:S(2)}, u32[]{:S(2)}) collective-permute-start(bf16[384,512]{1,0:T(8,128)(2,1)S(1)} %constant_dynamic-update-slice_fusion.refs_0_), channel_id=1, source_target_pairs={{0,24},{1,25},{2,26},{3,27},{4,28},{5,29},{6,30},{7,31},{8,16},{9,... | collective-permute-start | bytes 1179656 | tf_op jit(solution)/shard_map/ppermute | solution.py:32
  35.7 3.1 %collective-permute-done.3.refs_1_ = bf16[384,512]{1,0:T(8,128)(2,1)S(1)} collective-permute-done((bf16[384,512]{1,0:T(8,128)(2,1)S(1)}, bf16[384,512]{1,0:T(8,128)(2,1)S(1)}, u32[]{:S(2)}, u32[]{:S(2)}) %collective-permute-start.3) | collective-permute-done | bytes 393248 | tf_op jit(solution)/shard_map/ppermute | solution.py:32
  38.8 9.5 %collective-permute-done.4.refs_2_ = bf16[384,512]{1,0:T(8,128)(2,1)S(1)} collective-permute-done((bf16[384,512]{1,0:T(8,128)(2,1)S(1)}, bf16[384,512]{1,0:T(8,128)(2,1)S(1)}, u32[]{:S(2)}, u32[]{:S(2)}) %collective-permute-start.4) | collective-permute-done | bytes 393248 | tf_op jit(solution)/shard_map/ppermute | solution.py:32
  49.0 2.5 %collective-permute-start.20 = (f32[128,512]{1,0:T(8,128)S(1)}, f32[128,512]{1,0:T(8,128)S(1)}, u32[]{:S(2)}, u32[]{:S(2)}) collective-permute-start(f32[128,512]{1,0:T(8,128)S(1)} %slice.19), channel_id=1, source_target_pairs={{0,1},{1,0},{2,3},{3,2},{4,5},{5,4},{6,7},{7,6},{8,9},{9,8},{10,11... | collective-permute-start | bytes 786440 | tf_op jit(solution)/shard_map/ppermute | solution.py:32
  51.6 2.7 %collective-permute-start.19 = (f32[128,512]{1,0:T(8,128)S(1)}, f32[128,512]{1,0:T(8,128)S(1)}, u32[]{:S(2)}, u32[]{:S(2)}) collective-permute-start(f32[128,512]{1,0:T(8,128)S(1)} %get-tuple-element.32), channel_id=1, source_target_pairs={{0,3},{1,2},{2,1},{3,0},{4,7},{5,6},{6,5},{7,4},{8,11},{9,10},{10,... | collective-permute-start | bytes 786440 | tf_op jit(solution)/shard_map/ppermute | solution.py:32
  54.3 0.6 own_quarter.1
  55.0 2.8 %other_quarters.1 = (bf16[128,512]{1,0:T(8,128)(2,1)}, bf16[128,4096]{1,0:T(8,128)(2,1)}) custom-call(bf16[128,4096]{1,0:T(8,128)(2,1)S(1)} %copy-done, bf16[128,512]{1,0:T(8,128)(2,1)S(1)} %copy-done.1, f32[128,512]{1,0:T(8,128)S(1)} %get-tuple-element.17.acc, bf16[128,1024]{1,0:T(8,128)(2,1)S(1)} %get-tuple-element.18.quarter_grad, ...), custom_call_target="tpu_custom_call" | custom-call | flops 805306368 | bytes 6029312 | tf_op jit(solution)/shard_map/other_quarters/pallas_call | solution.py:38
  57.8 0.6 collective-permute-done.20
  58.4 8.6 %collective-permute-done.19 = f32[128,512]{1,0:T(8,128)S(1)} collective-permute-done((f32[128,512]{1,0:T(8,128)S(1)}, f32[128,512]{1,0:T(8,128)S(1)}, u32[]{:S(2)}, u32[]{:S(2)}) %collective-permute-start.19) | collective-permute-done | bytes 262176 | tf_op jit(solution)/shard_map/ppermute | solution.py:32
  66.9 9.7 %collective-permute-done.18 = f32[128,512]{1,0:T(8,128)S(1)} collective-permute-done((f32[128,512]{1,0:T(8,128)S(1)}, f32[128,512]{1,0:T(8,128)S(1)}, u32[]{:S(2)}, u32[]{:S(2)}) %collective-permute-start.18) | collective-permute-done | bytes 262176 | tf_op jit(solution)/shard_map/ppermute | solution.py:32
  76.6 0.8 %fusion.2 = f32[128,512]{1,0:T(8,128)} fusion(f32[128,512]{1,0:T(8,128)S(1)} %collective-permute-done.20, f32[128,512]{1,0:T(8,128)S(1)} %collective-permute-done.19, f32[128,512]{1,0:T(8,128)S(1)} %collective-permute-done.18, f32[256,512]{1,0:T(8,128)S(1)} %add.19), kind=kLoop, calls=%fused_computation.3 | loop fusion | flops 262144 | bytes 1310720 | tf_op jit(solution)/shard_map/div | solution.py:116
  (39 shorter events, 2.5 us)
Async XLA Ops:
  0.6 6.7 %copy-start.1 = (bf16[128,512]{1,0:T(8,128)(2,1)S(1)}, bf16[128,512]{1,0:T(8,128)(2,1)}, u32[]{:S(2)}) copy-start(bf16[128,512]{1,0:T(8,128)(2,1)} %cot.11) | copy-start | bytes 393220
  1.6 9.2 %collective-permute-start = (bf16[128,512]{1,0:T(8,128)(2,1)S(1)}, bf16[128,512]{1,0:T(8,128)(2,1)S(1)}, u32[]{:S(2)}, u32[]{:S(2)}) collective-permute-start(bf16[128,512]{1,0:T(8,128)(2,1)S(1)} %constant_dynamic-slice_fusion), channel_id=1, source_target_pairs={{0,1},{1,0},{2,3},{3,2},{4,5},{5,4},{6,7},{7,6},{8,9},{9,8},{10,11... | collective-permute-start | bytes 393224 | tf_op jit(solution)/shard_map/ppermute | solution.py:32
  4.7 12.9 %collective-permute-start.1 = (bf16[128,512]{1,0:T(8,128)(2,1)S(1)}, bf16[128,512]{1,0:T(8,128)(2,1)S(1)}, u32[]{:S(2)}, u32[]{:S(2)}) collective-permute-start(bf16[128,512]{1,0:T(8,128)(2,1)S(1)} %constant_dynamic-slice_fusion), channel_id=1, source_target_pairs={{0,2},{1,3},{2,0},{3,1},{4,6},{5,7},{6,4},{7,5},{8,10},{9,11},{10,... | collective-permute-start | bytes 393224 | tf_op jit(solution)/shard_map/ppermute | solution.py:32
  7.3 12.8 %collective-permute-start.2 = (bf16[128,512]{1,0:T(8,128)(2,1)S(1)}, bf16[128,512]{1,0:T(8,128)(2,1)S(1)}, u32[]{:S(2)}, u32[]{:S(2)}) collective-permute-start(bf16[128,512]{1,0:T(8,128)(2,1)S(1)} %constant_dynamic-slice_fusion), channel_id=1, source_target_pairs={{0,3},{1,2},{2,1},{3,0},{4,7},{5,6},{6,5},{7,4},{8,11},{9,10},{10,... | collective-permute-start | bytes 393224 | tf_op jit(solution)/shard_map/ppermute | solution.py:32
  7.3 1.2 %copy-start = (bf16[128,4096]{1,0:T(8,128)(2,1)S(1)}, bf16[128,4096]{1,0:T(8,128)(2,1)}, u32[]{:S(2)}) copy-start(bf16[128,4096]{1,0:T(8,128)(2,1)} %act.11) | copy-start | bytes 3145732
  8.6 12.1 %collective-permute-start.10 = (bf16[128,512]{1,0:T(8,128)(2,1)S(1)}, bf16[128,512]{1,0:T(8,128)(2,1)S(1)}, u32[]{:S(2)}, u32[]{:S(2)}) collective-permute-start(bf16[128,512]{1,0:T(8,128)(2,1)S(1)} %get-tuple-element.21), channel_id=1, source_target_pairs={{0,8},{1,9},{2,10},{3,11},{4,12},{5,13},{6,14},{7,15},{8,0},{9,1},... | collective-permute-start | bytes 393224 | tf_op jit(solution)/shard_map/ppermute | solution.py:32
  10.4 21.7 %collective-permute-start.13 = (bf16[128,1024]{1,0:T(8,128)(2,1)S(1)}, bf16[128,1024]{1,0:T(8,128)(2,1)S(1)}, u32[]{:S(2)}, u32[]{:S(2)}) collective-permute-start(bf16[128,1024]{1,0:T(8,128)(2,1)S(1)} %get-tuple-element.24), channel_id=1, source_target_pairs={{0,8},{1,9},{2,10},{3,11},{4,12},{5,13},{6,14},{7,15},{8,0},{9,1},... | collective-permute-start | bytes 786440 | tf_op jit(solution)/shard_map/ppermute | solution.py:32
  10.8 21.3 %collective-permute-start.14 = (bf16[128,1024]{1,0:T(8,128)(2,1)S(1)}, bf16[128,1024]{1,0:T(8,128)(2,1)S(1)}, u32[]{:S(2)}, u32[]{:S(2)}) collective-permute-start(bf16[128,1024]{1,0:T(8,128)(2,1)S(1)} %get-tuple-element.25), channel_id=1, source_target_pairs={{0,16},{1,17},{2,18},{3,19},{4,20},{5,21},{6,22},{7,23},{8,24},{9,... | collective-permute-start | bytes 786440 | tf_op jit(solution)/shard_map/ppermute | solution.py:32
  17.6 14.5 %collective-permute-start.15 = (bf16[128,1024]{1,0:T(8,128)(2,1)S(1)}, bf16[128,1024]{1,0:T(8,128)(2,1)S(1)}, u32[]{:S(2)}, u32[]{:S(2)}) collective-permute-start(bf16[128,1024]{1,0:T(8,128)(2,1)S(1)} %get-tuple-element.26), channel_id=1, source_target_pairs={{0,24},{1,25},{2,26},{3,27},{4,28},{5,29},{6,30},{7,31},{8,16},{9,... | collective-permute-start | bytes 786440 | tf_op jit(solution)/shard_map/ppermute | solution.py:32
  20.1 10.5 %collective-permute-start.11 = (bf16[128,512]{1,0:T(8,128)(2,1)S(1)}, bf16[128,512]{1,0:T(8,128)(2,1)S(1)}, u32[]{:S(2)}, u32[]{:S(2)}) collective-permute-start(bf16[128,512]{1,0:T(8,128)(2,1)S(1)} %get-tuple-element.22), channel_id=1, source_target_pairs={{0,16},{1,17},{2,18},{3,19},{4,20},{5,21},{6,22},{7,23},{8,24},{9,... | collective-permute-start | bytes 393224 | tf_op jit(solution)/shard_map/ppermute | solution.py:32
  20.7 11.4 %collective-permute-start.12 = (bf16[128,512]{1,0:T(8,128)(2,1)S(1)}, bf16[128,512]{1,0:T(8,128)(2,1)S(1)}, u32[]{:S(2)}, u32[]{:S(2)}) collective-permute-start(bf16[128,512]{1,0:T(8,128)(2,1)S(1)} %get-tuple-element.23), channel_id=1, source_target_pairs={{0,24},{1,25},{2,26},{3,27},{4,28},{5,29},{6,30},{7,31},{8,16},{9,... | collective-permute-start | bytes 393224 | tf_op jit(solution)/shard_map/ppermute | solution.py:32
  30.6 8.2 %collective-permute-start.3 = (bf16[384,512]{1,0:T(8,128)(2,1)S(1)}, bf16[384,512]{1,0:T(8,128)(2,1)S(1)}, u32[]{:S(2)}, u32[]{:S(2)}) collective-permute-start(bf16[384,512]{1,0:T(8,128)(2,1)S(1)} %constant_dynamic-update-slice_fusion.refs_0_), channel_id=1, source_target_pairs={{0,8},{1,9},{2,10},{3,11},{4,12},{5,13},{6,14},{7,15},{8,0},{9,1},... | collective-permute-start | bytes 1179656 | tf_op jit(solution)/shard_map/ppermute | solution.py:32
  32.1 16.2 %collective-permute-start.4 = (bf16[384,512]{1,0:T(8,128)(2,1)S(1)}, bf16[384,512]{1,0:T(8,128)(2,1)S(1)}, u32[]{:S(2)}, u32[]{:S(2)}) collective-permute-start(bf16[384,512]{1,0:T(8,128)(2,1)S(1)} %constant_dynamic-update-slice_fusion.refs_0_), channel_id=1, source_target_pairs={{0,16},{1,17},{2,18},{3,19},{4,20},{5,21},{6,22},{7,23},{8,24},{9,... | collective-permute-start | bytes 1179656 | tf_op jit(solution)/shard_map/ppermute | solution.py:32
  32.6 16.2 %collective-permute-start.16 = (f32[256,512]{1,0:T(8,128)S(1)}, f32[256,512]{1,0:T(8,128)S(1)}, u32[]{:S(2)}, u32[]{:S(2)}) collective-permute-start(f32[256,512]{1,0:T(8,128)S(1)} %get-tuple-element.28), channel_id=1, source_target_pairs={{0,4},{1,5},{2,6},{3,7},{4,0},{5,1},{6,2},{7,3},{8,12},{9,13},{10,... | collective-permute-start | bytes 1572872 | tf_op jit(solution)/shard_map/ppermute | solution.py:32
  33.2 15.8 %collective-permute-start.17 = (f32[256,512]{1,0:T(8,128)S(1)}, f32[256,512]{1,0:T(8,128)S(1)}, u32[]{:S(2)}, u32[]{:S(2)}) collective-permute-start(f32[256,512]{1,0:T(8,128)S(1)} %get-tuple-element.30), channel_id=1, source_target_pairs={{0,4},{1,5},{2,6},{3,7},{4,0},{5,1},{6,2},{7,3},{8,12},{9,13},{10,... | collective-permute-start | bytes 1572872 | tf_op jit(solution)/shard_map/ppermute | solution.py:32
  33.7 14.5 %collective-permute-start.5 = (bf16[384,512]{1,0:T(8,128)(2,1)S(1)}, bf16[384,512]{1,0:T(8,128)(2,1)S(1)}, u32[]{:S(2)}, u32[]{:S(2)}) collective-permute-start(bf16[384,512]{1,0:T(8,128)(2,1)S(1)} %constant_dynamic-update-slice_fusion.refs_0_), channel_id=1, source_target_pairs={{0,24},{1,25},{2,26},{3,27},{4,28},{5,29},{6,30},{7,31},{8,16},{9,... | collective-permute-start | bytes 1179656 | tf_op jit(solution)/shard_map/ppermute | solution.py:32
  38.8 12.8 %collective-permute-start.6 = (bf16[384,512]{1,0:T(8,128)(2,1)S(1)}, bf16[384,512]{1,0:T(8,128)(2,1)S(1)}, u32[]{:S(2)}, u32[]{:S(2)}) collective-permute-start(bf16[384,512]{1,0:T(8,128)(2,1)S(1)} %constant_dynamic-update-slice_fusion.refs_0_), channel_id=1, source_target_pairs={{0,4},{1,5},{2,6},{3,7},{4,0},{5,1},{6,2},{7,3},{8,12},{9,13},{10,... | collective-permute-start | bytes 1179656 | tf_op jit(solution)/shard_map/ppermute | solution.py:32
  48.3 6.1 %collective-permute-start.7 = (bf16[384,512]{1,0:T(8,128)(2,1)S(1)}, bf16[384,512]{1,0:T(8,128)(2,1)S(1)}, u32[]{:S(2)}, u32[]{:S(2)}) collective-permute-start(bf16[384,512]{1,0:T(8,128)(2,1)S(1)} %collective-permute-done.3.refs_1_), channel_id=1, source_target_pairs={{0,4},{1,5},{2,6},{3,7},{4,0},{5,1},{6,2},{7,3},{8,12},{9,13},{10,... | collective-permute-start | bytes 1179656 | tf_op jit(solution)/shard_map/ppermute | solution.py:32
  48.3 6.7 %collective-permute-start.8 = (bf16[384,512]{1,0:T(8,128)(2,1)S(1)}, bf16[384,512]{1,0:T(8,128)(2,1)S(1)}, u32[]{:S(2)}, u32[]{:S(2)}) collective-permute-start(bf16[384,512]{1,0:T(8,128)(2,1)S(1)} %collective-permute-done.4.refs_2_), channel_id=1, source_target_pairs={{0,4},{1,5},{2,6},{3,7},{4,0},{5,1},{6,2},{7,3},{8,12},{9,13},{10,... | collective-permute-start | bytes 1179656 | tf_op jit(solution)/shard_map/ppermute | solution.py:32
  48.8 6.2 %collective-permute-start.9 = (bf16[384,512]{1,0:T(8,128)(2,1)S(1)}, bf16[384,512]{1,0:T(8,128)(2,1)S(1)}, u32[]{:S(2)}, u32[]{:S(2)}) collective-permute-start(bf16[384,512]{1,0:T(8,128)(2,1)S(1)} %collective-permute-done.5.refs_3_), channel_id=1, source_target_pairs={{0,4},{1,5},{2,6},{3,7},{4,0},{5,1},{6,2},{7,3},{8,12},{9,13},{10,... | collective-permute-start | bytes 1179656 | tf_op jit(solution)/shard_map/ppermute | solution.py:32
  49.0 9.4 %collective-permute-start.20 = (f32[128,512]{1,0:T(8,128)S(1)}, f32[128,512]{1,0:T(8,128)S(1)}, u32[]{:S(2)}, u32[]{:S(2)}) collective-permute-start(f32[128,512]{1,0:T(8,128)S(1)} %slice.19), channel_id=1, source_target_pairs={{0,1},{1,0},{2,3},{3,2},{4,5},{5,4},{6,7},{7,6},{8,9},{9,8},{10,11... | collective-permute-start | bytes 786440 | tf_op jit(solution)/shard_map/ppermute | solution.py:32
  51.4 2.9 %copy-start.2 = (bf16[1024,512]{1,0:T(8,128)(2,1)S(1)}, bf16[1024,512]{1,0:T(8,128)(2,1)}, u32[]{:S(2)}) copy-start(bf16[1024,512]{1,0:T(8,128)(2,1)} %w.1) | copy-start | bytes 3145732
  51.6 15.3 %collective-permute-start.19 = (f32[128,512]{1,0:T(8,128)S(1)}, f32[128,512]{1,0:T(8,128)S(1)}, u32[]{:S(2)}, u32[]{:S(2)}) collective-permute-start(f32[128,512]{1,0:T(8,128)S(1)} %get-tuple-element.32), channel_id=1, source_target_pairs={{0,3},{1,2},{2,1},{3,0},{4,7},{5,6},{6,5},{7,4},{8,11},{9,10},{10,... | collective-permute-start | bytes 786440 | tf_op jit(solution)/shard_map/ppermute | solution.py:32
  54.3 22.3 %collective-permute-start.18 = (f32[128,512]{1,0:T(8,128)S(1)}, f32[128,512]{1,0:T(8,128)S(1)}, u32[]{:S(2)}, u32[]{:S(2)}) collective-permute-start(f32[128,512]{1,0:T(8,128)S(1)} %get-tuple-element.31), channel_id=1, source_target_pairs={{0,2},{1,3},{2,0},{3,1},{4,6},{5,7},{6,4},{7,5},{8,10},{9,11},{10,... | collective-permute-start | bytes 786440 | tf_op jit(solution)/shard_map/ppermute | solution.py:32

commit v2 on v0

v2 whole, which is shorter than its diff:
```python
import functools

import jax
import jax.numpy as jnp
from jax import lax
from jax.experimental import pallas as pl
from jax.experimental.pallas import tpu as pltpu
from jax.sharding import PartitionSpec as P

OPT = {'pf': 1, 's1_after3': 1, 'w_mode': 'whole', 'pack': 'vmem', 'pack_lim': 60, 's_mode': 'strip', 'z_mode': 'mix', 'e_mode': 'merged', 'sums_za': 1, 'sums_zb': 1, 'ca_zb': 1, 'mine_after': 0, 'st2_after': 1, 'e2_acc': 1, 'e2_s1': 1, 'e2_s2': 1, 'slice_after': 1, 'qtr_after': 'za', 'sums_qtr': 1, 'e1_s': 0, 'order': 'zs', 'c_pack': 0, 'c_slice': 0, 'c_zstack': 0, 'c_qtr': 0, 'c_sums1': 5, 'c_sums2': 0, 'c_join1': 0, 'c_join2': 0, 'c_joinf': 20, 'c_mine': 0, 'c_estack': 0, 'c_e2stack': 0, 'c_prod': 0, 'c_last': 0}
LANES = 128
PAD = 16
LOG2_E = 1.4426950408889634
TOP_POWER = 14.0
AXES = ("dp", "tensor")
VMEM_LIMIT = 32 * 1024 * 1024
PACK_LIMIT = 60 * 1024 * 1024


def contract(a, b, dim_a, dim_b):
    return lax.dot_general(a, b, (((dim_a,), (dim_b,)), ((), ())), preferred_element_type=jnp.float32)


def gathered_form(activations, value_weight, value_cotangent):
    tok_rows = activations.shape[0]
    full_weight = lax.all_gather(value_weight, "tensor", axis=0, tiled=True)
    value_proj = contract(activations, full_weight, 1, 0).astype(jnp.bfloat16)
    input_grad = contract(value_cotangent, full_weight, 1, 1).astype(jnp.bfloat16)
    own_columns = lax.all_to_all(activations, "tensor", split_axis=1, concat_axis=0, tiled=True)
    group_term = contract(own_columns, lax.all_gather(value_cotangent, "tensor", axis=0, tiled=True), 0, 0)
    summed = lax.psum_scatter(group_term, "dp", scatter_dimension=0, tiled=True)
    total_tokens = tok_rows * lax.axis_size("dp") * lax.axis_size("tensor")
    return value_proj, input_grad, summed / jnp.sqrt(jnp.float32(total_tokens))


def exchange(x, n_dp, n_tensor, dp_xor, tensor_xor):
    pairs = [(d * n_tensor + t, (d ^ dp_xor) * n_tensor + (t ^ tensor_xor)) for d in range(n_dp) for t in range(n_tensor)]
    return lax.ppermute(x, AXES, pairs)


def kernel_call(body, out_shapes, args, name, cost=0):
    whole = pl.BlockSpec(memory_space=pltpu.VMEM)
    return pl.pallas_call(
        body,
        out_shape=out_shapes,
        in_specs=[whole] * len(args),
        out_specs=[whole] * len(out_shapes),
        compiler_params=pltpu.CompilerParams(vmem_limit_bytes=VMEM_LIMIT),
        cost_estimate=pl.CostEstimate(flops=int(cost * 1.15e9), bytes_accessed=1024, transcendentals=0),
        name=name,
    )(*args)


def stack(parts, cost=0):
    parts = [p if isinstance(p, tuple) else (p, slice(0, p.shape[0])) for p in parts]

    def body(*refs):
        at = 0
        for ref, (_, cut) in zip(refs, parts):
            refs[-1][at : at + cut.stop - cut.start, :] = ref[cut, :]
            at += cut.stop - cut.start

    rows = sum(cut.stop - cut.start for _, cut in parts)
    out = jax.ShapeDtypeStruct((rows, parts[0][0].shape[1]), parts[0][0].dtype)
    return kernel_call(body, [out], [p for p, _ in parts], "stack", cost)[0]


def paired_form(n_dp, n_tensor, activations, value_weight, value_cotangent):
    tok, depth = activations.shape
    vdim = value_cotangent.shape[1]
    blk = depth // (n_dp * n_tensor)
    chips = n_dp // 2
    quarter = depth // n_tensor
    bf16, f32 = jnp.bfloat16, jnp.float32
    shape = jax.ShapeDtypeStruct
    barrier = lax.optimization_barrier

    def twin(x):
        return exchange(x, n_dp, n_tensor, 1, 0)

    def across(x, chip_xor):
        return exchange(x, n_dp, n_tensor, 2 * chip_xor, 0)

    def along(x, tensor_xor):
        return exchange(x, n_dp, n_tensor, 0, tensor_xor)

    def column(part, chip, core=0):
        return pl.multiple_of(((part * chips + chip) * 2 + core) * blk, LANES)

    def place():
        d = lax.axis_index("dp")
        return d // 2, d % 2, lax.axis_index("tensor")

    js = sorted(range(n_tensor), key=lambda j: (-j.bit_count(), -j)) if OPT["s_mode"] == "strip" else list(range(n_tensor - 1, -1, -1))
    width = n_tensor * 2 * blk

    def pack_body(act, cot, *outs):
        p, _, t = place()
        for q, out in enumerate(outs, 1):
            for i, j in enumerate(js):
                out[:, i * 2 * blk : (i + 1) * 2 * blk] = act[:, pl.ds(column(t ^ j, p ^ q), 2 * blk)]
            out[:, width:] = cot[...]

    def slice_body(weight, out):
        p, c, _ = place()
        out[...] = weight[pl.ds(pl.multiple_of((p * 2 + c) * blk, LANES), blk), :]

    if OPT["pack"] == "hbm":
        def pack_dma(act, cot, *refs):
            outs, sems = refs[:-1], refs[-1]
            p, _, t = place()
            pairs = []
            for q, out in enumerate(outs, 1):
                for i, j in enumerate(js):
                    pairs.append((act.at[:, pl.ds(column(t ^ j, p ^ q), 2 * blk)], out.at[:, i * 2 * blk : (i + 1) * 2 * blk]))
                pairs.append((cot, out.at[:, width:]))
            copies = [pltpu.make_async_copy(src, dst, sems.at[i]) for i, (src, dst) in enumerate(pairs)]
            for copy in copies:
                copy.start()
            for copy in copies:
                copy.wait()

        packs = pl.pallas_call(
            pack_dma,
            out_shape=[shape((tok, width + vdim), bf16)] * (chips - 1),
            in_specs=[pl.BlockSpec(memory_space=pltpu.HBM)] * 2,
            out_specs=[pl.BlockSpec(memory_space=pltpu.VMEM)] * (chips - 1),
            scratch_shapes=[pltpu.SemaphoreType.DMA(((chips - 1) * (n_tensor + 1),))],
            compiler_params=pltpu.CompilerParams(vmem_limit_bytes=int(OPT["pack_lim"] * 1024 * 1024)),
            cost_estimate=pl.CostEstimate(flops=int(OPT["c_pack"] * 1.15e9), bytes_accessed=1024, transcendentals=0),
            name="pack",
        )(activations, value_cotangent)
    else:
        packs = kernel_call(pack_body, [shape((tok, width + vdim), bf16)] * (chips - 1), [activations, value_cotangent], name="pack", cost=OPT["c_pack"])
    (own_slice,) = kernel_call(slice_body, [shape((blk, vdim), bf16)], [value_weight], name="own_slice", cost=OPT["c_slice"])
    if OPT["slice_after"]:
        own_slice, *packs = barrier((own_slice, *packs))
    got = [across(x, q) for q, x in enumerate(packs, 1)]

    if OPT["z_mode"] == "rec":
        held, slots = [own_slice], [0]
        bit = n_tensor // 2
        while bit:
            held.append(along(stack(held, OPT["c_zstack"]) if len(held) > 1 else held[0], bit))
            slots += [j ^ bit for j in slots]
            bit //= 2
        slots = slots[1:]
        held = held[1:]
    elif OPT["z_mode"] == "mix":
        slots = sorted(range(1, n_tensor), key=lambda j: (j.bit_count(), -j))
        by_slot = {0: own_slice}
        for j in slots:
            by_slot[j] = along(by_slot[j & (j - 1)], j & -j)
        held = [by_slot[j] for j in slots]
    else:
        slots = list(range(n_tensor - 1, 0, -1))
        held = [along(own_slice, j) for j in slots]

    def quarter_body(act, cot, w, acc, grad, columns, sem):
        _, _, t = place()
        own = pl.ds(pl.multiple_of(t * quarter, LANES), quarter)
        columns[...] = contract(cot[...], w[...], 1, 1).astype(bf16)
        copy = pltpu.make_async_copy(columns, grad.at[:, own], sem)
        copy.start()
        acc[...] = contract(act[:, own], w[...], 1, 0)
        copy.wait()

    whole, anywhere = pl.BlockSpec(memory_space=pltpu.VMEM), pl.BlockSpec(memory_space=pl.ANY)
    qw = value_weight
    if OPT["qtr_after"] == "pack":
        qw = barrier((value_weight, packs[0], got[0]))[0] if False else barrier((value_weight, own_slice))[0]
    elif OPT["qtr_after"] == "za":
        qw = barrier((value_weight, held[0]))[0]
    elif OPT["qtr_after"] == "a":
        qw = barrier((value_weight, got[0]))[0]
    acc, grad = pl.pallas_call(
        quarter_body,
        out_shape=[shape((tok, vdim), f32), shape((tok, depth), bf16)],
        in_specs=[whole] * 3,
        out_specs=[whole, anywhere],
        scratch_shapes=[pltpu.VMEM((tok, quarter), bf16), pltpu.SemaphoreType.DMA],
        compiler_params=pltpu.CompilerParams(vmem_limit_bytes=VMEM_LIMIT),
        cost_estimate=pl.CostEstimate(flops=int(OPT["c_qtr"] * 1.15e9), bytes_accessed=1024, transcendentals=0),
        name="own_quarter",
    )(activations, value_cotangent, value_weight)


    def sums_of(js_now, offset, cost):
        def body(act, cot, *refs):
            keep, send = refs[-2:]
            p, c, t = place()
            cots = jnp.concatenate([cot[...]] + [r[:, width:] for r in refs[:-2]], axis=0)
            for i, j in enumerate(js_now):
                for out, core in ((send, 1 - c), (keep, c)):
                    start = pl.multiple_of((offset + i) * 2 * blk + core * blk, LANES)
                    parts = [act[:, pl.ds(column(t ^ j, p, core), blk)]] + [r[:, pl.ds(start, blk)] for r in refs[:-2]]
                    out[i * blk : (i + 1) * blk, :] = contract(jnp.concatenate(parts, axis=0), cots, 0, 0)

        out = shape((len(js_now) * blk, vdim), f32)
        return kernel_call(body, [out, out], [activations, value_cotangent, *got], name="sums", cost=cost)

    def join(terms, pack, cost):
        def value(ref):
            return ref[...] if ref.shape[0] == blk else ref[:blk, :] * jnp.exp2(ref[blk : blk + 1, :])

        def body(*refs):
            out = refs[-1]
            total = sum((value(r) for r in refs[1:-1]), value(refs[0]))
            if not pack:
                out[...] = total
                return
            top = jnp.max(jnp.abs(total), axis=(0, 1), keepdims=True)
            power = jnp.clip(jnp.ceil(jnp.log(jnp.maximum(top, 1e-30)) * LOG2_E) - TOP_POWER, -110.0, 110.0)
            out[:blk, :] = total * jnp.exp2(-power)
            out[blk:, :] = jnp.broadcast_to(power, (PAD, vdim))

        (out,) = kernel_call(body, [shape((blk + PAD if pack else blk, vdim), f32)], terms, name="join", cost=cost)
        return out.astype(jnp.float16) if pack else out

    if OPT["sums_za"]:
        got[0], held[0] = barrier((got[0], held[0]))
    if OPT["sums_zb"]:
        got[0], *held = barrier((got[0], *held))
    if OPT["sums_qtr"]:
        got[0], acc = barrier((got[0], acc))
    if OPT["s_mode"] == "strip":
        firsts = [j for j in js if j.bit_count() > 1] or js[:1]
    else:
        firsts = js[: n_tensor // 2]
    others = [j for j in js if j not in firsts]
    keep_1, send_1 = sums_of(firsts, 0, OPT["c_sums1"])
    keep_2, send_2 = sums_of(others, len(firsts), OPT["c_sums2"])
    if OPT["ca_zb"]:
        send_1, held[-1] = barrier((send_1, held[-1]))
    mine = stack(held, OPT["c_mine"])
    if OPT["mine_after"]:
        mine, send_1 = barrier((mine, send_1))
    terms = {}
    for names, keep, twins_sum in ((firsts, keep_1, twin(send_1)), (others, keep_2, twin(send_2))):
        for i, j in enumerate(names):
            cut = slice(i * blk, (i + 1) * blk)
            terms[j] = [keep, twins_sum] if len(names) == 1 else [keep[cut], twins_sum[cut]]

    rows = (n_tensor - 1) * blk
    pieces = {0: [mine]}
    singles = [1 << b for b in range(chips.bit_length() - 1)]
    if OPT["w_mode"] == "pipe" and len(singles) > 1:
        cuts = [rows * i // len(singles) // 16 * 16 for i in range(len(singles))] + [rows]
    else:
        cuts = [0, rows]
    segs = [slice(a, b) for a, b in zip(cuts, cuts[1:])]
    for q in singles:
        pieces[q] = [across(mine[c] if len(segs) > 1 else mine, q) for c in segs]

    arrived = {}
    strip = OPT["s_mode"] == "strip"
    for j in js[:-1]:
        packed = join(terms[j], True, OPT["c_join1"] if j in firsts else OPT["c_join2"])
        if j == js[len(firsts)] and OPT["st2_after"]:
            _, *got_now = barrier((packed, *[x for q in singles for x in pieces[q]]))
            pieces.update({q: got_now[i * len(segs) : (i + 1) * len(segs)] for i, q in enumerate(singles)})
        arrived[j] = along(packed, j & -j if strip else j)
        if OPT["s1_after3"] and strip and j == js[len(firsts)]:
            for k in others[1:-1]:
                terms[k] = list(barrier((*terms[k], packed))[:-1])
        if strip and j in firsts:
            terms[j & (j - 1)].append(arrived[j].astype(f32))

    for q in sorted((q for q in range(1, chips) if q not in singles), key=lambda q: q.bit_count()):
        bits = [b for b in singles if q & b]
        if len(segs) > 1:
            pieces[q] = [across(pieces[q ^ bits[i % len(bits)]][i], bits[i % len(bits)]) for i in range(len(segs))]
            continue
        cuts = [rows * i // len(bits) // 16 * 16 for i in range(len(bits))] + [rows]
        ways = []
        for i, b in enumerate(bits):
            there = stack(pieces[q ^ b]) if len(pieces[q ^ b]) > 1 else pieces[q ^ b][0]
            ways.append(across(there[cuts[i] : cuts[i + 1]], b))
        pieces[q] = ways

    total = join(terms[0] + [arrived[j].astype(f32) for j in (others[:-1] if strip else js[:-1])], False, OPT["c_joinf"])
    weight_grad = total / jnp.sqrt(f32(tok * n_dp * n_tensor))
    if OPT["pf"]:
        acc, total = barrier((acc, total))

    def product(acc, grad, qs, last):
        n = (n_tensor - 1) * len(qs)
        ours = stack([x for q in qs for x in pieces[q]], OPT["c_e2stack"] if last else OPT["c_estack"])
        if last:
            after = [acc] * OPT["e2_acc"] + [arrived[1]] * OPT["e2_s1"] + [arrived[n_tensor // 2]] * OPT["e2_s2"]
            ours, *_ = barrier((ours, *after))
        elif OPT["e1_s"]:
            ours, *_ = barrier((ours, arrived[1]))
        operands = [ours, twin(ours)]

        def body(act, cot, acc, _, *refs):
            both, (out, grad, total, columns, sems) = refs[:2], refs[-5:]
            p, c, t = place()
            order = [(at_q * (n_tensor - 1) + i, q, j, core) for at_q, q in enumerate(qs) for i, j in enumerate(slots) for core in range(2)]
            weights = [both[k][at * blk : (at + 1) * blk, :] for at, _, _, k in order]
            columns_of = [pl.ds(column(t ^ j, p ^ q, (c, 1 - c)[k]), blk) for _, q, j, k in order]
            lhs = jnp.concatenate([act[:, cols] for cols in columns_of], axis=1)
            result = acc[...] + contract(lhs, jnp.concatenate(weights, axis=0), 1, 0)
            copies = []
            if last:
                total[...] = result.astype(bf16)
                copies.append(pltpu.make_async_copy(total, out, sems.at[n]))
                copies[0].start()
            else:
                out[...] = result
            for (at, q, j, k), w in zip(order, weights):
                cols = pl.ds(pl.multiple_of((c, 1 - c)[k] * blk, LANES), blk)
                columns[at, :, cols] = contract(cot[...], w, 1, 1).astype(bf16)
                if k:
                    copies.append(pltpu.make_async_copy(columns.at[at], grad.at[:, pl.ds(column(t ^ j, p ^ q), 2 * blk)], sems.at[at]))
                    copies[-1].start()
            for copy in copies:
                copy.wait()

        args = [activations, value_cotangent, acc, grad, *operands]
        return pl.pallas_call(
            body,
            out_shape=[shape((tok, vdim), bf16 if last else f32), shape((tok, depth), bf16)],
            in_specs=[whole] * 3 + [anywhere] + [whole] * len(operands),
            out_specs=[anywhere if last else whole, anywhere],
            scratch_shapes=[
                pltpu.VMEM((tok, vdim), bf16),
                pltpu.VMEM((n, tok, 2 * blk), bf16),
                pltpu.SemaphoreType.DMA((n + 1,)),
            ],
            input_output_aliases={3: 1},
            compiler_params=pltpu.CompilerParams(vmem_limit_bytes=VMEM_LIMIT),
            cost_estimate=pl.CostEstimate(flops=int((OPT["c_last"] if last else OPT["c_prod"]) * 1.15e9), bytes_accessed=1024, transcendentals=0),
            name="product",
        )(*args)

    late = [q for q in range(chips) if q.bit_count() >= 2]
    acc, grad = product(acc, grad, [0, *singles], not late)
    if late:
        acc, grad = product(acc, grad, late, True)
    return acc, grad, weight_grad


def solution(mesh):
    n_dp, n_tensor = mesh.shape["dp"], mesh.shape["tensor"]

    def per_device(activations, value_weight, value_cotangent):
        tok, depth = activations.shape
        powers = all(n > 1 and n & (n - 1) == 0 for n in (n_dp, n_tensor))
        if powers and depth % (n_dp * n_tensor * LANES) == 0 and tok % LANES == 0:
            return paired_form(n_dp, n_tensor, activations, value_weight, value_cotangent)
        return gathered_form(activations, value_weight, value_cotangent)

    return jax.shard_map(
        per_device,
        mesh=mesh,
        in_specs=(P(AXES, None), P("tensor", None), P(AXES, None)),
        out_specs=(P(AXES, None), P(AXES, None), P(("tensor", "dp"), None)),
        check_vma=False,
    )
```

time: 153 us -> 51.7 us (0.34)
  waiting for transfers between devices: 81.9 us -> 20.6 us
  blocking collectives: 36.1 us -> 0 us
  between operations: 15.5 us -> 0.86 us
  starting transfers between devices: 6.36 us -> 20.7 us
  matrix products: 8.22 us -> 0 us
  Pallas kernels: 0 us -> 6.02 us
    reduce_scatter x1 -> x0, waiting for transfers between devices: 41.8 us -> none  [per_device(): summed = lax.psum_scatter(group_term, 'dp', scatter_dimension=0, tiled=True)]
    all_gather x1 -> x0, waiting for transfers between devices: 39.6 us -> none  [per_device(): full_weight = lax.all_gather(value_weight, 'tensor', axis=0, tiled=True)]
    all_gather x1 -> x0, blocking collectives: 36.1 us -> none  [per_device(): lax.all_gather(value_cotangent, 'tensor', axis=0, tiled=True)]
    ppermute x0 -> x17, starting transfers between devices: none -> 20.7 us  [exchange(): return lax.ppermute(x, AXES, pairs)]
    ppermute x0 -> x17, waiting for transfers between devices: none -> 20.6 us  [exchange(): return lax.ppermute(x, AXES, pairs)]
    dot_general x3 -> x0, matrix products: 8.22 us -> none  [the longest x1 3.71 us: per_device(): jnp.dot(activations, full_weight, preferred_element_type=jnp.float32)]
    all_to_all x1 -> x0, starting transfers between devices: 6.32 us -> none  [per_device(): lax.all_to_all(activations, 'tensor', split_axis=1, concat_axis=0, tiled=...]
    pallas_call x0 -> x14, Pallas kernels: none -> 6.02 us  [the longest x2 2.98 us: product(): pl.pallas_call(body, out_shape=[shape((tok, vdim), bf16 if last else f32)...]
  transfers between devices with their start and end apart: 3 -> 17, of which waited for: 2 -> 9; matrix products, arithmetic and copies ran while one was open for 1% -> 2% of each run, Pallas kernels for 0% -> 4%
where the time goes in v2:
time: 51.7 us; the launch traced here: 51.5 us
  starting transfers between devices  20.7 us (40%)
  waiting for transfers between devices  20.6 us (40%)
  Pallas kernels  6.02 us (12%)
  local copies, waits for them, and re-layouts  2.56 us (5%)
  other arithmetic  0.86 us (2%)
  between operations  0.86 us (2%)
    ppermute x17, starting transfers between devices, exchange(): return lax.ppermute(x, AXES, pairs)  20.7 us
    ppermute x17, waiting for transfers between devices, exchange(): return lax.ppermute(x, AXES, pairs)  20.6 us
    pallas_call x2, Pallas kernels, product(): pl.pallas_call(body, out_shape=[shape((tok, vdim), bf16 if last else f32)...  2.98 us
    unnamed x6, local copies, waits for them, and re-layouts  2.43 us
    pallas_call x11, Pallas kernels, kernel_call(): pl.pallas_call(body, out_shape=out_shapes, in_specs=[whole] * len(args),...  1.83 us
    pallas_call x1, Pallas kernels, paired_form(): pl.pallas_call(quarter_body, out_shape=[shape((tok, vdim), f32), shape((t...  1.2 us
  transfers between devices with their start and end apart: 17, of which 9 were waited for; matrix products, arithmetic and copies ran while one was open for 2% of the time, Pallas kernels for 4%

profile of v2, /device:TPU:0, one launch (start us, length us, event | category | flops | bytes accessed | tf_op | source)
XLA Modules:
  0.0 51.5 jit_solution(2695053917453771522)
XLA Ops:
  0.6 1.2 %copy-done.1 = bf16[1024,512]{1,0:T(8,128)(2,1)S(1)} copy-done((bf16[1024,512]{1,0:T(8,128)(2,1)S(1)}, bf16[1024,512]{1,0:T(8,128)(2,1)}, u32[]{:S(2)}) %copy-start.1) | copy-done | bytes 1048600
  1.9 1.2 %copy-done = bf16[128,4096]{1,0:T(8,128)(2,1)S(1)} copy-done((bf16[128,4096]{1,0:T(8,128)(2,1)S(1)}, bf16[128,4096]{1,0:T(8,128)(2,1)}, u32[]{:S(2)}) %copy-start) | copy-done | bytes 1048600
  3.2 3.0 %collective-permute-start = (bf16[128,1536]{1,0:T(8,128)(2,1)S(1)}, bf16[128,1536]{1,0:T(8,128)(2,1)S(1)}, u32[]{:S(2)}, u32[]{:S(2)}) collective-permute-start(bf16[128,1536]{1,0:T(8,128)(2,1)S(1)} %get-tuple-element.39), channel_id=1, source_target_pairs={{0,8},{1,9},{2,10},{3,11},{4,12},{5,13},{6,14},{7,15},{8,0},{9,1},... | collective-permute-start | bytes 1179656 | tf_op jit(solution)/shard_map/ppermute | solution.py:38
  6.2 1.5 %collective-permute-start.4 = (bf16[128,1536]{1,0:T(8,128)(2,1)S(1)}, bf16[128,1536]{1,0:T(8,128)(2,1)S(1)}, u32[]{:S(2)}, u32[]{:S(2)}) collective-permute-start(bf16[128,1536]{1,0:T(8,128)(2,1)S(1)} %get-tuple-element.47), channel_id=1, source_target_pairs={{0,16},{1,17},{2,18},{3,19},{4,20},{5,21},{6,22},{7,23},{8,24},{9,... | collective-permute-start | bytes 1179656 | tf_op jit(solution)/shard_map/ppermute | solution.py:38
  7.8 3.0 %collective-permute-start.1 = (bf16[128,512]{1,0:T(8,128)(2,1)S(1)}, bf16[128,512]{1,0:T(8,128)(2,1)S(1)}, u32[]{:S(2)}, u32[]{:S(2)}) collective-permute-start(bf16[128,512]{1,0:T(8,128)(2,1)S(1)} %own_slice.1), channel_id=1, source_target_pairs={{0,2},{1,3},{2,0},{3,1},{4,6},{5,7},{6,4},{7,5},{8,10},{9,11},{10,... | collective-permute-start | bytes 393224 | tf_op jit(solution)/shard_map/ppermute | solution.py:38
  10.8 1.6 %collective-permute-start.2 = (bf16[128,512]{1,0:T(8,128)(2,1)S(1)}, bf16[128,512]{1,0:T(8,128)(2,1)S(1)}, u32[]{:S(2)}, u32[]{:S(2)}) collective-permute-start(bf16[128,512]{1,0:T(8,128)(2,1)S(1)} %own_slice.1), channel_id=1, source_target_pairs={{0,1},{1,0},{2,3},{3,2},{4,5},{5,4},{6,7},{7,6},{8,9},{9,8},{10,11... | collective-permute-start | bytes 393224 | tf_op jit(solution)/shard_map/ppermute | solution.py:38
  12.4 4.0 %collective-permute-done.1.refs_0_ = bf16[128,512]{1,0:T(8,128)(2,1)S(1)} collective-permute-done((bf16[128,512]{1,0:T(8,128)(2,1)S(1)}, bf16[128,512]{1,0:T(8,128)(2,1)S(1)}, u32[]{:S(2)}, u32[]{:S(2)}) %collective-permute-start.1) | collective-permute-done | bytes 131104 | tf_op jit(solution)/shard_map/ppermute | solution.py:38
  17.0 1.2 %own_quarter.1 = (f32[128,512]{1,0:T(8,128)S(1)}, bf16[128,4096]{1,0:T(8,128)(2,1)}) custom-call(bf16[128,4096]{1,0:T(8,128)(2,1)S(1)} %copy-done, bf16[128,512]{1,0:T(8,128)(2,1)S(1)} %copy-done.2, bf16[1024,512]{1,0:T(8,128)(2,1)S(1)} %copy-done.1), custom_call_target="tpu_custom_call" | custom-call | bytes 1024 | tf_op jit(solution)/shard_map/own_quarter/pallas_call | solution.py:176
  18.2 3.1 %collective-permute-done.3.refs_2_ = bf16[128,512]{1,0:T(8,128)(2,1)S(1)} collective-permute-done((bf16[128,512]{1,0:T(8,128)(2,1)S(1)}, bf16[128,512]{1,0:T(8,128)(2,1)S(1)}, u32[]{:S(2)}, u32[]{:S(2)}) %collective-permute-start.3) | collective-permute-done | bytes 131104 | tf_op jit(solution)/shard_map/ppermute | solution.py:38
  21.3 3.9 %collective-permute-done.4.refs_1_ = bf16[128,1536]{1,0:T(8,128)(2,1)S(1)} collective-permute-done((bf16[128,1536]{1,0:T(8,128)(2,1)S(1)}, bf16[128,1536]{1,0:T(8,128)(2,1)S(1)}, u32[]{:S(2)}, u32[]{:S(2)}) %collective-permute-start.4) | collective-permute-done | bytes 393248 | tf_op jit(solution)/shard_map/ppermute | solution.py:38
  26.9 1.6 %collective-permute-start.12 = (bf16[384,512]{1,0:T(8,128)(2,1)S(1)}, bf16[384,512]{1,0:T(8,128)(2,1)S(1)}, u32[]{:S(2)}, u32[]{:S(2)}) collective-permute-start(bf16[384,512]{1,0:T(8,128)(2,1)S(1)} %stack.3.refs_0_), channel_id=1, source_target_pairs={{0,16},{1,17},{2,18},{3,19},{4,20},{5,21},{6,22},{7,23},{8,24},{9,... | collective-permute-start | bytes 1179656 | tf_op jit(solution)/shard_map/ppermute | solution.py:38
  29.2 1.6 %collective-permute-start.8 = (f16[144,512]{1,0:T(8,128)(2,1)S(1)}, f16[144,512]{1,0:T(8,128)(2,1)S(1)}, u32[]{:S(2)}, u32[]{:S(2)}) collective-permute-start(f16[144,512]{1,0:T(8,128)(2,1)S(1)} %convert_element_type.18), channel_id=1, source_target_pairs={{0,1},{1,0},{2,3},{3,2},{4,5},{5,4},{6,7},{7,6},{8,9},{9,8},{10,11... | collective-permute-start | bytes 442376 | tf_op jit(solution)/shard_map/ppermute | solution.py:38
  30.9 3.8 %collective-permute-done.8 = f16[144,512]{1,0:T(8,128)(2,1)S(1)} collective-permute-done((f16[144,512]{1,0:T(8,128)(2,1)S(1)}, f16[144,512]{1,0:T(8,128)(2,1)S(1)}, u32[]{:S(2)}, u32[]{:S(2)}) %collective-permute-start.8) | collective-permute-done | bytes 147488 | tf_op jit(solution)/shard_map/ppermute | solution.py:38
  35.1 2.7 %collective-permute-start.9 = (f16[144,512]{1,0:T(8,128)(2,1)S(1)}, f16[144,512]{1,0:T(8,128)(2,1)S(1)}, u32[]{:S(2)}, u32[]{:S(2)}) collective-permute-start(f16[144,512]{1,0:T(8,128)(2,1)S(1)} %convert_element_type.20), channel_id=1, source_target_pairs={{0,2},{1,3},{2,0},{3,1},{4,6},{5,7},{6,4},{7,5},{8,10},{9,11},{10,... | collective-permute-start | bytes 442376 | tf_op jit(solution)/shard_map/ppermute | solution.py:38
  37.9 1.6 %collective-permute-start.10 = (f16[144,512]{1,0:T(8,128)(2,1)S(1)}, f16[144,512]{1,0:T(8,128)(2,1)S(1)}, u32[]{:S(2)}, u32[]{:S(2)}) collective-permute-start(f16[144,512]{1,0:T(8,128)(2,1)S(1)} %convert_element_type.22), channel_id=1, source_target_pairs={{0,1},{1,0},{2,3},{3,2},{4,5},{5,4},{6,7},{7,6},{8,9},{9,8},{10,11... | collective-permute-start | bytes 442376 | tf_op jit(solution)/shard_map/ppermute | solution.py:38
  39.7 1.3 %collective-permute-start.14 = (bf16[192,512]{1,0:T(8,128)(2,1)S(1)}, bf16[192,512]{1,0:T(8,128)(2,1)S(1)}, u32[]{:S(2)}, u32[]{:S(2)}) collective-permute-start(bf16[192,512]{1,0:T(8,128)(2,1)S(1)} %slice.30), channel_id=1, source_target_pairs={{0,8},{1,9},{2,10},{3,11},{4,12},{5,13},{6,14},{7,15},{8,0},{9,1},... | collective-permute-start | bytes 589832 | tf_op jit(solution)/shard_map/ppermute | solution.py:38
  41.0 0.8 %collective-permute-start.15 = (bf16[192,512]{1,0:T(8,128)(2,1)S(1)}, bf16[192,512]{1,0:T(8,128)(2,1)S(1)}, u32[]{:S(2)}, u32[]{:S(2)}) collective-permute-start(bf16[192,512]{1,0:T(8,128)(2,1)S(1)} %slice.31), channel_id=1, source_target_pairs={{0,16},{1,17},{2,18},{3,19},{4,20},{5,21},{6,22},{7,23},{8,24},{9,... | collective-permute-start | bytes 589832 | tf_op jit(solution)/shard_map/ppermute | solution.py:38
  41.8 2.0 %collective-permute-done.9 = f16[144,512]{1,0:T(8,128)(2,1)S(1)} collective-permute-done((f16[144,512]{1,0:T(8,128)(2,1)S(1)}, f16[144,512]{1,0:T(8,128)(2,1)S(1)}, u32[]{:S(2)}, u32[]{:S(2)}) %collective-permute-start.9) | collective-permute-done | bytes 147488 | tf_op jit(solution)/shard_map/ppermute | solution.py:38
  44.4 1.0 %collective-permute-done.14.refs_0_ = bf16[192,512]{1,0:T(8,128)(2,1)S(1)} collective-permute-done((bf16[192,512]{1,0:T(8,128)(2,1)S(1)}, bf16[192,512]{1,0:T(8,128)(2,1)S(1)}, u32[]{:S(2)}, u32[]{:S(2)}) %collective-permute-start.14) | collective-permute-done | bytes 196640 | tf_op jit(solution)/shard_map/ppermute | solution.py:38
  45.5 1.2 %collective-permute-done.15.refs_1_ = bf16[192,512]{1,0:T(8,128)(2,1)S(1)} collective-permute-done((bf16[192,512]{1,0:T(8,128)(2,1)S(1)}, bf16[192,512]{1,0:T(8,128)(2,1)S(1)}, u32[]{:S(2)}, u32[]{:S(2)}) %collective-permute-start.15) | collective-permute-done | bytes 196640 | tf_op jit(solution)/shard_map/ppermute | solution.py:38
  46.7 1.8 %product.2 = (f32[128,512]{1,0:T(8,128)S(1)}, bf16[128,4096]{1,0:T(8,128)(2,1)}) custom-call(bf16[128,4096]{1,0:T(8,128)(2,1)S(1)} %copy-done, bf16[128,512]{1,0:T(8,128)(2,1)S(1)} %copy-done.2, f32[128,512]{1,0:T(8,128)S(1)} %get-tuple-element.57.acc, bf16[128,4096]{1,0:T(8,128)(2,1)} %get-tuple-element.58._, ...), custom_call_target="tpu_custom_call", output_to_operand_aliasing={{1}: (3, {})} | custom-call | bytes 1024 | tf_op jit(solution)/shard_map/product/pallas_call | solution.py:321
  48.7 0.7 %broadcast_multiply_fusion = f32[128,512]{1,0:T(8,128)} fusion(f32[128,512]{1,0:T(8,128)S(1)} %join.7), kind=kLoop, calls=%fused_computation | loop fusion | flops 65536 | bytes 524288 | tf_op jit(solution)/shard_map/div | solution.py:282
  49.4 1.0 %collective-permute-done.16.refs_1_ = bf16[384,512]{1,0:T(8,128)(2,1)S(1)} collective-permute-done((bf16[384,512]{1,0:T(8,128)(2,1)S(1)}, bf16[384,512]{1,0:T(8,128)(2,1)S(1)}, u32[]{:S(2)}, u32[]{:S(2)}) %collective-permute-start.16) | collective-permute-done | bytes 393248 | tf_op jit(solution)/shard_map/ppermute | solution.py:38
  50.4 1.1 %product.3 = (bf16[128,512]{1,0:T(8,128)(2,1)}, bf16[128,4096]{1,0:T(8,128)(2,1)}) custom-call(bf16[128,4096]{1,0:T(8,128)(2,1)S(1)} %copy-done, bf16[128,512]{1,0:T(8,128)(2,1)S(1)} %copy-done.2, f32[128,512]{1,0:T(8,128)S(1)} %get-tuple-element.64.acc, bf16[128,4096]{1,0:T(8,128)(2,1)} %get-tuple-element.65._, ...), custom_call_target="tpu_custom_call", output_to_operand_aliasing={{1}: (3, {})} | custom-call | bytes 1024 | tf_op jit(solution)/shard_map/product/pallas_call | solution.py:321
  (41 shorter events, 4.4 us)
Async XLA Ops:
  0.6 1.2 %copy-start.1 = (bf16[1024,512]{1,0:T(8,128)(2,1)S(1)}, bf16[1024,512]{1,0:T(8,128)(2,1)}, u32[]{:S(2)}) copy-start(bf16[1024,512]{1,0:T(8,128)(2,1)} %w.1) | copy-start | bytes 3145732
  1.9 1.2 %copy-start = (bf16[128,4096]{1,0:T(8,128)(2,1)S(1)}, bf16[128,4096]{1,0:T(8,128)(2,1)}, u32[]{:S(2)}) copy-start(bf16[128,4096]{1,0:T(8,128)(2,1)} %act.11) | copy-start | bytes 3145732
  1.9 1.2 %copy-start.2 = (bf16[128,512]{1,0:T(8,128)(2,1)S(1)}, bf16[128,512]{1,0:T(8,128)(2,1)}, u32[]{:S(2)}) copy-start(bf16[128,512]{1,0:T(8,128)(2,1)} %cot.11) | copy-start | bytes 393220
  3.2 15.0 %collective-permute-start = (bf16[128,1536]{1,0:T(8,128)(2,1)S(1)}, bf16[128,1536]{1,0:T(8,128)(2,1)S(1)}, u32[]{:S(2)}, u32[]{:S(2)}) collective-permute-start(bf16[128,1536]{1,0:T(8,128)(2,1)S(1)} %get-tuple-element.39), channel_id=1, source_target_pairs={{0,8},{1,9},{2,10},{3,11},{4,12},{5,13},{6,14},{7,15},{8,0},{9,1},... | collective-permute-start | bytes 1179656 | tf_op jit(solution)/shard_map/ppermute | solution.py:38
  6.2 19.0 %collective-permute-start.4 = (bf16[128,1536]{1,0:T(8,128)(2,1)S(1)}, bf16[128,1536]{1,0:T(8,128)(2,1)S(1)}, u32[]{:S(2)}, u32[]{:S(2)}) collective-permute-start(bf16[128,1536]{1,0:T(8,128)(2,1)S(1)} %get-tuple-element.47), channel_id=1, source_target_pairs={{0,16},{1,17},{2,18},{3,19},{4,20},{5,21},{6,22},{7,23},{8,24},{9,... | collective-permute-start | bytes 1179656 | tf_op jit(solution)/shard_map/ppermute | solution.py:38
  7.7 17.5 %collective-permute-start.5 = (bf16[128,1536]{1,0:T(8,128)(2,1)S(1)}, bf16[128,1536]{1,0:T(8,128)(2,1)S(1)}, u32[]{:S(2)}, u32[]{:S(2)}) collective-permute-start(bf16[128,1536]{1,0:T(8,128)(2,1)S(1)} %get-tuple-element.48), channel_id=1, source_target_pairs={{0,24},{1,25},{2,26},{3,27},{4,28},{5,29},{6,30},{7,31},{8,16},{9,... | collective-permute-start | bytes 1179656 | tf_op jit(solution)/shard_map/ppermute | solution.py:38
  7.8 8.6 %collective-permute-start.1 = (bf16[128,512]{1,0:T(8,128)(2,1)S(1)}, bf16[128,512]{1,0:T(8,128)(2,1)S(1)}, u32[]{:S(2)}, u32[]{:S(2)}) collective-permute-start(bf16[128,512]{1,0:T(8,128)(2,1)S(1)} %own_slice.1), channel_id=1, source_target_pairs={{0,2},{1,3},{2,0},{3,1},{4,6},{5,7},{6,4},{7,5},{8,10},{9,11},{10,... | collective-permute-start | bytes 393224 | tf_op jit(solution)/shard_map/ppermute | solution.py:38
  10.8 7.4 %collective-permute-start.2 = (bf16[128,512]{1,0:T(8,128)(2,1)S(1)}, bf16[128,512]{1,0:T(8,128)(2,1)S(1)}, u32[]{:S(2)}, u32[]{:S(2)}) collective-permute-start(bf16[128,512]{1,0:T(8,128)(2,1)S(1)} %own_slice.1), channel_id=1, source_target_pairs={{0,1},{1,0},{2,3},{3,2},{4,5},{5,4},{6,7},{7,6},{8,9},{9,8},{10,11... | collective-permute-start | bytes 393224 | tf_op jit(solution)/shard_map/ppermute | solution.py:38
  16.4 5.0 %collective-permute-start.3 = (bf16[128,512]{1,0:T(8,128)(2,1)S(1)}, bf16[128,512]{1,0:T(8,128)(2,1)S(1)}, u32[]{:S(2)}, u32[]{:S(2)}) collective-permute-start(bf16[128,512]{1,0:T(8,128)(2,1)S(1)} %collective-permute-done.1.refs_0_), channel_id=1, source_target_pairs={{0,1},{1,0},{2,3},{3,2},{4,5},{5,4},{6,7},{7,6},{8,9},{9,8},{10,11... | collective-permute-start | bytes 393224 | tf_op jit(solution)/shard_map/ppermute | solution.py:38
  25.9 8.9 %collective-permute-start.6 = (f32[384,512]{1,0:T(8,128)S(1)}, f32[384,512]{1,0:T(8,128)S(1)}, u32[]{:S(2)}, u32[]{:S(2)}) collective-permute-start(f32[384,512]{1,0:T(8,128)S(1)} %get-tuple-element.50), channel_id=1, source_target_pairs={{0,4},{1,5},{2,6},{3,7},{4,0},{5,1},{6,2},{7,3},{8,12},{9,13},{10,... | collective-permute-start | bytes 2359304 | tf_op jit(solution)/shard_map/ppermute | solution.py:38
  26.3 2.7 %collective-permute-start.7 = (f32[128,512]{1,0:T(8,128)S(1)}, f32[128,512]{1,0:T(8,128)S(1)}, u32[]{:S(2)}, u32[]{:S(2)}) collective-permute-start(f32[128,512]{1,0:T(8,128)S(1)} %get-tuple-element.54), channel_id=1, source_target_pairs={{0,4},{1,5},{2,6},{3,7},{4,0},{5,1},{6,2},{7,3},{8,12},{9,13},{10,... | collective-permute-start | bytes 786440 | tf_op jit(solution)/shard_map/ppermute | solution.py:38
  26.9 12.7 %collective-permute-start.12 = (bf16[384,512]{1,0:T(8,128)(2,1)S(1)}, bf16[384,512]{1,0:T(8,128)(2,1)S(1)}, u32[]{:S(2)}, u32[]{:S(2)}) collective-permute-start(bf16[384,512]{1,0:T(8,128)(2,1)S(1)} %stack.3.refs_0_), channel_id=1, source_target_pairs={{0,16},{1,17},{2,18},{3,19},{4,20},{5,21},{6,22},{7,23},{8,24},{9,... | collective-permute-start | bytes 1179656 | tf_op jit(solution)/shard_map/ppermute | solution.py:38
  28.5 11.1 %collective-permute-start.11 = (bf16[384,512]{1,0:T(8,128)(2,1)S(1)}, bf16[384,512]{1,0:T(8,128)(2,1)S(1)}, u32[]{:S(2)}, u32[]{:S(2)}) collective-permute-start(bf16[384,512]{1,0:T(8,128)(2,1)S(1)} %stack.3.refs_0_), channel_id=1, source_target_pairs={{0,8},{1,9},{2,10},{3,11},{4,12},{5,13},{6,14},{7,15},{8,0},{9,1},... | collective-permute-start | bytes 1179656 | tf_op jit(solution)/shard_map/ppermute | solution.py:38
  29.2 5.5 %collective-permute-start.8 = (f16[144,512]{1,0:T(8,128)(2,1)S(1)}, f16[144,512]{1,0:T(8,128)(2,1)S(1)}, u32[]{:S(2)}, u32[]{:S(2)}) collective-permute-start(f16[144,512]{1,0:T(8,128)(2,1)S(1)} %convert_element_type.18), channel_id=1, source_target_pairs={{0,1},{1,0},{2,3},{3,2},{4,5},{5,4},{6,7},{7,6},{8,9},{9,8},{10,11... | collective-permute-start | bytes 442376 | tf_op jit(solution)/shard_map/ppermute | solution.py:38
  35.1 8.8 %collective-permute-start.9 = (f16[144,512]{1,0:T(8,128)(2,1)S(1)}, f16[144,512]{1,0:T(8,128)(2,1)S(1)}, u32[]{:S(2)}, u32[]{:S(2)}) collective-permute-start(f16[144,512]{1,0:T(8,128)(2,1)S(1)} %convert_element_type.20), channel_id=1, source_target_pairs={{0,2},{1,3},{2,0},{3,1},{4,6},{5,7},{6,4},{7,5},{8,10},{9,11},{10,... | collective-permute-start | bytes 442376 | tf_op jit(solution)/shard_map/ppermute | solution.py:38
  37.9 6.4 %collective-permute-start.10 = (f16[144,512]{1,0:T(8,128)(2,1)S(1)}, f16[144,512]{1,0:T(8,128)(2,1)S(1)}, u32[]{:S(2)}, u32[]{:S(2)}) collective-permute-start(f16[144,512]{1,0:T(8,128)(2,1)S(1)} %convert_element_type.22), channel_id=1, source_target_pairs={{0,1},{1,0},{2,3},{3,2},{4,5},{5,4},{6,7},{7,6},{8,9},{9,8},{10,11... | collective-permute-start | bytes 442376 | tf_op jit(solution)/shard_map/ppermute | solution.py:38
  39.7 5.7 %collective-permute-start.14 = (bf16[192,512]{1,0:T(8,128)(2,1)S(1)}, bf16[192,512]{1,0:T(8,128)(2,1)S(1)}, u32[]{:S(2)}, u32[]{:S(2)}) collective-permute-start(bf16[192,512]{1,0:T(8,128)(2,1)S(1)} %slice.30), channel_id=1, source_target_pairs={{0,8},{1,9},{2,10},{3,11},{4,12},{5,13},{6,14},{7,15},{8,0},{9,1},... | collective-permute-start | bytes 589832 | tf_op jit(solution)/shard_map/ppermute | solution.py:38
  41.0 5.7 %collective-permute-start.15 = (bf16[192,512]{1,0:T(8,128)(2,1)S(1)}, bf16[192,512]{1,0:T(8,128)(2,1)S(1)}, u32[]{:S(2)}, u32[]{:S(2)}) collective-permute-start(bf16[192,512]{1,0:T(8,128)(2,1)S(1)} %slice.31), channel_id=1, source_target_pairs={{0,16},{1,17},{2,18},{3,19},{4,20},{5,21},{6,22},{7,23},{8,24},{9,... | collective-permute-start | bytes 589832 | tf_op jit(solution)/shard_map/ppermute | solution.py:38
  41.8 4.9 %collective-permute-start.13 = (bf16[1152,512]{1,0:T(8,128)(2,1)S(1)}, bf16[1152,512]{1,0:T(8,128)(2,1)S(1)}, u32[]{:S(2)}, u32[]{:S(2)}) collective-permute-start(bf16[1152,512]{1,0:T(8,128)(2,1)S(1)} %stack.4.refs_0_), channel_id=1, source_target_pairs={{0,4},{1,5},{2,6},{3,7},{4,0},{5,1},{6,2},{7,3},{8,12},{9,13},{10,... | collective-permute-start | bytes 3538952 | tf_op jit(solution)/shard_map/ppermute | solution.py:38
  48.6 1.8 %collective-permute-start.16 = (bf16[384,512]{1,0:T(8,128)(2,1)S(1)}, bf16[384,512]{1,0:T(8,128)(2,1)S(1)}, u32[]{:S(2)}, u32[]{:S(2)}) collective-permute-start(bf16[384,512]{1,0:T(8,128)(2,1)S(1)} %stack.5.refs_0_), channel_id=1, source_target_pairs={{0,4},{1,5},{2,6},{3,7},{4,0},{5,1},{6,2},{7,3},{8,12},{9,13},{10,... | collective-permute-start | bytes 1179656 | tf_op jit(solution)/shard_map/ppermute | solution.py:38

commit v3 on v2

--- a/solution.py
+++ b/solution.py
@@ -7,7 +7,7 @@
 from jax.experimental.pallas import tpu as pltpu
 from jax.sharding import PartitionSpec as P
 
-OPT = {'pf': 1, 's1_after3': 1, 'w_mode': 'whole', 'pack': 'vmem', 'pack_lim': 60, 's_mode': 'strip', 'z_mode': 'mix', 'e_mode': 'merged', 'sums_za': 1, 'sums_zb': 1, 'ca_zb': 1, 'mine_after': 0, 'st2_after': 1, 'e2_acc': 1, 'e2_s1': 1, 'e2_s2': 1, 'slice_after': 1, 'qtr_after': 'za', 'sums_qtr': 1, 'e1_s': 0, 'order': 'zs', 'c_pack': 0, 'c_slice': 0, 'c_zstack': 0, 'c_qtr': 0, 'c_sums1': 5, 'c_sums2': 0, 'c_join1': 0, 'c_join2': 0, 'c_joinf': 20, 'c_mine': 0, 'c_estack': 0, 'c_e2stack': 0, 'c_prod': 0, 'c_last': 0}
+OPT = {'pl': 0, 'jl': 0, 'ws2': 1, 'f1': 0, 'c_f1': 10, 'jk': 0, 'cot_first': 0, 'held_free': 1, 'c_cots': 10, 'slice_in': 'pack', 'st2_prod': 1, 's1_late': 0, 'c_joinl': 0, 'pf': 1, 's1_after3': 1, 'w_mode': 'whole', 'pack': 'vmem', 'pack_lim': 60, 's_mode': 'strip', 'z_mode': 'mix', 'e_mode': 'merged', 'sums_za': 0, 'sums_zb': 1, 'ca_zb': 0, 'mine_after': 0, 'st2_after': 0, 'e2_acc': 1, 'e2_s1': 1, 'e2_s2': 1, 'slice_after': 0, 'qtr_after': 'za', 'sums_qtr': 1, 'e1_s': 0, 'order': 'zs', 'c_pack': 0, 'c_slice': 0, 'c_zstack': 0, 'c_qtr': 0, 'c_sums1': 0, 'c_sums2': 0, 'c_join1': 0, 'c_join2': 0, 'c_joinf': 20, 'c_mine': 0, 'c_estack': 60, 'c_e2stack': 0, 'c_prod': 10, 'c_last': 0}
 LANES = 128
 PAD = 16
 LOG2_E = 1.4426950408889634
@@ -94,12 +94,21 @@
     js = sorted(range(n_tensor), key=lambda j: (-j.bit_count(), -j)) if OPT["s_mode"] == "strip" else list(range(n_tensor - 1, -1, -1))
     width = n_tensor * 2 * blk
 
-    def pack_body(act, cot, *outs):
+    if OPT["cot_first"]:
+        cots = [across(value_cotangent, q) for q in range(1, chips)]
+        all_cots = stack([value_cotangent, *cots], OPT["c_cots"])
+
+    def pack_body(act, *outs):
+        if not OPT["cot_first"]:
+            cot, *outs = outs
         p, _, t = place()
         for q, out in enumerate(outs, 1):
             for i, j in enumerate(js):
                 out[:, i * 2 * blk : (i + 1) * 2 * blk] = act[:, pl.ds(column(t ^ j, p ^ q), 2 * blk)]
-            out[:, width:] = cot[...]
+            if not OPT["cot_first"]:
+                out[:, width:] = cot[...]
+
+    extra = 0 if OPT["cot_first"] else vdim
 
     def slice_body(weight, out):
         p, c, _ = place()
@@ -131,8 +140,15 @@
             name="pack",
         )(activations, value_cotangent)
     else:
-        packs = kernel_call(pack_body, [shape((tok, width + vdim), bf16)] * (chips - 1), [activations, value_cotangent], name="pack", cost=OPT["c_pack"])
-    (own_slice,) = kernel_call(slice_body, [shape((blk, vdim), bf16)], [value_weight], name="own_slice", cost=OPT["c_slice"])
+        packs = kernel_call(pack_body, [shape((tok, width + extra), bf16)] * (chips - 1), [activations] if OPT["cot_first"] else [activations, value_cotangent], name="pack", cost=OPT["c_pack"])
+    sw = value_weight
+    if OPT["slice_in"] == "cots":
+        sw = barrier((value_weight, all_cots))[0]
+    elif OPT["slice_in"] == "cot1":
+        sw = barrier((value_weight, cots[0]))[0]
+    elif OPT["slice_in"] == "pack":
+        sw, *packs = barrier((value_weight, *packs))
+    (own_slice,) = kernel_call(slice_body, [shape((blk, vdim), bf16)], [sw], name="own_slice", cost=OPT["c_slice"])
     if OPT["slice_after"]:
         own_slice, *packs = barrier((own_slice, *packs))
     got = [across(x, q) for q, x in enumerate(packs, 1)]
@@ -189,7 +205,10 @@
         def body(act, cot, *refs):
             keep, send = refs[-2:]
             p, c, t = place()
-            cots = jnp.concatenate([cot[...]] + [r[:, width:] for r in refs[:-2]], axis=0)
+            if OPT["cot_first"]:
+                cots = cot[...]
+            else:
+                cots = jnp.concatenate([cot[...]] + [r[:, width:] for r in refs[:-2]], axis=0)
             for i, j in enumerate(js_now):
                 for out, core in ((send, 1 - c), (keep, c)):
                     start = pl.multiple_of((offset + i) * 2 * blk + core * blk, LANES)
@@ -197,7 +216,7 @@
                     out[i * blk : (i + 1) * blk, :] = contract(jnp.concatenate(parts, axis=0), cots, 0, 0)
 
         out = shape((len(js_now) * blk, vdim), f32)
-        return kernel_call(body, [out, out], [activations, value_cotangent, *got], name="sums", cost=cost)
+        return kernel_call(body, [out, out], [activations, all_cots if OPT["cot_first"] else value_cotangent, *got], name="sums", cost=cost)
 
     def join(terms, pack, cost):
         def value(ref):
@@ -219,7 +238,9 @@
 
     if OPT["sums_za"]:
         got[0], held[0] = barrier((got[0], held[0]))
-    if OPT["sums_zb"]:
+    if OPT["sums_zb"] and OPT["held_free"]:
+        got[0], *_ = barrier((got[0], *held))
+    elif OPT["sums_zb"]:
         got[0], *held = barrier((got[0], *held))
     if OPT["sums_qtr"]:
         got[0], acc = barrier((got[0], acc))
@@ -235,6 +256,8 @@
     mine = stack(held, OPT["c_mine"])
     if OPT["mine_after"]:
         mine, send_1 = barrier((mine, send_1))
+    if OPT["jk"]:
+        keep_1, keep_2 = barrier((keep_1, keep_2))
     terms = {}
     for names, keep, twins_sum in ((firsts, keep_1, twin(send_1)), (others, keep_2, twin(send_2))):
         for i, j in enumerate(names):
@@ -252,15 +275,26 @@
     for q in singles:
         pieces[q] = [across(mine[c] if len(segs) > 1 else mine, q) for c in segs]
 
+    early = [q for q in range(chips) if q.bit_count() < 2]
+    ours_early = stack([x for q in early for x in pieces[q]], OPT["c_estack"]) if OPT["ws2"] else None
     arrived = {}
     strip = OPT["s_mode"] == "strip"
     for j in js[:-1]:
+        if OPT["ws2"] and j == js[len(firsts)]:
+            terms[j][0], ours_early = barrier((terms[j][0], ours_early))
         packed = join(terms[j], True, OPT["c_join1"] if j in firsts else OPT["c_join2"])
         if j == js[len(firsts)] and OPT["st2_after"]:
             _, *got_now = barrier((packed, *[x for q in singles for x in pieces[q]]))
             pieces.update({q: got_now[i * len(segs) : (i + 1) * len(segs)] for i, q in enumerate(singles)})
         arrived[j] = along(packed, j & -j if strip else j)
-        if OPT["s1_after3"] and strip and j == js[len(firsts)]:
+        if OPT["f1"] and strip and j in firsts:
+            nxt = j & (j - 1)
+            mark = stack([(packed, slice(blk, blk + PAD))], OPT["c_f1"])
+            terms[nxt][0] = barrier((terms[nxt][0], mark))[0]
+        if OPT["s1_after3"] == 2 and strip and j == js[len(firsts)]:
+            for k in others[1:-1]:
+                terms[k] = list(barrier((*terms[k], *[pieces[q][0] for q in singles]))[: len(terms[k])])
+        if OPT["s1_after3"] == 1 and strip and j == js[len(firsts)]:
             for k in others[1:-1]:
                 terms[k] = list(barrier((*terms[k], packed))[:-1])
         if strip and j in firsts:
@@ -278,20 +312,38 @@
             ways.append(across(there[cuts[i] : cuts[i + 1]], b))
         pieces[q] = ways
 
-    total = join(terms[0] + [arrived[j].astype(f32) for j in (others[:-1] if strip else js[:-1])], False, OPT["c_joinf"])
-    weight_grad = total / jnp.sqrt(f32(tok * n_dp * n_tensor))
-    if OPT["pf"]:
-        acc, total = barrier((acc, total))
+    def finish(after):
+        own = terms[0]
+        if after is not None:
+            own = [*barrier((own[0], after))[:1], *own[1:]]
+        if OPT["s1_late"]:
+            total = join(own + [arrived[others[0]].astype(f32)], False, OPT["c_joinf"])
+            return join([total] + [arrived[j].astype(f32) for j in others[1:-1]], False, OPT["c_joinl"])
+        return join(own + [arrived[j].astype(f32) for j in (others[:-1] if strip else js[:-1])], False, OPT["c_joinf"])
+
+    results = []
+    if not OPT["jl"]:
+        results.append(finish(None))
+        if OPT["pf"]:
+            acc, results[0] = barrier((acc, results[0]))
 
     def product(acc, grad, qs, last):
         n = (n_tensor - 1) * len(qs)
-        ours = stack([x for q in qs for x in pieces[q]], OPT["c_e2stack"] if last else OPT["c_estack"])
+        if OPT["ws2"] and not last:
+            ours = ours_early
+        elif OPT["pl"] and last:
+            ours = ours_late
+        else:
+            ours = stack([x for q in qs for x in pieces[q]], OPT["c_e2stack"] if last else OPT["c_estack"])
         if last:
             after = [acc] * OPT["e2_acc"] + [arrived[1]] * OPT["e2_s1"] + [arrived[n_tensor // 2]] * OPT["e2_s2"]
-            ours, *_ = barrier((ours, *after))
+            if not OPT["pl"]:
+                ours, *_ = barrier((ours, *after))
         elif OPT["e1_s"]:
             ours, *_ = barrier((ours, arrived[1]))
         operands = [ours, twin(ours)]
+        if last and OPT["jl"]:
+            results.append(finish(ours))
 
         def body(act, cot, acc, _, *refs):
             both, (out, grad, total, columns, sems) = refs[:2], refs[-5:]
@@ -335,9 +387,17 @@
         )(*args)
 
     late = [q for q in range(chips) if q.bit_count() >= 2]
+    if OPT["pl"] and late:
+        ours_late = stack([x for q in late for x in pieces[q]], OPT["c_e2stack"])
+        acc, ours_late = barrier((acc, ours_late))
     acc, grad = product(acc, grad, [0, *singles], not late)
     if late:
+        if OPT["st2_prod"]:
+            acc, *parts = barrier((acc, *[x for q in late for x in pieces[q]]))
+            for q in late:
+                pieces[q], parts = parts[: len(pieces[q])], parts[len(pieces[q]) :]
         acc, grad = product(acc, grad, late, True)
+    weight_grad = results[0] / jnp.sqrt(f32(tok * n_dp * n_tensor))
     return acc, grad, weight_grad
 
 

time: 51.7 us -> 49.2 us (0.952)
  waiting for transfers between devices: 20.6 us -> 17.6 us
  starting transfers between devices: 20.7 us -> 21.5 us
    ppermute x17, waiting for transfers between devices: 20.6 us -> 17.6 us  [exchange(): return lax.ppermute(x, AXES, pairs)]
    ppermute x17, starting transfers between devices: 20.7 us -> 21.5 us  [exchange(): return lax.ppermute(x, AXES, pairs)]
    unnamed x6 -> x10, local copies, waits for them, and re-layouts: 2.43 us -> 2.14 us
  transfers between devices with their start and end apart: 17 -> 17, of which waited for: 9 -> 10; matrix products, arithmetic and copies ran while one was open for 2% -> 2% of each run, Pallas kernels for 4% -> 9%
where the time goes in v3:
time: 49.2 us; the launch traced here: 49.1 us
  starting transfers between devices  21.5 us (44%)
  waiting for transfers between devices  17.6 us (36%)
  Pallas kernels  6.01 us (12%)
  local copies, waits for them, and re-layouts  2.27 us (5%)
  between operations  0.88 us (2%)
  other arithmetic  0.86 us (2%)
    ppermute x17, starting transfers between devices, exchange(): return lax.ppermute(x, AXES, pairs)  21.5 us
    ppermute x17, waiting for transfers between devices, exchange(): return lax.ppermute(x, AXES, pairs)  17.6 us
    pallas_call x2, Pallas kernels, product(): pl.pallas_call(body, out_shape=[shape((tok, vdim), bf16 if last else f32)...  2.98 us
    unnamed x10, local copies, waits for them, and re-layouts  2.14 us
    pallas_call x11, Pallas kernels, kernel_call(): pl.pallas_call(body, out_shape=out_shapes, in_specs=[whole] * len(args),...  1.82 us
    pallas_call x1, Pallas kernels, paired_form(): pl.pallas_call(quarter_body, out_shape=[shape((tok, vdim), f32), shape((t...  1.21 us
  transfers between devices with their start and end apart: 17, of which 10 were waited for; matrix products, arithmetic and copies ran while one was open for 2% of the time, Pallas kernels for 9%

profile of v3, /device:TPU:0, one launch (start us, length us, event | category | flops | bytes accessed | tf_op | source)
XLA Modules:
  0.0 49.1 jit_solution(586480330583445352)
XLA Ops:
  0.6 1.2 %copy-done = bf16[128,4096]{1,0:T(8,128)(2,1)S(1)} copy-done((bf16[128,4096]{1,0:T(8,128)(2,1)S(1)}, bf16[128,4096]{1,0:T(8,128)(2,1)}, u32[]{:S(2)}) %copy-start) | copy-done | bytes 1048600
  1.9 0.9 %copy-done.3 = bf16[128,512]{1,0:T(8,128)(2,1)S(1)} copy-done((bf16[128,512]{1,0:T(8,128)(2,1)S(1)}, bf16[128,512]{1,0:T(8,128)(2,1)}, u32[]{:S(2)}) %copy-start.3) | copy-done | bytes 131096
  2.9 3.0 %collective-permute-start = (bf16[128,1536]{1,0:T(8,128)(2,1)S(1)}, bf16[128,1536]{1,0:T(8,128)(2,1)S(1)}, u32[]{:S(2)}, u32[]{:S(2)}) collective-permute-start(bf16[128,1536]{1,0:T(8,128)(2,1)S(1)} %get-tuple-element.36), channel_id=1, source_target_pairs={{0,8},{1,9},{2,10},{3,11},{4,12},{5,13},{6,14},{7,15},{8,0},{9,1},... | collective-permute-start | bytes 1179656 | tf_op jit(solution)/shard_map/ppermute | solution.py:38
  5.9 1.5 %collective-permute-start.4 = (bf16[128,1536]{1,0:T(8,128)(2,1)S(1)}, bf16[128,1536]{1,0:T(8,128)(2,1)S(1)}, u32[]{:S(2)}, u32[]{:S(2)}) collective-permute-start(bf16[128,1536]{1,0:T(8,128)(2,1)S(1)} %get-tuple-element.42), channel_id=1, source_target_pairs={{0,16},{1,17},{2,18},{3,19},{4,20},{5,21},{6,22},{7,23},{8,24},{9,... | collective-permute-start | bytes 1179656 | tf_op jit(solution)/shard_map/ppermute | solution.py:38
  7.5 3.1 %collective-permute-start.1 = (bf16[128,512]{1,0:T(8,128)(2,1)S(1)}, bf16[128,512]{1,0:T(8,128)(2,1)S(1)}, u32[]{:S(2)}, u32[]{:S(2)}) collective-permute-start(bf16[128,512]{1,0:T(8,128)(2,1)S(1)} %own_slice.1), channel_id=1, source_target_pairs={{0,2},{1,3},{2,0},{3,1},{4,6},{5,7},{6,4},{7,5},{8,10},{9,11},{10,... | collective-permute-start | bytes 393224 | tf_op jit(solution)/shard_map/ppermute | solution.py:38
  10.6 1.6 %collective-permute-start.2 = (bf16[128,512]{1,0:T(8,128)(2,1)S(1)}, bf16[128,512]{1,0:T(8,128)(2,1)S(1)}, u32[]{:S(2)}, u32[]{:S(2)}) collective-permute-start(bf16[128,512]{1,0:T(8,128)(2,1)S(1)} %own_slice.1), channel_id=1, source_target_pairs={{0,1},{1,0},{2,3},{3,2},{4,5},{5,4},{6,7},{7,6},{8,9},{9,8},{10,11... | collective-permute-start | bytes 393224 | tf_op jit(solution)/shard_map/ppermute | solution.py:38
  12.2 4.0 %collective-permute-done.1.refs_0_ = bf16[128,512]{1,0:T(8,128)(2,1)S(1)} collective-permute-done((bf16[128,512]{1,0:T(8,128)(2,1)S(1)}, bf16[128,512]{1,0:T(8,128)(2,1)S(1)}, u32[]{:S(2)}, u32[]{:S(2)}) %collective-permute-start.1) | collective-permute-done | bytes 131104 | tf_op jit(solution)/shard_map/ppermute | solution.py:38
  16.2 0.6 %collective-permute-start.3 = (bf16[128,512]{1,0:T(8,128)(2,1)S(1)}, bf16[128,512]{1,0:T(8,128)(2,1)S(1)}, u32[]{:S(2)}, u32[]{:S(2)}) collective-permute-start(bf16[128,512]{1,0:T(8,128)(2,1)S(1)} %collective-permute-done.1.refs_0_), channel_id=1, source_target_pairs={{0,1},{1,0},{2,3},{3,2},{4,5},{5,4},{6,7},{7,6},{8,9},{9,8},{10,11... | collective-permute-start | bytes 393224 | tf_op jit(solution)/shard_map/ppermute | solution.py:38
  16.8 4.3 %collective-permute-done.3.refs_2_ = bf16[128,512]{1,0:T(8,128)(2,1)S(1)} collective-permute-done((bf16[128,512]{1,0:T(8,128)(2,1)S(1)}, bf16[128,512]{1,0:T(8,128)(2,1)S(1)}, u32[]{:S(2)}, u32[]{:S(2)}) %collective-permute-start.3) | collective-permute-done | bytes 131104 | tf_op jit(solution)/shard_map/ppermute | solution.py:38
  21.2 1.6 %collective-permute-start.8 = (bf16[384,512]{1,0:T(8,128)(2,1)S(1)}, bf16[384,512]{1,0:T(8,128)(2,1)S(1)}, u32[]{:S(2)}, u32[]{:S(2)}) collective-permute-start(bf16[384,512]{1,0:T(8,128)(2,1)S(1)} %stack.3.refs_0_), channel_id=1, source_target_pairs={{0,16},{1,17},{2,18},{3,19},{4,20},{5,21},{6,22},{7,23},{8,24},{9,... | collective-permute-start | bytes 1179656 | tf_op jit(solution)/shard_map/ppermute | solution.py:38
  22.8 1.5 %collective-permute-start.7 = (bf16[384,512]{1,0:T(8,128)(2,1)S(1)}, bf16[384,512]{1,0:T(8,128)(2,1)S(1)}, u32[]{:S(2)}, u32[]{:S(2)}) collective-permute-start(bf16[384,512]{1,0:T(8,128)(2,1)S(1)} %stack.3.refs_0_), channel_id=1, source_target_pairs={{0,8},{1,9},{2,10},{3,11},{4,12},{5,13},{6,14},{7,15},{8,0},{9,1},... | collective-permute-start | bytes 1179656 | tf_op jit(solution)/shard_map/ppermute | solution.py:38
  24.3 1.2 %own_quarter.1 = (f32[128,512]{1,0:T(8,128)S(1)}, bf16[128,4096]{1,0:T(8,128)(2,1)}) custom-call(bf16[128,4096]{1,0:T(8,128)(2,1)S(1)} %copy-done.1, bf16[128,512]{1,0:T(8,128)(2,1)S(1)} %copy-done.4, bf16[1024,512]{1,0:T(8,128)(2,1)S(1)} %copy-done.2), custom_call_target="tpu_custom_call" | custom-call | bytes 1024 | tf_op jit(solution)/shard_map/own_quarter/pallas_call | solution.py:192
  26.3 0.6 %sums.2 = (f32[384,512]{1,0:T(8,128)S(1)}, f32[384,512]{1,0:T(8,128)S(1)}) custom-call(bf16[128,4096]{1,0:T(8,128)(2,1)S(1)} %copy-done.1, bf16[128,512]{1,0:T(8,128)(2,1)S(1)} %copy-done.4, bf16[128,1536]{1,0:T(8,128)(2,1)S(1)} %collective-permute-done.refs_0_, bf16[128,1536]{1,0:T(8,128)(2,1)S(1)} %collective-permute-done.4.refs_1_, ...), custom_call_target="tpu_custom_call" | custom-call | bytes 1024 | tf_op jit(solution)/shard_map/sums/pallas_call | solution.py:43
  26.9 0.6 %collective-permute-start.6 = (f32[384,512]{1,0:T(8,128)S(1)}, f32[384,512]{1,0:T(8,128)S(1)}, u32[]{:S(2)}, u32[]{:S(2)}) collective-permute-start(f32[384,512]{1,0:T(8,128)S(1)} %get-tuple-element.45), channel_id=1, source_target_pairs={{0,4},{1,5},{2,6},{3,7},{4,0},{5,1},{6,2},{7,3},{8,12},{9,13},{10,... | collective-permute-start | bytes 2359304 | tf_op jit(solution)/shard_map/ppermute | solution.py:38
  28.0 1.6 %collective-permute-start.10 = (f16[144,512]{1,0:T(8,128)(2,1)S(1)}, f16[144,512]{1,0:T(8,128)(2,1)S(1)}, u32[]{:S(2)}, u32[]{:S(2)}) collective-permute-start(f16[144,512]{1,0:T(8,128)(2,1)S(1)} %convert_element_type.18), channel_id=1, source_target_pairs={{0,1},{1,0},{2,3},{3,2},{4,5},{5,4},{6,7},{7,6},{8,9},{9,8},{10,11... | collective-permute-start | bytes 442376 | tf_op jit(solution)/shard_map/ppermute | solution.py:38
  29.7 3.7 %collective-permute-done.8.refs_2_ = bf16[384,512]{1,0:T(8,128)(2,1)S(1)} collective-permute-done((bf16[384,512]{1,0:T(8,128)(2,1)S(1)}, bf16[384,512]{1,0:T(8,128)(2,1)S(1)}, u32[]{:S(2)}, u32[]{:S(2)}) %collective-permute-start.8) | collective-permute-done | bytes 393248 | tf_op jit(solution)/shard_map/ppermute | solution.py:38
  34.3 2.7 %collective-permute-start.11 = (f16[144,512]{1,0:T(8,128)(2,1)S(1)}, f16[144,512]{1,0:T(8,128)(2,1)S(1)}, u32[]{:S(2)}, u32[]{:S(2)}) collective-permute-start(f16[144,512]{1,0:T(8,128)(2,1)S(1)} %convert_element_type.20), channel_id=1, source_target_pairs={{0,2},{1,3},{2,0},{3,1},{4,6},{5,7},{6,4},{7,5},{8,10},{9,11},{10,... | collective-permute-start | bytes 442376 | tf_op jit(solution)/shard_map/ppermute | solution.py:38
  37.2 1.6 %collective-permute-start.12 = (f16[144,512]{1,0:T(8,128)(2,1)S(1)}, f16[144,512]{1,0:T(8,128)(2,1)S(1)}, u32[]{:S(2)}, u32[]{:S(2)}) collective-permute-start(f16[144,512]{1,0:T(8,128)(2,1)S(1)} %convert_element_type.22), channel_id=1, source_target_pairs={{0,1},{1,0},{2,3},{3,2},{4,5},{5,4},{6,7},{7,6},{8,9},{9,8},{10,11... | collective-permute-start | bytes 442376 | tf_op jit(solution)/shard_map/ppermute | solution.py:38
  38.8 1.5 %collective-permute-start.14 = (bf16[192,512]{1,0:T(8,128)(2,1)S(1)}, bf16[192,512]{1,0:T(8,128)(2,1)S(1)}, u32[]{:S(2)}, u32[]{:S(2)}) collective-permute-start(bf16[192,512]{1,0:T(8,128)(2,1)S(1)} %slice.35), channel_id=1, source_target_pairs={{0,8},{1,9},{2,10},{3,11},{4,12},{5,13},{6,14},{7,15},{8,0},{9,1},... | collective-permute-start | bytes 589832 | tf_op jit(solution)/shard_map/ppermute | solution.py:38
  40.7 3.0 %collective-permute-done.11 = f16[144,512]{1,0:T(8,128)(2,1)S(1)} collective-permute-done((f16[144,512]{1,0:T(8,128)(2,1)S(1)}, f16[144,512]{1,0:T(8,128)(2,1)S(1)}, u32[]{:S(2)}, u32[]{:S(2)}) %collective-permute-start.11) | collective-permute-done | bytes 147488 | tf_op jit(solution)/shard_map/ppermute | solution.py:38
  44.2 1.8 %product.2 = (f32[128,512]{1,0:T(8,128)S(1)}, bf16[128,4096]{1,0:T(8,128)(2,1)}) custom-call(bf16[128,4096]{1,0:T(8,128)(2,1)S(1)} %copy-done.1, bf16[128,512]{1,0:T(8,128)(2,1)S(1)} %copy-done.4, f32[128,512]{1,0:T(8,128)S(1)} %get-tuple-element.51.acc, bf16[128,4096]{1,0:T(8,128)(2,1)} %get-tuple-element.52._, ...), custom_call_target="tpu_custom_call", output_to_operand_aliasing={{1}: (3, {})} | custom-call | flops 11500000256 | bytes 1024 | tf_op jit(solution)/shard_map/product/pallas_call | solution.py:373
  46.2 0.7 %broadcast_multiply_fusion = f32[128,512]{1,0:T(8,128)} fusion(f32[128,512]{1,0:T(8,128)S(1)} %join.7), kind=kLoop, calls=%fused_computation | loop fusion | flops 65536 | bytes 524288 | tf_op jit(solution)/shard_map/div | solution.py:400
  46.9 1.0 %collective-permute-done.16.refs_1_ = bf16[384,512]{1,0:T(8,128)(2,1)S(1)} collective-permute-done((bf16[384,512]{1,0:T(8,128)(2,1)S(1)}, bf16[384,512]{1,0:T(8,128)(2,1)S(1)}, u32[]{:S(2)}, u32[]{:S(2)}) %collective-permute-start.16) | collective-permute-done | bytes 393248 | tf_op jit(solution)/shard_map/ppermute | solution.py:38
  47.9 1.1 %product.3 = (bf16[128,512]{1,0:T(8,128)(2,1)}, bf16[128,4096]{1,0:T(8,128)(2,1)}) custom-call(bf16[128,4096]{1,0:T(8,128)(2,1)S(1)} %copy-done.1, bf16[128,512]{1,0:T(8,128)(2,1)S(1)} %copy-done.4, f32[128,512]{1,0:T(8,128)S(1)} %get-tuple-element.55.acc, bf16[128,4096]{1,0:T(8,128)(2,1)} %get-tuple-element.56._, ...), custom_call_target="tpu_custom_call", output_to_operand_aliasing={{1}: (3, {})} | custom-call | bytes 1024 | tf_op jit(solution)/shard_map/product/pallas_call | solution.py:373
  (45 shorter events, 3.6 us)
Async XLA Ops:
  0.6 1.2 %copy-start = (bf16[128,4096]{1,0:T(8,128)(2,1)S(1)}, bf16[128,4096]{1,0:T(8,128)(2,1)}, u32[]{:S(2)}) copy-start(bf16[128,4096]{1,0:T(8,128)(2,1)} %act.11) | copy-start | bytes 3145732
  1.9 0.9 %copy-start.3 = (bf16[128,512]{1,0:T(8,128)(2,1)S(1)}, bf16[128,512]{1,0:T(8,128)(2,1)}, u32[]{:S(2)}) copy-start(bf16[128,512]{1,0:T(8,128)(2,1)} %cot.9) | copy-start | bytes 393220
  2.8 4.7 %copy-start.2 = (bf16[1024,512]{1,0:T(8,128)(2,1)S(1)}, bf16[1024,512]{1,0:T(8,128)(2,1)}, u32[]{:S(2)}) copy-start(bf16[1024,512]{1,0:T(8,128)(2,1)} %w.1) | copy-start | bytes 3145732
  2.9 21.4 %copy-start.1 = (bf16[128,4096]{1,0:T(8,128)(2,1)S(1)}, bf16[128,4096]{1,0:T(8,128)(2,1)}, u32[]{:S(2)}) copy-start(bf16[128,4096]{1,0:T(8,128)(2,1)} %act.11) | copy-start | bytes 3145732
  2.9 21.4 %copy-start.4 = (bf16[128,512]{1,0:T(8,128)(2,1)S(1)}, bf16[128,512]{1,0:T(8,128)(2,1)}, u32[]{:S(2)}) copy-start(bf16[128,512]{1,0:T(8,128)(2,1)} %cot.9) | copy-start | bytes 393220
  2.9 22.6 %collective-permute-start = (bf16[128,1536]{1,0:T(8,128)(2,1)S(1)}, bf16[128,1536]{1,0:T(8,128)(2,1)S(1)}, u32[]{:S(2)}, u32[]{:S(2)}) collective-permute-start(bf16[128,1536]{1,0:T(8,128)(2,1)S(1)} %get-tuple-element.36), channel_id=1, source_target_pairs={{0,8},{1,9},{2,10},{3,11},{4,12},{5,13},{6,14},{7,15},{8,0},{9,1},... | collective-permute-start | bytes 1179656 | tf_op jit(solution)/shard_map/ppermute | solution.py:38
  5.9 19.6 %collective-permute-start.4 = (bf16[128,1536]{1,0:T(8,128)(2,1)S(1)}, bf16[128,1536]{1,0:T(8,128)(2,1)S(1)}, u32[]{:S(2)}, u32[]{:S(2)}) collective-permute-start(bf16[128,1536]{1,0:T(8,128)(2,1)S(1)} %get-tuple-element.42), channel_id=1, source_target_pairs={{0,16},{1,17},{2,18},{3,19},{4,20},{5,21},{6,22},{7,23},{8,24},{9,... | collective-permute-start | bytes 1179656 | tf_op jit(solution)/shard_map/ppermute | solution.py:38
  7.4 18.4 %collective-permute-start.5 = (bf16[128,1536]{1,0:T(8,128)(2,1)S(1)}, bf16[128,1536]{1,0:T(8,128)(2,1)S(1)}, u32[]{:S(2)}, u32[]{:S(2)}) collective-permute-start(bf16[128,1536]{1,0:T(8,128)(2,1)S(1)} %get-tuple-element.43), channel_id=1, source_target_pairs={{0,24},{1,25},{2,26},{3,27},{4,28},{5,29},{6,30},{7,31},{8,16},{9,... | collective-permute-start | bytes 1179656 | tf_op jit(solution)/shard_map/ppermute | solution.py:38
  7.5 8.7 %collective-permute-start.1 = (bf16[128,512]{1,0:T(8,128)(2,1)S(1)}, bf16[128,512]{1,0:T(8,128)(2,1)S(1)}, u32[]{:S(2)}, u32[]{:S(2)}) collective-permute-start(bf16[128,512]{1,0:T(8,128)(2,1)S(1)} %own_slice.1), channel_id=1, source_target_pairs={{0,2},{1,3},{2,0},{3,1},{4,6},{5,7},{6,4},{7,5},{8,10},{9,11},{10,... | collective-permute-start | bytes 393224 | tf_op jit(solution)/shard_map/ppermute | solution.py:38
  10.6 6.2 %collective-permute-start.2 = (bf16[128,512]{1,0:T(8,128)(2,1)S(1)}, bf16[128,512]{1,0:T(8,128)(2,1)S(1)}, u32[]{:S(2)}, u32[]{:S(2)}) collective-permute-start(bf16[128,512]{1,0:T(8,128)(2,1)S(1)} %own_slice.1), channel_id=1, source_target_pairs={{0,1},{1,0},{2,3},{3,2},{4,5},{5,4},{6,7},{7,6},{8,9},{9,8},{10,11... | collective-permute-start | bytes 393224 | tf_op jit(solution)/shard_map/ppermute | solution.py:38
  16.2 5.0 %collective-permute-start.3 = (bf16[128,512]{1,0:T(8,128)(2,1)S(1)}, bf16[128,512]{1,0:T(8,128)(2,1)S(1)}, u32[]{:S(2)}, u32[]{:S(2)}) collective-permute-start(bf16[128,512]{1,0:T(8,128)(2,1)S(1)} %collective-permute-done.1.refs_0_), channel_id=1, source_target_pairs={{0,1},{1,0},{2,3},{3,2},{4,5},{5,4},{6,7},{7,6},{8,9},{9,8},{10,11... | collective-permute-start | bytes 393224 | tf_op jit(solution)/shard_map/ppermute | solution.py:38
  21.2 12.2 %collective-permute-start.8 = (bf16[384,512]{1,0:T(8,128)(2,1)S(1)}, bf16[384,512]{1,0:T(8,128)(2,1)S(1)}, u32[]{:S(2)}, u32[]{:S(2)}) collective-permute-start(bf16[384,512]{1,0:T(8,128)(2,1)S(1)} %stack.3.refs_0_), channel_id=1, source_target_pairs={{0,16},{1,17},{2,18},{3,19},{4,20},{5,21},{6,22},{7,23},{8,24},{9,... | collective-permute-start | bytes 1179656 | tf_op jit(solution)/shard_map/ppermute | solution.py:38
  22.8 10.6 %collective-permute-start.7 = (bf16[384,512]{1,0:T(8,128)(2,1)S(1)}, bf16[384,512]{1,0:T(8,128)(2,1)S(1)}, u32[]{:S(2)}, u32[]{:S(2)}) collective-permute-start(bf16[384,512]{1,0:T(8,128)(2,1)S(1)} %stack.3.refs_0_), channel_id=1, source_target_pairs={{0,8},{1,9},{2,10},{3,11},{4,12},{5,13},{6,14},{7,15},{8,0},{9,1},... | collective-permute-start | bytes 1179656 | tf_op jit(solution)/shard_map/ppermute | solution.py:38
  26.2 1.6 %collective-permute-start.9 = (f32[128,512]{1,0:T(8,128)S(1)}, f32[128,512]{1,0:T(8,128)S(1)}, u32[]{:S(2)}, u32[]{:S(2)}) collective-permute-start(f32[128,512]{1,0:T(8,128)S(1)} %get-tuple-element.48), channel_id=1, source_target_pairs={{0,4},{1,5},{2,6},{3,7},{4,0},{5,1},{6,2},{7,3},{8,12},{9,13},{10,... | collective-permute-start | bytes 786440 | tf_op jit(solution)/shard_map/ppermute | solution.py:38
  26.9 7.1 %collective-permute-start.6 = (f32[384,512]{1,0:T(8,128)S(1)}, f32[384,512]{1,0:T(8,128)S(1)}, u32[]{:S(2)}, u32[]{:S(2)}) collective-permute-start(f32[384,512]{1,0:T(8,128)S(1)} %get-tuple-element.45), channel_id=1, source_target_pairs={{0,4},{1,5},{2,6},{3,7},{4,0},{5,1},{6,2},{7,3},{8,12},{9,13},{10,... | collective-permute-start | bytes 2359304 | tf_op jit(solution)/shard_map/ppermute | solution.py:38
  28.0 6.0 %collective-permute-start.10 = (f16[144,512]{1,0:T(8,128)(2,1)S(1)}, f16[144,512]{1,0:T(8,128)(2,1)S(1)}, u32[]{:S(2)}, u32[]{:S(2)}) collective-permute-start(f16[144,512]{1,0:T(8,128)(2,1)S(1)} %convert_element_type.18), channel_id=1, source_target_pairs={{0,1},{1,0},{2,3},{3,2},{4,5},{5,4},{6,7},{7,6},{8,9},{9,8},{10,11... | collective-permute-start | bytes 442376 | tf_op jit(solution)/shard_map/ppermute | solution.py:38
  34.3 9.4 %collective-permute-start.11 = (f16[144,512]{1,0:T(8,128)(2,1)S(1)}, f16[144,512]{1,0:T(8,128)(2,1)S(1)}, u32[]{:S(2)}, u32[]{:S(2)}) collective-permute-start(f16[144,512]{1,0:T(8,128)(2,1)S(1)} %convert_element_type.20), channel_id=1, source_target_pairs={{0,2},{1,3},{2,0},{3,1},{4,6},{5,7},{6,4},{7,5},{8,10},{9,11},{10,... | collective-permute-start | bytes 442376 | tf_op jit(solution)/shard_map/ppermute | solution.py:38
  37.2 6.9 %collective-permute-start.12 = (f16[144,512]{1,0:T(8,128)(2,1)S(1)}, f16[144,512]{1,0:T(8,128)(2,1)S(1)}, u32[]{:S(2)}, u32[]{:S(2)}) collective-permute-start(f16[144,512]{1,0:T(8,128)(2,1)S(1)} %convert_element_type.22), channel_id=1, source_target_pairs={{0,1},{1,0},{2,3},{3,2},{4,5},{5,4},{6,7},{7,6},{8,9},{9,8},{10,11... | collective-permute-start | bytes 442376 | tf_op jit(solution)/shard_map/ppermute | solution.py:38
  38.8 7.2 %collective-permute-start.14 = (bf16[192,512]{1,0:T(8,128)(2,1)S(1)}, bf16[192,512]{1,0:T(8,128)(2,1)S(1)}, u32[]{:S(2)}, u32[]{:S(2)}) collective-permute-start(bf16[192,512]{1,0:T(8,128)(2,1)S(1)} %slice.35), channel_id=1, source_target_pairs={{0,8},{1,9},{2,10},{3,11},{4,12},{5,13},{6,14},{7,15},{8,0},{9,1},... | collective-permute-start | bytes 589832 | tf_op jit(solution)/shard_map/ppermute | solution.py:38
  40.4 5.7 %collective-permute-start.15 = (bf16[192,512]{1,0:T(8,128)(2,1)S(1)}, bf16[192,512]{1,0:T(8,128)(2,1)S(1)}, u32[]{:S(2)}, u32[]{:S(2)}) collective-permute-start(bf16[192,512]{1,0:T(8,128)(2,1)S(1)} %slice.36), channel_id=1, source_target_pairs={{0,16},{1,17},{2,18},{3,19},{4,20},{5,21},{6,22},{7,23},{8,24},{9,... | collective-permute-start | bytes 589832 | tf_op jit(solution)/shard_map/ppermute | solution.py:38
  40.7 3.5 %collective-permute-start.13 = (bf16[1152,512]{1,0:T(8,128)(2,1)S(1)}, bf16[1152,512]{1,0:T(8,128)(2,1)S(1)}, u32[]{:S(2)}, u32[]{:S(2)}) collective-permute-start(bf16[1152,512]{1,0:T(8,128)(2,1)S(1)} %stack.4.refs_0_), channel_id=1, source_target_pairs={{0,4},{1,5},{2,6},{3,7},{4,0},{5,1},{6,2},{7,3},{8,12},{9,13},{10,... | collective-permute-start | bytes 3538952 | tf_op jit(solution)/shard_map/ppermute | solution.py:38
  46.1 1.8 %collective-permute-start.16 = (bf16[384,512]{1,0:T(8,128)(2,1)S(1)}, bf16[384,512]{1,0:T(8,128)(2,1)S(1)}, u32[]{:S(2)}, u32[]{:S(2)}) collective-permute-start(bf16[384,512]{1,0:T(8,128)(2,1)S(1)} %stack.5.refs_0_), channel_id=1, source_target_pairs={{0,4},{1,5},{2,6},{3,7},{4,0},{5,1},{6,2},{7,3},{8,12},{9,13},{10,... | collective-permute-start | bytes 1179656 | tf_op jit(solution)/shard_map/ppermute | solution.py:38

commit v4 on v2

v4 whole, which is shorter than its diff:
```python
import math

import jax
import jax.numpy as jnp
from jax import lax
from jax.experimental import pallas as pl
from jax.experimental.pallas import tpu as pltpu
from jax.sharding import PartitionSpec as P

OPT = {'s1t': 0, 's1e': 0, 'tok': 1, 'jl': 0, 'c_pack': 0, 'c_slice': 0, 'c_qtr': 0, 'c_sums1': 30, 'c_sums2': 20, 'c_join1': 0, 'c_join2': 30, 'c_join3': 0, 'c_joinf': 5, 'c_mine': 0, 'c_estack': 60, 'c_e2stack': 0, 'c_prod': 0, 'c_last': 0, 's1p': 2, 'ws2': 1, 'st2_after': 2, 'e2p': 0, 'pt': 0}
LANES = 128
PAD = 16
LOG2_E = 1.4426950408889634
TOP_POWER = 14.0
AXES = ("dp", "tensor")
VMEM_LIMIT = 32 * 1024 * 1024
PACK_LIMIT = 60 * 1024 * 1024


def contract(a, b, dim_a, dim_b):
    return lax.dot_general(a, b, (((dim_a,), (dim_b,)), ((), ())), preferred_element_type=jnp.float32)


def gathered_form(activations, value_weight, value_cotangent):
    tok_rows = activations.shape[0]
    full_weight = lax.all_gather(value_weight, "tensor", axis=0, tiled=True)
    value_proj = contract(activations, full_weight, 1, 0).astype(jnp.bfloat16)
    input_grad = contract(value_cotangent, full_weight, 1, 1).astype(jnp.bfloat16)
    own_columns = lax.all_to_all(activations, "tensor", split_axis=1, concat_axis=0, tiled=True)
    group_term = contract(own_columns, lax.all_gather(value_cotangent, "tensor", axis=0, tiled=True), 0, 0)
    summed = lax.psum_scatter(group_term, "dp", scatter_dimension=0, tiled=True)
    total_tokens = tok_rows * lax.axis_size("dp") * lax.axis_size("tensor")
    return value_proj, input_grad, summed / jnp.sqrt(jnp.float32(total_tokens))


def exchange(x, n_dp, n_tensor, dp_xor, tensor_xor):
    pairs = [(d * n_tensor + t, (d ^ dp_xor) * n_tensor + (t ^ tensor_xor)) for d in range(n_dp) for t in range(n_tensor)]
    return lax.ppermute(x, AXES, pairs)


def estimate(cost):
    return pl.CostEstimate(flops=int(cost * 1.15e9), bytes_accessed=1024, transcendentals=0)


def kernel_call(body, out_shapes, args, name, cost=0):
    whole = pl.BlockSpec(memory_space=pltpu.VMEM)
    return pl.pallas_call(
        body,
        out_shape=out_shapes,
        in_specs=[whole] * len(args),
        out_specs=[whole] * len(out_shapes),
        compiler_params=pltpu.CompilerParams(vmem_limit_bytes=VMEM_LIMIT),
        cost_estimate=estimate(cost),
        name=name,
    )(*args)


def stack(parts, cost=0):
    parts = [p if isinstance(p, tuple) else (p, slice(0, p.shape[0])) for p in parts]

    def body(*refs):
        at = 0
        for ref, (_, cut) in zip(refs, parts):
            refs[-1][at : at + cut.stop - cut.start, :] = ref[cut, :]
            at += cut.stop - cut.start

    rows = sum(cut.stop - cut.start for _, cut in parts)
    out = jax.ShapeDtypeStruct((rows, parts[0][0].shape[1]), parts[0][0].dtype)
    return kernel_call(body, [out], [p for p, _ in parts], "stack", cost)[0]


def paired_form(n_dp, n_tensor, activations, value_weight, value_cotangent):
    tok, depth = activations.shape
    vdim = value_cotangent.shape[1]
    blk = depth // (n_dp * n_tensor)
    chips = n_dp // 2
    quarter = depth // n_tensor
    bf16, f32 = jnp.bfloat16, jnp.float32
    shape = jax.ShapeDtypeStruct
    barrier = lax.optimization_barrier
    whole, anywhere = pl.BlockSpec(memory_space=pltpu.VMEM), pl.BlockSpec(memory_space=pl.ANY)
    root = math.sqrt(tok * n_dp * n_tensor)

    def twin(x):
        return exchange(x, n_dp, n_tensor, 1, 0)

    def across(x, chip_xor):
        return exchange(x, n_dp, n_tensor, 2 * chip_xor, 0)

    def along(x, tensor_xor):
        return exchange(x, n_dp, n_tensor, 0, tensor_xor)

    def column(part, chip, core=0):
        return pl.multiple_of(((part * chips + chip) * 2 + core) * blk, LANES)

    def place():
        d = lax.axis_index("dp")
        return d // 2, d % 2, lax.axis_index("tensor")

    if OPT["s1e"]:
        js = sorted(range(1, n_tensor), key=lambda j: (-j.bit_count(), -j if j.bit_count() > 1 else j)) + [0]
    else:
        js = sorted(range(n_tensor), key=lambda j: (-j.bit_count(), -j))
    half = max(1, sum(j.bit_count() > 1 for j in js))
    width = n_tensor * 2 * blk

    def pack_body(act, cot, *outs):
        p, _, t = place()
        for q, out in enumerate(outs, 1):
            for i, j in enumerate(js):
                out[:, i * 2 * blk : (i + 1) * 2 * blk] = act[:, pl.ds(column(t ^ j, p ^ q), 2 * blk)]
            out[:, width:] = cot[...]

    def slice_body(weight, out):
        p, c, _ = place()
        out[...] = weight[pl.ds(pl.multiple_of((p * 2 + c) * blk, LANES), blk), :]

    packs = kernel_call(pack_body, [shape((tok, width + vdim), bf16)] * (chips - 1), [activations, value_cotangent], "pack", OPT["c_pack"])
    weight_then, *packs = barrier((value_weight, *packs))
    (own_slice,) = kernel_call(slice_body, [shape((blk, vdim), bf16)], [weight_then], "own_slice", OPT["c_slice"])
    got = [across(x, q) for q, x in enumerate(packs, 1)]

    slots = sorted(range(1, n_tensor), key=lambda j: (j.bit_count(), -j))
    by_slot = {0: own_slice}
    for j in slots:
        by_slot[j] = along(by_slot[j & (j - 1)], j & -j)
    held = [by_slot[j] for j in slots]

    def quarter_body(act, cot, w, acc, grad, columns, sem):
        _, _, t = place()
        own = pl.ds(pl.multiple_of(t * quarter, LANES), quarter)
        columns[...] = contract(cot[...], w[...], 1, 1).astype(bf16)
        copy = pltpu.make_async_copy(columns, grad.at[:, own], sem)
        copy.start()
        acc[...] = contract(act[:, own], w[...], 1, 0)
        copy.wait()

    weight_then, _ = barrier((value_weight, held[0]))
    acc, grad = pl.pallas_call(
        quarter_body,
        out_shape=[shape((tok, vdim), f32), shape((tok, depth), bf16)],
        in_specs=[whole] * 3,
        out_specs=[whole, anywhere],
        scratch_shapes=[pltpu.VMEM((tok, quarter), bf16), pltpu.SemaphoreType.DMA],
        compiler_params=pltpu.CompilerParams(vmem_limit_bytes=VMEM_LIMIT),
        cost_estimate=estimate(OPT["c_qtr"]),
        name="own_quarter",
    )(activations, value_cotangent, weight_then)

    def sums_of(js_now, offset, cost):
        def body(act, cot, *refs):
            keep, send = refs[-2:]
            p, c, t = place()
            cots = jnp.concatenate([cot[...]] + [r[:, width:] for r in refs[:-2]], axis=0)
            for i, j in enumerate(js_now):
                for out, core in ((send, 1 - c), (keep, c)):
                    start = pl.multiple_of((offset + i) * 2 * blk + core * blk, LANES)
                    parts = [act[:, pl.ds(column(t ^ j, p, core), blk)]] + [r[:, pl.ds(start, blk)] for r in refs[:-2]]
                    out[i * blk : (i + 1) * blk, :] = contract(jnp.concatenate(parts, axis=0), cots, 0, 0)

        out = shape((len(js_now) * blk, vdim), f32)
        return kernel_call(body, [out, out], [activations, value_cotangent, *got], "sums", cost)

    def join(groups, pack, cost, after=()):
        arrays = []
        for group in groups:
            arrays += [a for a, _, _ in group if not any(a is b for b in arrays)]
        found = [[([a is b for b in arrays].index(True), at, power_at) for a, at, power_at in g] for g in groups]
        rows = len(groups) * blk

        def body(*refs):
            out = refs[-1]

            def value(k, at, power_at):
                x = refs[k][at : at + blk, :]
                return x if power_at is None else x * jnp.exp2(refs[k][power_at : power_at + 1, :])

            totals = []
            for g in found:
                total = value(*g[0])
                for term in g[1:]:
                    total = total + value(*term)
                totals.append(total)
            total = jnp.concatenate(totals, axis=0)
            if not pack:
                out[...] = total
                return
            top = jnp.max(jnp.abs(total), axis=(0, 1), keepdims=True)
            power = jnp.clip(jnp.ceil(jnp.log(jnp.maximum(top, 1e-30)) * LOG2_E) - TOP_POWER, -110.0, 110.0)
            out[:rows, :] = total * jnp.exp2(-power)
            out[rows:, :] = jnp.broadcast_to(power, (PAD, vdim))

        (out,) = kernel_call(body, [shape((rows + PAD if pack else rows, vdim), f32)], [*arrays, *after], "join", cost)
        return out.astype(jnp.float16) if pack else out

    got[0], acc, *_ = barrier((got[0], acc, *held))
    keep_1, send_1 = sums_of(js[:half], 0, OPT["c_sums1"])
    keep_2, send_2 = sums_of(js[half:], half, OPT["c_sums2"])
    mine = stack(held, OPT["c_mine"])
    twin_1, twin_2 = twin(send_1), twin(send_2)
    terms = {j: [(keep_1, i * blk, None), (twin_1, i * blk, None)] for i, j in enumerate(js[:half])}
    terms.update({j: [(keep_2, i * blk, None), (twin_2, i * blk, None)] for i, j in enumerate(js[half:])})

    rows = (n_tensor - 1) * blk
    singles = [1 << b for b in range(chips.bit_length() - 1)]
    late = [q for q in range(chips) if q.bit_count() >= 2]
    pieces = {0: [mine], **{q: [across(mine, q)] for q in singles}}

    def product(acc, grad, qs, ours, total=None, twins=None):
        last = total is not None
        n = (n_tensor - 1) * len(qs)

        def body(act, cot, acc, _, mine, twins, *refs):
            both = mine, twins
            p, c, t = place()
            if last:
                total, proj, grad, weight_grad, proj_out, grad_out, columns, sems = refs
                grad_out[...] = total[...] * (1.0 / root)
                copies = [pltpu.make_async_copy(grad_out, weight_grad, sems.at[n + 1])]
                copies[0].start()
            else:
                out, grad, columns, sems = refs
                copies = []
            order = [(at_q * (n_tensor - 1) + i, q, j, core) for at_q, q in enumerate(qs) for i, j in enumerate(slots) for core in range(2)]
            weights = [both[k][at * blk : (at + 1) * blk, :] for at, _, _, k in order]
            columns_of = [pl.ds(column(t ^ j, p ^ q, (c, 1 - c)[k]), blk) for _, q, j, k in order]
            lhs = jnp.concatenate([act[:, cols] for cols in columns_of], axis=1)
            result = acc[...] + contract(lhs, jnp.concatenate(weights, axis=0), 1, 0)
            if last:
                proj_out[...] = result.astype(bf16)
                copies.append(pltpu.make_async_copy(proj_out, proj, sems.at[n]))
                copies[-1].start()
            else:
                out[...] = result
            for (at, q, j, k), w in zip(order, weights):
                cols = pl.ds(pl.multiple_of((c, 1 - c)[k] * blk, LANES), blk)
                columns[at, :, cols] = contract(cot[...], w, 1, 1).astype(bf16)
                if k:
                    copies.append(pltpu.make_async_copy(columns.at[at], grad.at[:, pl.ds(column(t ^ j, p ^ q), 2 * blk)], sems.at[at]))
                    copies[-1].start()
            for copy in copies:
                copy.wait()

        args = [activations, value_cotangent, acc, grad, ours, twin(ours) if twins is None else twins] + [total] * last
        outs = [shape((tok, vdim), bf16 if last else f32), shape((tok, depth), bf16)] + [shape((blk, vdim), f32)] * last
        scratch = [pltpu.VMEM((tok, vdim), bf16), pltpu.VMEM((blk, vdim), f32)] * last
        return pl.pallas_call(
            body,
            out_shape=outs,
            in_specs=[whole] * 3 + [anywhere] + [whole] * (2 + last),
            out_specs=[anywhere] * 3 if last else [whole, anywhere],
            scratch_shapes=scratch + [pltpu.VMEM((n, tok, 2 * blk), bf16), pltpu.SemaphoreType.DMA((n + 2,))],
            input_output_aliases={3: 1},
            compiler_params=pltpu.CompilerParams(vmem_limit_bytes=VMEM_LIMIT),
            cost_estimate=estimate(OPT["c_last"] if last else OPT["c_prod"]),
            name="product",
        )(*args)

    def tie(j, x):
        (a, at, power_at), *others = terms[j]
        a, x = barrier((a, x))
        terms[j] = [(a, at, power_at), *others]
        return x

    early, ours_early, done = [0, *singles], None, False
    for i, j in enumerate(js[:-1]):
        last_hop = i == (n_tensor - 2 if OPT["s1e"] else half)
        if last_hop:
            if OPT["s1e"] and i > half:
                arrived = tie(j, arrived)
                (x, at, power_at) = terms[0][-1]
                terms[0][-1] = (arrived, at, power_at)
            ours_early = stack([x for q in early for x in pieces[q]], OPT["c_estack"])
            if OPT["ws2"]:
                ours_early = tie(j, ours_early)
        if i == half and OPT["s1p"] == 2:
            twin_early = twin(ours_early)
        if not OPT["s1e"] and i > half and OPT["s1p"] == 2:
            twin_early = tie(j, twin_early)
        if not OPT["s1e"] and i > half and not done and late and OPT["s1p"] < 2:
            acc, grad = product(acc, grad, early, ours_early)
            done = True
        if i > half and done and OPT["s1p"] == 1:
            acc = tie(j, acc)
        packed = join([terms[j]], True, OPT["c_join1"] if i < half else OPT["c_join2"] if last_hop else OPT["c_join3"])
        if i == half - 1 and OPT["s1t"] and len(js) > half + 2:
            packed = tie(js[half], packed)
        if i == (half if OPT["s1e"] and len(js) > half + 2 else 0) and OPT["st2_after"] == 2:
            _, *then = barrier((packed, *[pieces[q][0] for q in singles]))
            pieces.update({q: [x] for q, x in zip(singles, then)})
        arrived = along(packed, j & -j).astype(f32)
        terms[j & (j - 1)].append((arrived, 0, blk))
    if ours_early is None:
        ours_early = stack([x for q in early for x in pieces[q]], OPT["c_estack"])
    if late and not done:
        acc, grad = product(acc, grad, early, ours_early, None, twin_early if OPT["s1p"] == 2 else None)

    if late and OPT["pt"]:
        acc = tie(0, acc)
    after = [twin(acc[:8, :LANES])] if OPT["tok"] and late else []
    if not OPT["jl"] or not late:
        total = join([terms[0]], False, OPT["c_joinf"], after)
    if not late:
        return product(acc, grad, early, ours_early, total)
    for q in sorted(late, key=lambda q: q.bit_count()):
        bits = [b for b in singles if q & b]
        cuts = [rows * i // len(bits) // 16 * 16 for i in range(len(bits))] + [rows]
        ways = []
        for i, b in enumerate(bits):
            there = stack(pieces[q ^ b]) if len(pieces[q ^ b]) > 1 else pieces[q ^ b][0]
            ways.append(across(there[cuts[i] : cuts[i + 1]], b))
        pieces[q] = ways
    ours_late = stack([x for q in late for x in pieces[q]], OPT["c_e2stack"])
    if OPT["jl"]:
        ours_late = tie(0, ours_late)
        total = join([terms[0]], False, OPT["c_joinf"])
    if OPT["e2p"]:
        ours_late, acc = barrier((ours_late, acc))
    return product(acc, grad, late, ours_late, total)


def solution(mesh):
    n_dp, n_tensor = mesh.shape["dp"], mesh.shape["tensor"]

    def per_device(activations, value_weight, value_cotangent):
        tok, depth = activations.shape
        powers = all(n > 1 and n & (n - 1) == 0 for n in (n_dp, n_tensor))
        if powers and depth % (n_dp * n_tensor * LANES) == 0 and tok % LANES == 0:
            return paired_form(n_dp, n_tensor, activations, value_weight, value_cotangent)
        return gathered_form(activations, value_weight, value_cotangent)

    return jax.shard_map(
        per_device,
        mesh=mesh,
        in_specs=(P(AXES, None), P("tensor", None), P(AXES, None)),
        out_specs=(P(AXES, None), P(AXES, None), P(("tensor", "dp"), None)),
        check_vma=False,
    )
```

time: 51.7 us -> 47.8 us (0.925)
  waiting for transfers between devices: 20.6 us -> 14.8 us
  starting transfers between devices: 20.7 us -> 22.4 us
  local copies, waits for them, and re-layouts: 2.56 us -> 3.39 us
  other arithmetic: 0.86 us -> 0.13 us
    ppermute x17 -> x18, waiting for transfers between devices: 20.6 us -> 14.8 us  [exchange(): return lax.ppermute(x, AXES, pairs)]
    ppermute x17 -> x18, starting transfers between devices: 20.7 us -> 22.4 us  [exchange(): return lax.ppermute(x, AXES, pairs)]
    unnamed x6 -> x10, local copies, waits for them, and re-layouts: 2.43 us -> 3.35 us
    div x1 -> x0, other arithmetic: 0.72 us -> none  [paired_form(): weight_grad = total / jnp.sqrt(f32(tok * n_dp * n_tensor))]
  transfers between devices with their start and end apart: 17 -> 18, of which waited for: 9 -> 8; matrix products, arithmetic and copies ran while one was open for 2% -> 0% of each run, Pallas kernels for 4% -> 10%
where the time goes in v4:
time: 47.8 us; the launch traced here: 47.6 us
  starting transfers between devices  22.4 us (47%)
  waiting for transfers between devices  14.8 us (31%)
  Pallas kernels  6.03 us (13%)
  local copies, waits for them, and re-layouts  3.39 us (7%)
  between operations  0.89 us (2%)
    ppermute x18, starting transfers between devices, exchange(): return lax.ppermute(x, AXES, pairs)  22.4 us
    ppermute x18, waiting for transfers between devices, exchange(): return lax.ppermute(x, AXES, pairs)  14.8 us
    unnamed x10, local copies, waits for them, and re-layouts  3.35 us
    pallas_call x2, Pallas kernels, product(): pl.pallas_call(body, out_shape=outs, in_specs=[whole] * 3 + [anywhere] +...  3.01 us
    pallas_call x11, Pallas kernels, kernel_call(): pl.pallas_call(body, out_shape=out_shapes, in_specs=[whole] * len(args),...  1.82 us
    pallas_call x1, Pallas kernels, paired_form(): pl.pallas_call(quarter_body, out_shape=[shape((tok, vdim), f32), shape((t...  1.2 us
  transfers between devices with their start and end apart: 18, of which 8 were waited for; matrix products, arithmetic and copies ran while one was open for 0% of the time, Pallas kernels for 10%

profile of v4, /device:TPU:0, one launch (start us, length us, event | category | flops | bytes accessed | tf_op | source)
XLA Modules:
  0.0 47.6 jit_solution(17308099210892367816)
XLA Ops:
  0.6 1.2 %copy-done = bf16[128,4096]{1,0:T(8,128)(2,1)S(1)} copy-done((bf16[128,4096]{1,0:T(8,128)(2,1)S(1)}, bf16[128,4096]{1,0:T(8,128)(2,1)}, u32[]{:S(2)}) %copy-start) | copy-done | bytes 1048600
  1.9 0.9 %copy-done.3 = bf16[128,512]{1,0:T(8,128)(2,1)S(1)} copy-done((bf16[128,512]{1,0:T(8,128)(2,1)S(1)}, bf16[128,512]{1,0:T(8,128)(2,1)}, u32[]{:S(2)}) %copy-start.3) | copy-done | bytes 131096
  2.9 3.0 %collective-permute-start = (bf16[128,1536]{1,0:T(8,128)(2,1)S(1)}, bf16[128,1536]{1,0:T(8,128)(2,1)S(1)}, u32[]{:S(2)}, u32[]{:S(2)}) collective-permute-start(bf16[128,1536]{1,0:T(8,128)(2,1)S(1)} %get-tuple-element.30), channel_id=1, source_target_pairs={{0,8},{1,9},{2,10},{3,11},{4,12},{5,13},{6,14},{7,15},{8,0},{9,1},... | collective-permute-start | bytes 1179656 | tf_op jit(solution)/shard_map/ppermute | solution.py:38
  5.9 1.5 %collective-permute-start.4 = (bf16[128,1536]{1,0:T(8,128)(2,1)S(1)}, bf16[128,1536]{1,0:T(8,128)(2,1)S(1)}, u32[]{:S(2)}, u32[]{:S(2)}) collective-permute-start(bf16[128,1536]{1,0:T(8,128)(2,1)S(1)} %get-tuple-element.37), channel_id=1, source_target_pairs={{0,16},{1,17},{2,18},{3,19},{4,20},{5,21},{6,22},{7,23},{8,24},{9,... | collective-permute-start | bytes 1179656 | tf_op jit(solution)/shard_map/ppermute | solution.py:38
  7.4 1.2 %copy-done.2 = bf16[1024,512]{1,0:T(8,128)(2,1)S(1)} copy-done((bf16[1024,512]{1,0:T(8,128)(2,1)S(1)}, bf16[1024,512]{1,0:T(8,128)(2,1)}, u32[]{:S(2)}) %copy-start.2) | copy-done | bytes 1048600
  8.7 3.1 %collective-permute-start.1 = (bf16[128,512]{1,0:T(8,128)(2,1)S(1)}, bf16[128,512]{1,0:T(8,128)(2,1)S(1)}, u32[]{:S(2)}, u32[]{:S(2)}) collective-permute-start(bf16[128,512]{1,0:T(8,128)(2,1)S(1)} %own_slice.1), channel_id=1, source_target_pairs={{0,2},{1,3},{2,0},{3,1},{4,6},{5,7},{6,4},{7,5},{8,10},{9,11},{10,... | collective-permute-start | bytes 393224 | tf_op jit(solution)/shard_map/ppermute | solution.py:38
  11.8 1.6 %collective-permute-start.2 = (bf16[128,512]{1,0:T(8,128)(2,1)S(1)}, bf16[128,512]{1,0:T(8,128)(2,1)S(1)}, u32[]{:S(2)}, u32[]{:S(2)}) collective-permute-start(bf16[128,512]{1,0:T(8,128)(2,1)S(1)} %own_slice.1), channel_id=1, source_target_pairs={{0,1},{1,0},{2,3},{3,2},{4,5},{5,4},{6,7},{7,6},{8,9},{9,8},{10,11... | collective-permute-start | bytes 393224 | tf_op jit(solution)/shard_map/ppermute | solution.py:38
  13.4 4.0 %collective-permute-done.1.refs_0_ = bf16[128,512]{1,0:T(8,128)(2,1)S(1)} collective-permute-done((bf16[128,512]{1,0:T(8,128)(2,1)S(1)}, bf16[128,512]{1,0:T(8,128)(2,1)S(1)}, u32[]{:S(2)}, u32[]{:S(2)}) %collective-permute-start.1) | collective-permute-done | bytes 131104 | tf_op jit(solution)/shard_map/ppermute | solution.py:38
  17.4 0.6 %collective-permute-start.3 = (bf16[128,512]{1,0:T(8,128)(2,1)S(1)}, bf16[128,512]{1,0:T(8,128)(2,1)S(1)}, u32[]{:S(2)}, u32[]{:S(2)}) collective-permute-start(bf16[128,512]{1,0:T(8,128)(2,1)S(1)} %collective-permute-done.1.refs_0_), channel_id=1, source_target_pairs={{0,1},{1,0},{2,3},{3,2},{4,5},{5,4},{6,7},{7,6},{8,9},{9,8},{10,11... | collective-permute-start | bytes 393224 | tf_op jit(solution)/shard_map/ppermute | solution.py:38
  18.0 1.2 %own_quarter.1 = (f32[128,512]{1,0:T(8,128)S(1)}, bf16[128,4096]{1,0:T(8,128)(2,1)}) custom-call(bf16[128,4096]{1,0:T(8,128)(2,1)S(1)} %copy-done.1, bf16[128,512]{1,0:T(8,128)(2,1)S(1)} %copy-done.4, bf16[1024,512]{1,0:T(8,128)(2,1)S(1)} %copy-done.2), custom_call_target="tpu_custom_call" | custom-call | bytes 1024 | tf_op jit(solution)/shard_map/own_quarter/pallas_call | solution.py:139
  19.2 3.1 %collective-permute-done.3.refs_2_ = bf16[128,512]{1,0:T(8,128)(2,1)S(1)} collective-permute-done((bf16[128,512]{1,0:T(8,128)(2,1)S(1)}, bf16[128,512]{1,0:T(8,128)(2,1)S(1)}, u32[]{:S(2)}, u32[]{:S(2)}) %collective-permute-start.3) | collective-permute-done | bytes 131104 | tf_op jit(solution)/shard_map/ppermute | solution.py:38
  22.4 1.6 %collective-permute-start.7 = (bf16[384,512]{1,0:T(8,128)(2,1)S(1)}, bf16[384,512]{1,0:T(8,128)(2,1)S(1)}, u32[]{:S(2)}, u32[]{:S(2)}) collective-permute-start(bf16[384,512]{1,0:T(8,128)(2,1)S(1)} %stack.3.refs_0_), channel_id=1, source_target_pairs={{0,8},{1,9},{2,10},{3,11},{4,12},{5,13},{6,14},{7,15},{8,0},{9,1},... | collective-permute-start | bytes 1179656 | tf_op jit(solution)/shard_map/ppermute | solution.py:38
  24.0 1.5 %collective-permute-start.8 = (bf16[384,512]{1,0:T(8,128)(2,1)S(1)}, bf16[384,512]{1,0:T(8,128)(2,1)S(1)}, u32[]{:S(2)}, u32[]{:S(2)}) collective-permute-start(bf16[384,512]{1,0:T(8,128)(2,1)S(1)} %stack.3.refs_0_), channel_id=1, source_target_pairs={{0,16},{1,17},{2,18},{3,19},{4,20},{5,21},{6,22},{7,23},{8,24},{9,... | collective-permute-start | bytes 1179656 | tf_op jit(solution)/shard_map/ppermute | solution.py:38
  26.3 0.6 %sums.2 = (f32[384,512]{1,0:T(8,128)S(1)}, f32[384,512]{1,0:T(8,128)S(1)}) custom-call(bf16[128,4096]{1,0:T(8,128)(2,1)S(1)} %copy-done.1, bf16[128,512]{1,0:T(8,128)(2,1)S(1)} %copy-done.4, bf16[128,1536]{1,0:T(8,128)(2,1)S(1)} %collective-permute-done.refs_0_, bf16[128,1536]{1,0:T(8,128)(2,1)S(1)} %collective-permute-done.4.refs_1_, ...), custom_call_target="tpu_custom_call" | custom-call | flops 23000000512 | bytes 1024 | tf_op jit(solution)/shard_map/sums/pallas_call | solution.py:47
  28.0 1.6 %collective-permute-start.14 = (f16[144,512]{1,0:T(8,128)(2,1)S(1)}, f16[144,512]{1,0:T(8,128)(2,1)S(1)}, u32[]{:S(2)}, u32[]{:S(2)}) collective-permute-start(f16[144,512]{1,0:T(8,128)(2,1)S(1)} %convert_element_type.18), channel_id=1, source_target_pairs={{0,1},{1,0},{2,3},{3,2},{4,5},{5,4},{6,7},{7,6},{8,9},{9,8},{10,11... | collective-permute-start | bytes 442376 | tf_op jit(solution)/shard_map/ppermute | solution.py:38
  29.6 2.3 %collective-permute-done.7.refs_1_ = bf16[384,512]{1,0:T(8,128)(2,1)S(1)} collective-permute-done((bf16[384,512]{1,0:T(8,128)(2,1)S(1)}, bf16[384,512]{1,0:T(8,128)(2,1)S(1)}, u32[]{:S(2)}, u32[]{:S(2)}) %collective-permute-start.7) | collective-permute-done | bytes 393248 | tf_op jit(solution)/shard_map/ppermute | solution.py:38
  31.9 1.4 %collective-permute-done.8.refs_2_ = bf16[384,512]{1,0:T(8,128)(2,1)S(1)} collective-permute-done((bf16[384,512]{1,0:T(8,128)(2,1)S(1)}, bf16[384,512]{1,0:T(8,128)(2,1)S(1)}, u32[]{:S(2)}, u32[]{:S(2)}) %collective-permute-start.8) | collective-permute-done | bytes 393248 | tf_op jit(solution)/shard_map/ppermute | solution.py:38
  33.5 1.3 %collective-permute-start.10 = (bf16[192,512]{1,0:T(8,128)(2,1)S(1)}, bf16[192,512]{1,0:T(8,128)(2,1)S(1)}, u32[]{:S(2)}, u32[]{:S(2)}) collective-permute-start(bf16[192,512]{1,0:T(8,128)(2,1)S(1)} %slice.9), channel_id=1, source_target_pairs={{0,8},{1,9},{2,10},{3,11},{4,12},{5,13},{6,14},{7,15},{8,0},{9,1},... | collective-permute-start | bytes 589832 | tf_op jit(solution)/shard_map/ppermute | solution.py:38
  34.8 0.8 %collective-permute-start.11 = (bf16[192,512]{1,0:T(8,128)(2,1)S(1)}, bf16[192,512]{1,0:T(8,128)(2,1)S(1)}, u32[]{:S(2)}, u32[]{:S(2)}) collective-permute-start(bf16[192,512]{1,0:T(8,128)(2,1)S(1)} %slice.10), channel_id=1, source_target_pairs={{0,16},{1,17},{2,18},{3,19},{4,20},{5,21},{6,22},{7,23},{8,24},{9,... | collective-permute-start | bytes 589832 | tf_op jit(solution)/shard_map/ppermute | solution.py:38
  35.9 2.7 %collective-permute-start.15 = (f16[144,512]{1,0:T(8,128)(2,1)S(1)}, f16[144,512]{1,0:T(8,128)(2,1)S(1)}, u32[]{:S(2)}, u32[]{:S(2)}) collective-permute-start(f16[144,512]{1,0:T(8,128)(2,1)S(1)} %convert_element_type.20), channel_id=1, source_target_pairs={{0,2},{1,3},{2,0},{3,1},{4,6},{5,7},{6,4},{7,5},{8,10},{9,11},{10,... | collective-permute-start | bytes 442376 | tf_op jit(solution)/shard_map/ppermute | solution.py:38
  38.8 1.6 %collective-permute-start.16 = (f16[144,512]{1,0:T(8,128)(2,1)S(1)}, f16[144,512]{1,0:T(8,128)(2,1)S(1)}, u32[]{:S(2)}, u32[]{:S(2)}) collective-permute-start(f16[144,512]{1,0:T(8,128)(2,1)S(1)} %convert_element_type.22), channel_id=1, source_target_pairs={{0,1},{1,0},{2,3},{3,2},{4,5},{5,4},{6,7},{7,6},{8,9},{9,8},{10,11... | collective-permute-start | bytes 442376 | tf_op jit(solution)/shard_map/ppermute | solution.py:38
  40.4 1.8 %product.2 = (f32[128,512]{1,0:T(8,128)S(1)}, bf16[128,4096]{1,0:T(8,128)(2,1)}) custom-call(bf16[128,4096]{1,0:T(8,128)(2,1)S(1)} %copy-done.1, bf16[128,512]{1,0:T(8,128)(2,1)S(1)} %copy-done.4, f32[128,512]{1,0:T(8,128)S(1)} %get-tuple-element.34.acc, bf16[128,4096]{1,0:T(8,128)(2,1)} %get-tuple-element.35._, ...), custom_call_target="tpu_custom_call", output_to_operand_aliasing={{1}: (3, {})} | custom-call | bytes 1024 | tf_op jit(solution)/shard_map/product/pallas_call | solution.py:247
  43.0 2.8 %collective-permute-done.15 = f16[144,512]{1,0:T(8,128)(2,1)S(1)} collective-permute-done((f16[144,512]{1,0:T(8,128)(2,1)S(1)}, f16[144,512]{1,0:T(8,128)(2,1)S(1)}, u32[]{:S(2)}, u32[]{:S(2)}) %collective-permute-start.15) | collective-permute-done | bytes 147488 | tf_op jit(solution)/shard_map/ppermute | solution.py:38
  46.4 1.2 %product.3 = (bf16[128,512]{1,0:T(8,128)(2,1)}, bf16[128,4096]{1,0:T(8,128)(2,1)}, f32[128,512]{1,0:T(8,128)}) custom-call(bf16[128,4096]{1,0:T(8,128)(2,1)S(1)} %copy-done.1, bf16[128,512]{1,0:T(8,128)(2,1)S(1)} %copy-done.4, f32[128,512]{1,0:T(8,128)S(1)} %get-tuple-element.46.acc, ...), custom_call_target="tpu_custom_call", output_to_operand_aliasing={{1}: (3, {})} | custom-call | bytes 1024 | tf_op jit(solution)/shard_map/product/pallas_call | solution.py:247
  (45 shorter events, 3.9 us)
Async XLA Ops:
  0.6 1.2 %copy-start = (bf16[128,4096]{1,0:T(8,128)(2,1)S(1)}, bf16[128,4096]{1,0:T(8,128)(2,1)}, u32[]{:S(2)}) copy-start(bf16[128,4096]{1,0:T(8,128)(2,1)} %act.11) | copy-start | bytes 3145732
  1.9 0.9 %copy-start.3 = (bf16[128,512]{1,0:T(8,128)(2,1)S(1)}, bf16[128,512]{1,0:T(8,128)(2,1)}, u32[]{:S(2)}) copy-start(bf16[128,512]{1,0:T(8,128)(2,1)} %cot.11) | copy-start | bytes 393220
  2.8 15.2 %copy-start.1 = (bf16[128,4096]{1,0:T(8,128)(2,1)S(1)}, bf16[128,4096]{1,0:T(8,128)(2,1)}, u32[]{:S(2)}) copy-start(bf16[128,4096]{1,0:T(8,128)(2,1)} %act.11) | copy-start | bytes 3145732
  2.8 15.2 %copy-start.4 = (bf16[128,512]{1,0:T(8,128)(2,1)S(1)}, bf16[128,512]{1,0:T(8,128)(2,1)}, u32[]{:S(2)}) copy-start(bf16[128,512]{1,0:T(8,128)(2,1)} %cot.11) | copy-start | bytes 393220
  2.9 22.6 %collective-permute-start = (bf16[128,1536]{1,0:T(8,128)(2,1)S(1)}, bf16[128,1536]{1,0:T(8,128)(2,1)S(1)}, u32[]{:S(2)}, u32[]{:S(2)}) collective-permute-start(bf16[128,1536]{1,0:T(8,128)(2,1)S(1)} %get-tuple-element.30), channel_id=1, source_target_pairs={{0,8},{1,9},{2,10},{3,11},{4,12},{5,13},{6,14},{7,15},{8,0},{9,1},... | collective-permute-start | bytes 1179656 | tf_op jit(solution)/shard_map/ppermute | solution.py:38
  5.9 19.6 %collective-permute-start.4 = (bf16[128,1536]{1,0:T(8,128)(2,1)S(1)}, bf16[128,1536]{1,0:T(8,128)(2,1)S(1)}, u32[]{:S(2)}, u32[]{:S(2)}) collective-permute-start(bf16[128,1536]{1,0:T(8,128)(2,1)S(1)} %get-tuple-element.37), channel_id=1, source_target_pairs={{0,16},{1,17},{2,18},{3,19},{4,20},{5,21},{6,22},{7,23},{8,24},{9,... | collective-permute-start | bytes 1179656 | tf_op jit(solution)/shard_map/ppermute | solution.py:38
  7.4 18.4 %collective-permute-start.5 = (bf16[128,1536]{1,0:T(8,128)(2,1)S(1)}, bf16[128,1536]{1,0:T(8,128)(2,1)S(1)}, u32[]{:S(2)}, u32[]{:S(2)}) collective-permute-start(bf16[128,1536]{1,0:T(8,128)(2,1)S(1)} %get-tuple-element.38), channel_id=1, source_target_pairs={{0,24},{1,25},{2,26},{3,27},{4,28},{5,29},{6,30},{7,31},{8,16},{9,... | collective-permute-start | bytes 1179656 | tf_op jit(solution)/shard_map/ppermute | solution.py:38
  7.4 1.2 %copy-start.2 = (bf16[1024,512]{1,0:T(8,128)(2,1)S(1)}, bf16[1024,512]{1,0:T(8,128)(2,1)}, u32[]{:S(2)}) copy-start(bf16[1024,512]{1,0:T(8,128)(2,1)} %w) | copy-start | bytes 3145732
  8.7 8.7 %collective-permute-start.1 = (bf16[128,512]{1,0:T(8,128)(2,1)S(1)}, bf16[128,512]{1,0:T(8,128)(2,1)S(1)}, u32[]{:S(2)}, u32[]{:S(2)}) collective-permute-start(bf16[128,512]{1,0:T(8,128)(2,1)S(1)} %own_slice.1), channel_id=1, source_target_pairs={{0,2},{1,3},{2,0},{3,1},{4,6},{5,7},{6,4},{7,5},{8,10},{9,11},{10,... | collective-permute-start | bytes 393224 | tf_op jit(solution)/shard_map/ppermute | solution.py:38
  11.8 7.4 %collective-permute-start.2 = (bf16[128,512]{1,0:T(8,128)(2,1)S(1)}, bf16[128,512]{1,0:T(8,128)(2,1)S(1)}, u32[]{:S(2)}, u32[]{:S(2)}) collective-permute-start(bf16[128,512]{1,0:T(8,128)(2,1)S(1)} %own_slice.1), channel_id=1, source_target_pairs={{0,1},{1,0},{2,3},{3,2},{4,5},{5,4},{6,7},{7,6},{8,9},{9,8},{10,11... | collective-permute-start | bytes 393224 | tf_op jit(solution)/shard_map/ppermute | solution.py:38
  17.4 5.0 %collective-permute-start.3 = (bf16[128,512]{1,0:T(8,128)(2,1)S(1)}, bf16[128,512]{1,0:T(8,128)(2,1)S(1)}, u32[]{:S(2)}, u32[]{:S(2)}) collective-permute-start(bf16[128,512]{1,0:T(8,128)(2,1)S(1)} %collective-permute-done.1.refs_0_), channel_id=1, source_target_pairs={{0,1},{1,0},{2,3},{3,2},{4,5},{5,4},{6,7},{7,6},{8,9},{9,8},{10,11... | collective-permute-start | bytes 393224 | tf_op jit(solution)/shard_map/ppermute | solution.py:38
  22.4 9.6 %collective-permute-start.7 = (bf16[384,512]{1,0:T(8,128)(2,1)S(1)}, bf16[384,512]{1,0:T(8,128)(2,1)S(1)}, u32[]{:S(2)}, u32[]{:S(2)}) collective-permute-start(bf16[384,512]{1,0:T(8,128)(2,1)S(1)} %stack.3.refs_0_), channel_id=1, source_target_pairs={{0,8},{1,9},{2,10},{3,11},{4,12},{5,13},{6,14},{7,15},{8,0},{9,1},... | collective-permute-start | bytes 1179656 | tf_op jit(solution)/shard_map/ppermute | solution.py:38
  24.0 9.4 %collective-permute-start.8 = (bf16[384,512]{1,0:T(8,128)(2,1)S(1)}, bf16[384,512]{1,0:T(8,128)(2,1)S(1)}, u32[]{:S(2)}, u32[]{:S(2)}) collective-permute-start(bf16[384,512]{1,0:T(8,128)(2,1)S(1)} %stack.3.refs_0_), channel_id=1, source_target_pairs={{0,16},{1,17},{2,18},{3,19},{4,20},{5,21},{6,22},{7,23},{8,24},{9,... | collective-permute-start | bytes 1179656 | tf_op jit(solution)/shard_map/ppermute | solution.py:38
  26.2 1.6 %collective-permute-start.6 = (f32[128,512]{1,0:T(8,128)S(1)}, f32[128,512]{1,0:T(8,128)S(1)}, u32[]{:S(2)}, u32[]{:S(2)}) collective-permute-start(f32[128,512]{1,0:T(8,128)S(1)} %get-tuple-element.41), channel_id=1, source_target_pairs={{0,4},{1,5},{2,6},{3,7},{4,0},{5,1},{6,2},{7,3},{8,12},{9,13},{10,... | collective-permute-start | bytes 786440 | tf_op jit(solution)/shard_map/ppermute | solution.py:38
  26.9 8.8 %collective-permute-start.13 = (f32[384,512]{1,0:T(8,128)S(1)}, f32[384,512]{1,0:T(8,128)S(1)}, u32[]{:S(2)}, u32[]{:S(2)}) collective-permute-start(f32[384,512]{1,0:T(8,128)S(1)} %get-tuple-element.48), channel_id=1, source_target_pairs={{0,4},{1,5},{2,6},{3,7},{4,0},{5,1},{6,2},{7,3},{8,12},{9,13},{10,... | collective-permute-start | bytes 2359304 | tf_op jit(solution)/shard_map/ppermute | solution.py:38
  28.0 7.6 %collective-permute-start.14 = (f16[144,512]{1,0:T(8,128)(2,1)S(1)}, f16[144,512]{1,0:T(8,128)(2,1)S(1)}, u32[]{:S(2)}, u32[]{:S(2)}) collective-permute-start(f16[144,512]{1,0:T(8,128)(2,1)S(1)} %convert_element_type.18), channel_id=1, source_target_pairs={{0,1},{1,0},{2,3},{3,2},{4,5},{5,4},{6,7},{7,6},{8,9},{9,8},{10,11... | collective-permute-start | bytes 442376 | tf_op jit(solution)/shard_map/ppermute | solution.py:38
  33.5 5.1 %collective-permute-start.9 = (bf16[1152,512]{1,0:T(8,128)(2,1)S(1)}, bf16[1152,512]{1,0:T(8,128)(2,1)S(1)}, u32[]{:S(2)}, u32[]{:S(2)}) collective-permute-start(bf16[1152,512]{1,0:T(8,128)(2,1)S(1)} %stack.4.mine), channel_id=1, source_target_pairs={{0,4},{1,5},{2,6},{3,7},{4,0},{5,1},{6,2},{7,3},{8,12},{9,13},{10,... | collective-permute-start | bytes 3538952 | tf_op jit(solution)/shard_map/ppermute | solution.py:38
  33.5 8.8 %collective-permute-start.10 = (bf16[192,512]{1,0:T(8,128)(2,1)S(1)}, bf16[192,512]{1,0:T(8,128)(2,1)S(1)}, u32[]{:S(2)}, u32[]{:S(2)}) collective-permute-start(bf16[192,512]{1,0:T(8,128)(2,1)S(1)} %slice.9), channel_id=1, source_target_pairs={{0,8},{1,9},{2,10},{3,11},{4,12},{5,13},{6,14},{7,15},{8,0},{9,1},... | collective-permute-start | bytes 589832 | tf_op jit(solution)/shard_map/ppermute | solution.py:38
  34.8 7.5 %collective-permute-start.11 = (bf16[192,512]{1,0:T(8,128)(2,1)S(1)}, bf16[192,512]{1,0:T(8,128)(2,1)S(1)}, u32[]{:S(2)}, u32[]{:S(2)}) collective-permute-start(bf16[192,512]{1,0:T(8,128)(2,1)S(1)} %slice.10), channel_id=1, source_target_pairs={{0,16},{1,17},{2,18},{3,19},{4,20},{5,21},{6,22},{7,23},{8,24},{9,... | collective-permute-start | bytes 589832 | tf_op jit(solution)/shard_map/ppermute | solution.py:38
  35.9 9.9 %collective-permute-start.15 = (f16[144,512]{1,0:T(8,128)(2,1)S(1)}, f16[144,512]{1,0:T(8,128)(2,1)S(1)}, u32[]{:S(2)}, u32[]{:S(2)}) collective-permute-start(f16[144,512]{1,0:T(8,128)(2,1)S(1)} %convert_element_type.20), channel_id=1, source_target_pairs={{0,2},{1,3},{2,0},{3,1},{4,6},{5,7},{6,4},{7,5},{8,10},{9,11},{10,... | collective-permute-start | bytes 442376 | tf_op jit(solution)/shard_map/ppermute | solution.py:38
  38.8 7.5 %collective-permute-start.16 = (f16[144,512]{1,0:T(8,128)(2,1)S(1)}, f16[144,512]{1,0:T(8,128)(2,1)S(1)}, u32[]{:S(2)}, u32[]{:S(2)}) collective-permute-start(f16[144,512]{1,0:T(8,128)(2,1)S(1)} %convert_element_type.22), channel_id=1, source_target_pairs={{0,1},{1,0},{2,3},{3,2},{4,5},{5,4},{6,7},{7,6},{8,9},{9,8},{10,11... | collective-permute-start | bytes 442376 | tf_op jit(solution)/shard_map/ppermute | solution.py:38
  42.3 4.0 %collective-permute-start.17 = (f32[8,128]{1,0:T(8,128)S(1)}, f32[8,128]{1,0:T(8,128)S(1)}, u32[]{:S(2)}, u32[]{:S(2)}) collective-permute-start(f32[8,128]{1,0:T(8,128)S(1)} %slice.11), channel_id=1, source_target_pairs={{0,4},{1,5},{2,6},{3,7},{4,0},{5,1},{6,2},{7,3},{8,12},{9,13},{10,... | collective-permute-start | bytes 12296 | tf_op jit(solution)/shard_map/ppermute | solution.py:38
  42.4 3.9 %collective-permute-start.12 = (bf16[384,512]{1,0:T(8,128)(2,1)S(1)}, bf16[384,512]{1,0:T(8,128)(2,1)S(1)}, u32[]{:S(2)}, u32[]{:S(2)}) collective-permute-start(bf16[384,512]{1,0:T(8,128)(2,1)S(1)} %stack.5.mine), channel_id=1, source_target_pairs={{0,4},{1,5},{2,6},{3,7},{4,0},{5,1},{6,2},{7,3},{8,12},{9,13},{10,... | collective-permute-start | bytes 1179656 | tf_op jit(solution)/shard_map/ppermute | solution.py:38

commit v5 on v4

--- a/solution.py
+++ b/solution.py
@@ -7,14 +7,12 @@
 from jax.experimental.pallas import tpu as pltpu
 from jax.sharding import PartitionSpec as P
 
-OPT = {'s1t': 0, 's1e': 0, 'tok': 1, 'jl': 0, 'c_pack': 0, 'c_slice': 0, 'c_qtr': 0, 'c_sums1': 30, 'c_sums2': 20, 'c_join1': 0, 'c_join2': 30, 'c_join3': 0, 'c_joinf': 5, 'c_mine': 0, 'c_estack': 60, 'c_e2stack': 0, 'c_prod': 0, 'c_last': 0, 's1p': 2, 'ws2': 1, 'st2_after': 2, 'e2p': 0, 'pt': 0}
 LANES = 128
 PAD = 16
 LOG2_E = 1.4426950408889634
 TOP_POWER = 14.0
 AXES = ("dp", "tensor")
 VMEM_LIMIT = 32 * 1024 * 1024
-PACK_LIMIT = 60 * 1024 * 1024
 
 
 def contract(a, b, dim_a, dim_b):
@@ -97,10 +95,7 @@
         d = lax.axis_index("dp")
         return d // 2, d % 2, lax.axis_index("tensor")
 
-    if OPT["s1e"]:
-        js = sorted(range(1, n_tensor), key=lambda j: (-j.bit_count(), -j if j.bit_count() > 1 else j)) + [0]
-    else:
-        js = sorted(range(n_tensor), key=lambda j: (-j.bit_count(), -j))
+    js = sorted(range(n_tensor), key=lambda j: (-j.bit_count(), -j))
     half = max(1, sum(j.bit_count() > 1 for j in js))
     width = n_tensor * 2 * blk
 
@@ -115,9 +110,9 @@
         p, c, _ = place()
         out[...] = weight[pl.ds(pl.multiple_of((p * 2 + c) * blk, LANES), blk), :]
 
-    packs = kernel_call(pack_body, [shape((tok, width + vdim), bf16)] * (chips - 1), [activations, value_cotangent], "pack", OPT["c_pack"])
+    packs = kernel_call(pack_body, [shape((tok, width + vdim), bf16)] * (chips - 1), [activations, value_cotangent], "pack")
     weight_then, *packs = barrier((value_weight, *packs))
-    (own_slice,) = kernel_call(slice_body, [shape((blk, vdim), bf16)], [weight_then], "own_slice", OPT["c_slice"])
+    (own_slice,) = kernel_call(slice_body, [shape((blk, vdim), bf16)], [weight_then], "own_slice")
     got = [across(x, q) for q, x in enumerate(packs, 1)]
 
     slots = sorted(range(1, n_tensor), key=lambda j: (j.bit_count(), -j))
@@ -143,7 +138,7 @@
         out_specs=[whole, anywhere],
         scratch_shapes=[pltpu.VMEM((tok, quarter), bf16), pltpu.SemaphoreType.DMA],
         compiler_params=pltpu.CompilerParams(vmem_limit_bytes=VMEM_LIMIT),
-        cost_estimate=estimate(OPT["c_qtr"]),
+        cost_estimate=estimate(0),
         name="own_quarter",
     )(activations, value_cotangent, weight_then)
 
@@ -194,9 +189,9 @@
         return out.astype(jnp.float16) if pack else out
 
     got[0], acc, *_ = barrier((got[0], acc, *held))
-    keep_1, send_1 = sums_of(js[:half], 0, OPT["c_sums1"])
-    keep_2, send_2 = sums_of(js[half:], half, OPT["c_sums2"])
-    mine = stack(held, OPT["c_mine"])
+    keep_1, send_1 = sums_of(js[:half], 0, 30)
+    keep_2, send_2 = sums_of(js[half:], half, 20)
+    mine = stack(held)
     twin_1, twin_2 = twin(send_1), twin(send_2)
     terms = {j: [(keep_1, i * blk, None), (twin_1, i * blk, None)] for i, j in enumerate(js[:half])}
     terms.update({j: [(keep_2, i * blk, None), (twin_2, i * blk, None)] for i, j in enumerate(js[half:])})
@@ -206,7 +201,7 @@
     late = [q for q in range(chips) if q.bit_count() >= 2]
     pieces = {0: [mine], **{q: [across(mine, q)] for q in singles}}
 
-    def product(acc, grad, qs, ours, total=None, twins=None):
+    def product(acc, grad, qs, ours, twins, total=None):
         last = total is not None
         n = (n_tensor - 1) * len(qs)
 
@@ -241,7 +236,7 @@
             for copy in copies:
                 copy.wait()
 
-        args = [activations, value_cotangent, acc, grad, ours, twin(ours) if twins is None else twins] + [total] * last
+        args = [activations, value_cotangent, acc, grad, ours, twins] + [total] * last
         outs = [shape((tok, vdim), bf16 if last else f32), shape((tok, depth), bf16)] + [shape((blk, vdim), f32)] * last
         scratch = [pltpu.VMEM((tok, vdim), bf16), pltpu.VMEM((blk, vdim), f32)] * last
         return pl.pallas_call(
@@ -252,7 +247,7 @@
             scratch_shapes=scratch + [pltpu.VMEM((n, tok, 2 * blk), bf16), pltpu.SemaphoreType.DMA((n + 2,))],
             input_output_aliases={3: 1},
             compiler_params=pltpu.CompilerParams(vmem_limit_bytes=VMEM_LIMIT),
-            cost_estimate=estimate(OPT["c_last"] if last else OPT["c_prod"]),
+            cost_estimate=estimate(0),
             name="product",
         )(*args)
 
@@ -262,46 +257,27 @@
         terms[j] = [(a, at, power_at), *others]
         return x
 
-    early, ours_early, done = [0, *singles], None, False
+    early, ours_early = [0, *singles], None
     for i, j in enumerate(js[:-1]):
-        last_hop = i == (n_tensor - 2 if OPT["s1e"] else half)
-        if last_hop:
-            if OPT["s1e"] and i > half:
-                arrived = tie(j, arrived)
-                (x, at, power_at) = terms[0][-1]
-                terms[0][-1] = (arrived, at, power_at)
-            ours_early = stack([x for q in early for x in pieces[q]], OPT["c_estack"])
-            if OPT["ws2"]:
-                ours_early = tie(j, ours_early)
-        if i == half and OPT["s1p"] == 2:
+        if i == half:
+            ours_early = tie(j, stack([x for q in early for x in pieces[q]], 60))
             twin_early = twin(ours_early)
-        if not OPT["s1e"] and i > half and OPT["s1p"] == 2:
+        if i > half:
             twin_early = tie(j, twin_early)
-        if not OPT["s1e"] and i > half and not done and late and OPT["s1p"] < 2:
-            acc, grad = product(acc, grad, early, ours_early)
-            done = True
-        if i > half and done and OPT["s1p"] == 1:
-            acc = tie(j, acc)
-        packed = join([terms[j]], True, OPT["c_join1"] if i < half else OPT["c_join2"] if last_hop else OPT["c_join3"])
-        if i == half - 1 and OPT["s1t"] and len(js) > half + 2:
-            packed = tie(js[half], packed)
-        if i == (half if OPT["s1e"] and len(js) > half + 2 else 0) and OPT["st2_after"] == 2:
+        packed = join([terms[j]], True, 30 if i == half else 0)
+        if i == 0:
             _, *then = barrier((packed, *[pieces[q][0] for q in singles]))
             pieces.update({q: [x] for q, x in zip(singles, then)})
         arrived = along(packed, j & -j).astype(f32)
         terms[j & (j - 1)].append((arrived, 0, blk))
     if ours_early is None:
-        ours_early = stack([x for q in early for x in pieces[q]], OPT["c_estack"])
-    if late and not done:
-        acc, grad = product(acc, grad, early, ours_early, None, twin_early if OPT["s1p"] == 2 else None)
-
-    if late and OPT["pt"]:
-        acc = tie(0, acc)
-    after = [twin(acc[:8, :LANES])] if OPT["tok"] and late else []
-    if not OPT["jl"] or not late:
-        total = join([terms[0]], False, OPT["c_joinf"], after)
+        ours_early = stack([x for q in early for x in pieces[q]], 60)
+        twin_early = twin(ours_early)
     if not late:
-        return product(acc, grad, early, ours_early, total)
+        return product(acc, grad, early, ours_early, twin_early, join([terms[0]], False, 5))
+    acc, grad = product(acc, grad, early, ours_early, twin_early)
+
+    total = join([terms[0]], False, 5, [twin(acc[:8, :LANES])])
     for q in sorted(late, key=lambda q: q.bit_count()):
         bits = [b for b in singles if q & b]
         cuts = [rows * i // len(bits) // 16 * 16 for i in range(len(bits))] + [rows]
@@ -310,13 +286,8 @@
             there = stack(pieces[q ^ b]) if len(pieces[q ^ b]) > 1 else pieces[q ^ b][0]
             ways.append(across(there[cuts[i] : cuts[i + 1]], b))
         pieces[q] = ways
-    ours_late = stack([x for q in late for x in pieces[q]], OPT["c_e2stack"])
-    if OPT["jl"]:
-        ours_late = tie(0, ours_late)
-        total = join([terms[0]], False, OPT["c_joinf"])
-    if OPT["e2p"]:
-        ours_late, acc = barrier((ours_late, acc))
-    return product(acc, grad, late, ours_late, total)
+    ours_late = stack([x for q in late for x in pieces[q]])
+    return product(acc, grad, late, ours_late, twin(ours_late), total)
 
 
 def solution(mesh):

time: 47.8 us -> 47.8 us (level)
  no operation moved by 1% of the time
where the time goes in v5:
time: 47.8 us; the launch traced here: 47.6 us
  starting transfers between devices  22.4 us (47%)
  waiting for transfers between devices  14.8 us (31%)
  Pallas kernels  6.03 us (13%)
  local copies, waits for them, and re-layouts  3.39 us (7%)
  between operations  0.89 us (2%)
    ppermute x18, starting transfers between devices, exchange(): return lax.ppermute(x, AXES, pairs)  22.4 us
    ppermute x18, waiting for transfers between devices, exchange(): return lax.ppermute(x, AXES, pairs)  14.8 us
    unnamed x10, local copies, waits for them, and re-layouts  3.35 us
    pallas_call x2, Pallas kernels, product(): pl.pallas_call(body, out_shape=outs, in_specs=[whole] * 3 + [anywhere] +...  3.01 us
    pallas_call x11, Pallas kernels, kernel_call(): pl.pallas_call(body, out_shape=out_shapes, in_specs=[whole] * len(args),...  1.82 us
    pallas_call x1, Pallas kernels, paired_form(): pl.pallas_call(quarter_body, out_shape=[shape((tok, vdim), f32), shape((t...  1.2 us
  transfers between devices with their start and end apart: 18, of which 8 were waited for; matrix products, arithmetic and copies ran while one was open for 0% of the time, Pallas kernels for 10%

profile of v5, /device:TPU:0, one launch (start us, length us, event | category | flops | bytes accessed | tf_op | source)
XLA Modules:
  0.0 47.6 jit_solution(17308099210892367816)
XLA Ops:
  0.6 1.2 %copy-done = bf16[128,4096]{1,0:T(8,128)(2,1)S(1)} copy-done((bf16[128,4096]{1,0:T(8,128)(2,1)S(1)}, bf16[128,4096]{1,0:T(8,128)(2,1)}, u32[]{:S(2)}) %copy-start) | copy-done | bytes 1048600
  1.9 0.9 %copy-done.3 = bf16[128,512]{1,0:T(8,128)(2,1)S(1)} copy-done((bf16[128,512]{1,0:T(8,128)(2,1)S(1)}, bf16[128,512]{1,0:T(8,128)(2,1)}, u32[]{:S(2)}) %copy-start.3) | copy-done | bytes 131096
  2.9 3.0 %collective-permute-start = (bf16[128,1536]{1,0:T(8,128)(2,1)S(1)}, bf16[128,1536]{1,0:T(8,128)(2,1)S(1)}, u32[]{:S(2)}, u32[]{:S(2)}) collective-permute-start(bf16[128,1536]{1,0:T(8,128)(2,1)S(1)} %get-tuple-element.30), channel_id=1, source_target_pairs={{0,8},{1,9},{2,10},{3,11},{4,12},{5,13},{6,14},{7,15},{8,0},{9,1},... | collective-permute-start | bytes 1179656 | tf_op jit(solution)/shard_map/ppermute | solution.py:36
  5.9 1.5 %collective-permute-start.4 = (bf16[128,1536]{1,0:T(8,128)(2,1)S(1)}, bf16[128,1536]{1,0:T(8,128)(2,1)S(1)}, u32[]{:S(2)}, u32[]{:S(2)}) collective-permute-start(bf16[128,1536]{1,0:T(8,128)(2,1)S(1)} %get-tuple-element.37), channel_id=1, source_target_pairs={{0,16},{1,17},{2,18},{3,19},{4,20},{5,21},{6,22},{7,23},{8,24},{9,... | collective-permute-start | bytes 1179656 | tf_op jit(solution)/shard_map/ppermute | solution.py:36
  7.4 1.2 %copy-done.2 = bf16[1024,512]{1,0:T(8,128)(2,1)S(1)} copy-done((bf16[1024,512]{1,0:T(8,128)(2,1)S(1)}, bf16[1024,512]{1,0:T(8,128)(2,1)}, u32[]{:S(2)}) %copy-start.2) | copy-done | bytes 1048600
  8.7 3.1 %collective-permute-start.1 = (bf16[128,512]{1,0:T(8,128)(2,1)S(1)}, bf16[128,512]{1,0:T(8,128)(2,1)S(1)}, u32[]{:S(2)}, u32[]{:S(2)}) collective-permute-start(bf16[128,512]{1,0:T(8,128)(2,1)S(1)} %own_slice.1), channel_id=1, source_target_pairs={{0,2},{1,3},{2,0},{3,1},{4,6},{5,7},{6,4},{7,5},{8,10},{9,11},{10,... | collective-permute-start | bytes 393224 | tf_op jit(solution)/shard_map/ppermute | solution.py:36
  11.8 1.6 %collective-permute-start.2 = (bf16[128,512]{1,0:T(8,128)(2,1)S(1)}, bf16[128,512]{1,0:T(8,128)(2,1)S(1)}, u32[]{:S(2)}, u32[]{:S(2)}) collective-permute-start(bf16[128,512]{1,0:T(8,128)(2,1)S(1)} %own_slice.1), channel_id=1, source_target_pairs={{0,1},{1,0},{2,3},{3,2},{4,5},{5,4},{6,7},{7,6},{8,9},{9,8},{10,11... | collective-permute-start | bytes 393224 | tf_op jit(solution)/shard_map/ppermute | solution.py:36
  13.4 4.0 %collective-permute-done.1.refs_0_ = bf16[128,512]{1,0:T(8,128)(2,1)S(1)} collective-permute-done((bf16[128,512]{1,0:T(8,128)(2,1)S(1)}, bf16[128,512]{1,0:T(8,128)(2,1)S(1)}, u32[]{:S(2)}, u32[]{:S(2)}) %collective-permute-start.1) | collective-permute-done | bytes 131104 | tf_op jit(solution)/shard_map/ppermute | solution.py:36
  17.4 0.6 %collective-permute-start.3 = (bf16[128,512]{1,0:T(8,128)(2,1)S(1)}, bf16[128,512]{1,0:T(8,128)(2,1)S(1)}, u32[]{:S(2)}, u32[]{:S(2)}) collective-permute-start(bf16[128,512]{1,0:T(8,128)(2,1)S(1)} %collective-permute-done.1.refs_0_), channel_id=1, source_target_pairs={{0,1},{1,0},{2,3},{3,2},{4,5},{5,4},{6,7},{7,6},{8,9},{9,8},{10,11... | collective-permute-start | bytes 393224 | tf_op jit(solution)/shard_map/ppermute | solution.py:36
  18.0 1.2 %own_quarter.1 = (f32[128,512]{1,0:T(8,128)S(1)}, bf16[128,4096]{1,0:T(8,128)(2,1)}) custom-call(bf16[128,4096]{1,0:T(8,128)(2,1)S(1)} %copy-done.1, bf16[128,512]{1,0:T(8,128)(2,1)S(1)} %copy-done.4, bf16[1024,512]{1,0:T(8,128)(2,1)S(1)} %copy-done.2), custom_call_target="tpu_custom_call" | custom-call | bytes 1024 | tf_op jit(solution)/shard_map/own_quarter/pallas_call | solution.py:134
  19.2 3.1 %collective-permute-done.3.refs_2_ = bf16[128,512]{1,0:T(8,128)(2,1)S(1)} collective-permute-done((bf16[128,512]{1,0:T(8,128)(2,1)S(1)}, bf16[128,512]{1,0:T(8,128)(2,1)S(1)}, u32[]{:S(2)}, u32[]{:S(2)}) %collective-permute-start.3) | collective-permute-done | bytes 131104 | tf_op jit(solution)/shard_map/ppermute | solution.py:36
  22.4 1.6 %collective-permute-start.7 = (bf16[384,512]{1,0:T(8,128)(2,1)S(1)}, bf16[384,512]{1,0:T(8,128)(2,1)S(1)}, u32[]{:S(2)}, u32[]{:S(2)}) collective-permute-start(bf16[384,512]{1,0:T(8,128)(2,1)S(1)} %stack.3.refs_0_), channel_id=1, source_target_pairs={{0,8},{1,9},{2,10},{3,11},{4,12},{5,13},{6,14},{7,15},{8,0},{9,1},... | collective-permute-start | bytes 1179656 | tf_op jit(solution)/shard_map/ppermute | solution.py:36
  24.0 1.5 %collective-permute-start.8 = (bf16[384,512]{1,0:T(8,128)(2,1)S(1)}, bf16[384,512]{1,0:T(8,128)(2,1)S(1)}, u32[]{:S(2)}, u32[]{:S(2)}) collective-permute-start(bf16[384,512]{1,0:T(8,128)(2,1)S(1)} %stack.3.refs_0_), channel_id=1, source_target_pairs={{0,16},{1,17},{2,18},{3,19},{4,20},{5,21},{6,22},{7,23},{8,24},{9,... | collective-permute-start | bytes 1179656 | tf_op jit(solution)/shard_map/ppermute | solution.py:36
  26.3 0.6 %sums.2 = (f32[384,512]{1,0:T(8,128)S(1)}, f32[384,512]{1,0:T(8,128)S(1)}) custom-call(bf16[128,4096]{1,0:T(8,128)(2,1)S(1)} %copy-done.1, bf16[128,512]{1,0:T(8,128)(2,1)S(1)} %copy-done.4, bf16[128,1536]{1,0:T(8,128)(2,1)S(1)} %collective-permute-done.refs_0_, bf16[128,1536]{1,0:T(8,128)(2,1)S(1)} %collective-permute-done.4.refs_1_, ...), custom_call_target="tpu_custom_call" | custom-call | flops 23000000512 | bytes 1024 | tf_op jit(solution)/shard_map/sums/pallas_call | solution.py:45
  28.0 1.6 %collective-permute-start.14 = (f16[144,512]{1,0:T(8,128)(2,1)S(1)}, f16[144,512]{1,0:T(8,128)(2,1)S(1)}, u32[]{:S(2)}, u32[]{:S(2)}) collective-permute-start(f16[144,512]{1,0:T(8,128)(2,1)S(1)} %convert_element_type.18), channel_id=1, source_target_pairs={{0,1},{1,0},{2,3},{3,2},{4,5},{5,4},{6,7},{7,6},{8,9},{9,8},{10,11... | collective-permute-start | bytes 442376 | tf_op jit(solution)/shard_map/ppermute | solution.py:36
  29.6 2.3 %collective-permute-done.7.refs_1_ = bf16[384,512]{1,0:T(8,128)(2,1)S(1)} collective-permute-done((bf16[384,512]{1,0:T(8,128)(2,1)S(1)}, bf16[384,512]{1,0:T(8,128)(2,1)S(1)}, u32[]{:S(2)}, u32[]{:S(2)}) %collective-permute-start.7) | collective-permute-done | bytes 393248 | tf_op jit(solution)/shard_map/ppermute | solution.py:36
  31.9 1.4 %collective-permute-done.8.refs_2_ = bf16[384,512]{1,0:T(8,128)(2,1)S(1)} collective-permute-done((bf16[384,512]{1,0:T(8,128)(2,1)S(1)}, bf16[384,512]{1,0:T(8,128)(2,1)S(1)}, u32[]{:S(2)}, u32[]{:S(2)}) %collective-permute-start.8) | collective-permute-done | bytes 393248 | tf_op jit(solution)/shard_map/ppermute | solution.py:36
  33.5 1.3 %collective-permute-start.10 = (bf16[192,512]{1,0:T(8,128)(2,1)S(1)}, bf16[192,512]{1,0:T(8,128)(2,1)S(1)}, u32[]{:S(2)}, u32[]{:S(2)}) collective-permute-start(bf16[192,512]{1,0:T(8,128)(2,1)S(1)} %slice.9), channel_id=1, source_target_pairs={{0,8},{1,9},{2,10},{3,11},{4,12},{5,13},{6,14},{7,15},{8,0},{9,1},... | collective-permute-start | bytes 589832 | tf_op jit(solution)/shard_map/ppermute | solution.py:36
  34.8 0.8 %collective-permute-start.11 = (bf16[192,512]{1,0:T(8,128)(2,1)S(1)}, bf16[192,512]{1,0:T(8,128)(2,1)S(1)}, u32[]{:S(2)}, u32[]{:S(2)}) collective-permute-start(bf16[192,512]{1,0:T(8,128)(2,1)S(1)} %slice.10), channel_id=1, source_target_pairs={{0,16},{1,17},{2,18},{3,19},{4,20},{5,21},{6,22},{7,23},{8,24},{9,... | collective-permute-start | bytes 589832 | tf_op jit(solution)/shard_map/ppermute | solution.py:36
  35.9 2.7 %collective-permute-start.15 = (f16[144,512]{1,0:T(8,128)(2,1)S(1)}, f16[144,512]{1,0:T(8,128)(2,1)S(1)}, u32[]{:S(2)}, u32[]{:S(2)}) collective-permute-start(f16[144,512]{1,0:T(8,128)(2,1)S(1)} %convert_element_type.20), channel_id=1, source_target_pairs={{0,2},{1,3},{2,0},{3,1},{4,6},{5,7},{6,4},{7,5},{8,10},{9,11},{10,... | collective-permute-start | bytes 442376 | tf_op jit(solution)/shard_map/ppermute | solution.py:36
  38.8 1.6 %collective-permute-start.16 = (f16[144,512]{1,0:T(8,128)(2,1)S(1)}, f16[144,512]{1,0:T(8,128)(2,1)S(1)}, u32[]{:S(2)}, u32[]{:S(2)}) collective-permute-start(f16[144,512]{1,0:T(8,128)(2,1)S(1)} %convert_element_type.22), channel_id=1, source_target_pairs={{0,1},{1,0},{2,3},{3,2},{4,5},{5,4},{6,7},{7,6},{8,9},{9,8},{10,11... | collective-permute-start | bytes 442376 | tf_op jit(solution)/shard_map/ppermute | solution.py:36
  40.4 1.8 %product.2 = (f32[128,512]{1,0:T(8,128)S(1)}, bf16[128,4096]{1,0:T(8,128)(2,1)}) custom-call(bf16[128,4096]{1,0:T(8,128)(2,1)S(1)} %copy-done.1, bf16[128,512]{1,0:T(8,128)(2,1)S(1)} %copy-done.4, f32[128,512]{1,0:T(8,128)S(1)} %get-tuple-element.34.acc, bf16[128,4096]{1,0:T(8,128)(2,1)} %get-tuple-element.35._, ...), custom_call_target="tpu_custom_call", output_to_operand_aliasing={{1}: (3, {})} | custom-call | bytes 1024 | tf_op jit(solution)/shard_map/product/pallas_call | solution.py:242
  43.0 2.8 %collective-permute-done.15 = f16[144,512]{1,0:T(8,128)(2,1)S(1)} collective-permute-done((f16[144,512]{1,0:T(8,128)(2,1)S(1)}, f16[144,512]{1,0:T(8,128)(2,1)S(1)}, u32[]{:S(2)}, u32[]{:S(2)}) %collective-permute-start.15) | collective-permute-done | bytes 147488 | tf_op jit(solution)/shard_map/ppermute | solution.py:36
  46.4 1.2 %product.3 = (bf16[128,512]{1,0:T(8,128)(2,1)}, bf16[128,4096]{1,0:T(8,128)(2,1)}, f32[128,512]{1,0:T(8,128)}) custom-call(bf16[128,4096]{1,0:T(8,128)(2,1)S(1)} %copy-done.1, bf16[128,512]{1,0:T(8,128)(2,1)S(1)} %copy-done.4, f32[128,512]{1,0:T(8,128)S(1)} %get-tuple-element.46.acc, ...), custom_call_target="tpu_custom_call", output_to_operand_aliasing={{1}: (3, {})} | custom-call | bytes 1024 | tf_op jit(solution)/shard_map/product/pallas_call | solution.py:242
  (45 shorter events, 3.9 us)
Async XLA Ops:
  0.6 1.2 %copy-start = (bf16[128,4096]{1,0:T(8,128)(2,1)S(1)}, bf16[128,4096]{1,0:T(8,128)(2,1)}, u32[]{:S(2)}) copy-start(bf16[128,4096]{1,0:T(8,128)(2,1)} %act.11) | copy-start | bytes 3145732
  1.9 0.9 %copy-start.3 = (bf16[128,512]{1,0:T(8,128)(2,1)S(1)}, bf16[128,512]{1,0:T(8,128)(2,1)}, u32[]{:S(2)}) copy-start(bf16[128,512]{1,0:T(8,128)(2,1)} %cot.11) | copy-start | bytes 393220
  2.8 15.2 %copy-start.1 = (bf16[128,4096]{1,0:T(8,128)(2,1)S(1)}, bf16[128,4096]{1,0:T(8,128)(2,1)}, u32[]{:S(2)}) copy-start(bf16[128,4096]{1,0:T(8,128)(2,1)} %act.11) | copy-start | bytes 3145732
  2.8 15.2 %copy-start.4 = (bf16[128,512]{1,0:T(8,128)(2,1)S(1)}, bf16[128,512]{1,0:T(8,128)(2,1)}, u32[]{:S(2)}) copy-start(bf16[128,512]{1,0:T(8,128)(2,1)} %cot.11) | copy-start | bytes 393220
  2.9 22.6 %collective-permute-start = (bf16[128,1536]{1,0:T(8,128)(2,1)S(1)}, bf16[128,1536]{1,0:T(8,128)(2,1)S(1)}, u32[]{:S(2)}, u32[]{:S(2)}) collective-permute-start(bf16[128,1536]{1,0:T(8,128)(2,1)S(1)} %get-tuple-element.30), channel_id=1, source_target_pairs={{0,8},{1,9},{2,10},{3,11},{4,12},{5,13},{6,14},{7,15},{8,0},{9,1},... | collective-permute-start | bytes 1179656 | tf_op jit(solution)/shard_map/ppermute | solution.py:36
  5.9 19.6 %collective-permute-start.4 = (bf16[128,1536]{1,0:T(8,128)(2,1)S(1)}, bf16[128,1536]{1,0:T(8,128)(2,1)S(1)}, u32[]{:S(2)}, u32[]{:S(2)}) collective-permute-start(bf16[128,1536]{1,0:T(8,128)(2,1)S(1)} %get-tuple-element.37), channel_id=1, source_target_pairs={{0,16},{1,17},{2,18},{3,19},{4,20},{5,21},{6,22},{7,23},{8,24},{9,... | collective-permute-start | bytes 1179656 | tf_op jit(solution)/shard_map/ppermute | solution.py:36
  7.4 18.4 %collective-permute-start.5 = (bf16[128,1536]{1,0:T(8,128)(2,1)S(1)}, bf16[128,1536]{1,0:T(8,128)(2,1)S(1)}, u32[]{:S(2)}, u32[]{:S(2)}) collective-permute-start(bf16[128,1536]{1,0:T(8,128)(2,1)S(1)} %get-tuple-element.38), channel_id=1, source_target_pairs={{0,24},{1,25},{2,26},{3,27},{4,28},{5,29},{6,30},{7,31},{8,16},{9,... | collective-permute-start | bytes 1179656 | tf_op jit(solution)/shard_map/ppermute | solution.py:36
  7.4 1.2 %copy-start.2 = (bf16[1024,512]{1,0:T(8,128)(2,1)S(1)}, bf16[1024,512]{1,0:T(8,128)(2,1)}, u32[]{:S(2)}) copy-start(bf16[1024,512]{1,0:T(8,128)(2,1)} %w) | copy-start | bytes 3145732
  8.7 8.7 %collective-permute-start.1 = (bf16[128,512]{1,0:T(8,128)(2,1)S(1)}, bf16[128,512]{1,0:T(8,128)(2,1)S(1)}, u32[]{:S(2)}, u32[]{:S(2)}) collective-permute-start(bf16[128,512]{1,0:T(8,128)(2,1)S(1)} %own_slice.1), channel_id=1, source_target_pairs={{0,2},{1,3},{2,0},{3,1},{4,6},{5,7},{6,4},{7,5},{8,10},{9,11},{10,... | collective-permute-start | bytes 393224 | tf_op jit(solution)/shard_map/ppermute | solution.py:36
  11.8 7.4 %collective-permute-start.2 = (bf16[128,512]{1,0:T(8,128)(2,1)S(1)}, bf16[128,512]{1,0:T(8,128)(2,1)S(1)}, u32[]{:S(2)}, u32[]{:S(2)}) collective-permute-start(bf16[128,512]{1,0:T(8,128)(2,1)S(1)} %own_slice.1), channel_id=1, source_target_pairs={{0,1},{1,0},{2,3},{3,2},{4,5},{5,4},{6,7},{7,6},{8,9},{9,8},{10,11... | collective-permute-start | bytes 393224 | tf_op jit(solution)/shard_map/ppermute | solution.py:36
  17.4 5.0 %collective-permute-start.3 = (bf16[128,512]{1,0:T(8,128)(2,1)S(1)}, bf16[128,512]{1,0:T(8,128)(2,1)S(1)}, u32[]{:S(2)}, u32[]{:S(2)}) collective-permute-start(bf16[128,512]{1,0:T(8,128)(2,1)S(1)} %collective-permute-done.1.refs_0_), channel_id=1, source_target_pairs={{0,1},{1,0},{2,3},{3,2},{4,5},{5,4},{6,7},{7,6},{8,9},{9,8},{10,11... | collective-permute-start | bytes 393224 | tf_op jit(solution)/shard_map/ppermute | solution.py:36
  22.4 9.6 %collective-permute-start.7 = (bf16[384,512]{1,0:T(8,128)(2,1)S(1)}, bf16[384,512]{1,0:T(8,128)(2,1)S(1)}, u32[]{:S(2)}, u32[]{:S(2)}) collective-permute-start(bf16[384,512]{1,0:T(8,128)(2,1)S(1)} %stack.3.refs_0_), channel_id=1, source_target_pairs={{0,8},{1,9},{2,10},{3,11},{4,12},{5,13},{6,14},{7,15},{8,0},{9,1},... | collective-permute-start | bytes 1179656 | tf_op jit(solution)/shard_map/ppermute | solution.py:36
  24.0 9.4 %collective-permute-start.8 = (bf16[384,512]{1,0:T(8,128)(2,1)S(1)}, bf16[384,512]{1,0:T(8,128)(2,1)S(1)}, u32[]{:S(2)}, u32[]{:S(2)}) collective-permute-start(bf16[384,512]{1,0:T(8,128)(2,1)S(1)} %stack.3.refs_0_), channel_id=1, source_target_pairs={{0,16},{1,17},{2,18},{3,19},{4,20},{5,21},{6,22},{7,23},{8,24},{9,... | collective-permute-start | bytes 1179656 | tf_op jit(solution)/shard_map/ppermute | solution.py:36
  26.2 1.6 %collective-permute-start.6 = (f32[128,512]{1,0:T(8,128)S(1)}, f32[128,512]{1,0:T(8,128)S(1)}, u32[]{:S(2)}, u32[]{:S(2)}) collective-permute-start(f32[128,512]{1,0:T(8,128)S(1)} %get-tuple-element.41), channel_id=1, source_target_pairs={{0,4},{1,5},{2,6},{3,7},{4,0},{5,1},{6,2},{7,3},{8,12},{9,13},{10,... | collective-permute-start | bytes 786440 | tf_op jit(solution)/shard_map/ppermute | solution.py:36
  26.9 8.8 %collective-permute-start.13 = (f32[384,512]{1,0:T(8,128)S(1)}, f32[384,512]{1,0:T(8,128)S(1)}, u32[]{:S(2)}, u32[]{:S(2)}) collective-permute-start(f32[384,512]{1,0:T(8,128)S(1)} %get-tuple-element.48), channel_id=1, source_target_pairs={{0,4},{1,5},{2,6},{3,7},{4,0},{5,1},{6,2},{7,3},{8,12},{9,13},{10,... | collective-permute-start | bytes 2359304 | tf_op jit(solution)/shard_map/ppermute | solution.py:36
  28.0 7.6 %collective-permute-start.14 = (f16[144,512]{1,0:T(8,128)(2,1)S(1)}, f16[144,512]{1,0:T(8,128)(2,1)S(1)}, u32[]{:S(2)}, u32[]{:S(2)}) collective-permute-start(f16[144,512]{1,0:T(8,128)(2,1)S(1)} %convert_element_type.18), channel_id=1, source_target_pairs={{0,1},{1,0},{2,3},{3,2},{4,5},{5,4},{6,7},{7,6},{8,9},{9,8},{10,11... | collective-permute-start | bytes 442376 | tf_op jit(solution)/shard_map/ppermute | solution.py:36
  33.5 5.1 %collective-permute-start.9 = (bf16[1152,512]{1,0:T(8,128)(2,1)S(1)}, bf16[1152,512]{1,0:T(8,128)(2,1)S(1)}, u32[]{:S(2)}, u32[]{:S(2)}) collective-permute-start(bf16[1152,512]{1,0:T(8,128)(2,1)S(1)} %stack.4.mine), channel_id=1, source_target_pairs={{0,4},{1,5},{2,6},{3,7},{4,0},{5,1},{6,2},{7,3},{8,12},{9,13},{10,... | collective-permute-start | bytes 3538952 | tf_op jit(solution)/shard_map/ppermute | solution.py:36
  33.5 8.8 %collective-permute-start.10 = (bf16[192,512]{1,0:T(8,128)(2,1)S(1)}, bf16[192,512]{1,0:T(8,128)(2,1)S(1)}, u32[]{:S(2)}, u32[]{:S(2)}) collective-permute-start(bf16[192,512]{1,0:T(8,128)(2,1)S(1)} %slice.9), channel_id=1, source_target_pairs={{0,8},{1,9},{2,10},{3,11},{4,12},{5,13},{6,14},{7,15},{8,0},{9,1},... | collective-permute-start | bytes 589832 | tf_op jit(solution)/shard_map/ppermute | solution.py:36
  34.8 7.5 %collective-permute-start.11 = (bf16[192,512]{1,0:T(8,128)(2,1)S(1)}, bf16[192,512]{1,0:T(8,128)(2,1)S(1)}, u32[]{:S(2)}, u32[]{:S(2)}) collective-permute-start(bf16[192,512]{1,0:T(8,128)(2,1)S(1)} %slice.10), channel_id=1, source_target_pairs={{0,16},{1,17},{2,18},{3,19},{4,20},{5,21},{6,22},{7,23},{8,24},{9,... | collective-permute-start | bytes 589832 | tf_op jit(solution)/shard_map/ppermute | solution.py:36
  35.9 9.9 %collective-permute-start.15 = (f16[144,512]{1,0:T(8,128)(2,1)S(1)}, f16[144,512]{1,0:T(8,128)(2,1)S(1)}, u32[]{:S(2)}, u32[]{:S(2)}) collective-permute-start(f16[144,512]{1,0:T(8,128)(2,1)S(1)} %convert_element_type.20), channel_id=1, source_target_pairs={{0,2},{1,3},{2,0},{3,1},{4,6},{5,7},{6,4},{7,5},{8,10},{9,11},{10,... | collective-permute-start | bytes 442376 | tf_op jit(solution)/shard_map/ppermute | solution.py:36
  38.8 7.5 %collective-permute-start.16 = (f16[144,512]{1,0:T(8,128)(2,1)S(1)}, f16[144,512]{1,0:T(8,128)(2,1)S(1)}, u32[]{:S(2)}, u32[]{:S(2)}) collective-permute-start(f16[144,512]{1,0:T(8,128)(2,1)S(1)} %convert_element_type.22), channel_id=1, source_target_pairs={{0,1},{1,0},{2,3},{3,2},{4,5},{5,4},{6,7},{7,6},{8,9},{9,8},{10,11... | collective-permute-start | bytes 442376 | tf_op jit(solution)/shard_map/ppermute | solution.py:36
  42.3 4.0 %collective-permute-start.17 = (f32[8,128]{1,0:T(8,128)S(1)}, f32[8,128]{1,0:T(8,128)S(1)}, u32[]{:S(2)}, u32[]{:S(2)}) collective-permute-start(f32[8,128]{1,0:T(8,128)S(1)} %slice.11), channel_id=1, source_target_pairs={{0,4},{1,5},{2,6},{3,7},{4,0},{5,1},{6,2},{7,3},{8,12},{9,13},{10,... | collective-permute-start | bytes 12296 | tf_op jit(solution)/shard_map/ppermute | solution.py:36
  42.4 3.9 %collective-permute-start.12 = (bf16[384,512]{1,0:T(8,128)(2,1)S(1)}, bf16[384,512]{1,0:T(8,128)(2,1)S(1)}, u32[]{:S(2)}, u32[]{:S(2)}) collective-permute-start(bf16[384,512]{1,0:T(8,128)(2,1)S(1)} %stack.5.mine), channel_id=1, source_target_pairs={{0,4},{1,5},{2,6},{3,7},{4,0},{5,1},{6,2},{7,3},{8,12},{9,13},{10,... | collective-permute-start | bytes 1179656 | tf_op jit(solution)/shard_map/ppermute | solution.py:36

commit v6 on v5

--- a/solution.py
+++ b/solution.py
@@ -99,18 +99,20 @@
     half = max(1, sum(j.bit_count() > 1 for j in js))
     width = n_tensor * 2 * blk
 
-    def pack_body(act, cot, *outs):
+    both = jnp.concatenate([activations, value_cotangent], axis=1)
+
+    def pack_body(both, *outs):
         p, _, t = place()
         for q, out in enumerate(outs, 1):
             for i, j in enumerate(js):
-                out[:, i * 2 * blk : (i + 1) * 2 * blk] = act[:, pl.ds(column(t ^ j, p ^ q), 2 * blk)]
-            out[:, width:] = cot[...]
+                out[:, i * 2 * blk : (i + 1) * 2 * blk] = both[:, pl.ds(column(t ^ j, p ^ q), 2 * blk)]
+            out[:, width:] = both[:, depth:]
 
     def slice_body(weight, out):
         p, c, _ = place()
         out[...] = weight[pl.ds(pl.multiple_of((p * 2 + c) * blk, LANES), blk), :]
 
-    packs = kernel_call(pack_body, [shape((tok, width + vdim), bf16)] * (chips - 1), [activations, value_cotangent], "pack")
+    packs = kernel_call(pack_body, [shape((tok, width + vdim), bf16)] * (chips - 1), [both], "pack")
     weight_then, *packs = barrier((value_weight, *packs))
     (own_slice,) = kernel_call(slice_body, [shape((blk, vdim), bf16)], [weight_then], "own_slice")
     got = [across(x, q) for q, x in enumerate(packs, 1)]

time: 47.8 us -> 47 us (0.983)
  local copies, waits for them, and re-layouts: 3.39 us -> 0.05 us
  other arithmetic: 0.13 us -> 1.59 us
  waiting for transfers between devices: 14.8 us -> 16 us
    unnamed x10 -> x6, local copies, waits for them, and re-layouts: 3.35 us -> 0.02 us
    concatenate x0 -> x1, other arithmetic: none -> 1.45 us  [paired_form(): both = jnp.concatenate([activations, value_cotangent], axis=1)]
    ppermute x18, waiting for transfers between devices: 14.8 us -> 16 us  [exchange(): return lax.ppermute(x, AXES, pairs)]
  transfers between devices with their start and end apart: 18 -> 18, of which waited for: 8 -> 9; matrix products, arithmetic and copies ran while one was open for 0% -> 0% of each run, Pallas kernels for 10% -> 10%
where the time goes in v6:
time: 47 us; the launch traced here: 46.9 us
  starting transfers between devices  22.4 us (48%)
  waiting for transfers between devices  16 us (34%)
  Pallas kernels  5.98 us (13%)
  other arithmetic  1.59 us (3%)
  between operations  0.91 us (2%)
    ppermute x18, starting transfers between devices, exchange(): return lax.ppermute(x, AXES, pairs)  22.4 us
    ppermute x18, waiting for transfers between devices, exchange(): return lax.ppermute(x, AXES, pairs)  16 us
    pallas_call x2, Pallas kernels, product(): pl.pallas_call(body, out_shape=outs, in_specs=[whole] * 3 + [anywhere] +...  3 us
    pallas_call x11, Pallas kernels, kernel_call(): pl.pallas_call(body, out_shape=out_shapes, in_specs=[whole] * len(args),...  1.78 us
    concatenate x1, other arithmetic, paired_form(): both = jnp.concatenate([activations, value_cotangent], axis=1)  1.45 us
    pallas_call x1, Pallas kernels, paired_form(): pl.pallas_call(quarter_body, out_shape=[shape((tok, vdim), f32), shape((t...  1.2 us
  transfers between devices with their start and end apart: 18, of which 9 were waited for; matrix products, arithmetic and copies ran while one was open for 0% of the time, Pallas kernels for 10%

profile of v6, /device:TPU:0, one launch (start us, length us, event | category | flops | bytes accessed | tf_op | source)
XLA Modules:
  0.0 46.9 jit_solution(18432220499979696262)
XLA Ops:
  0.6 1.5 %pad_maximum_fusion.both = bf16[128,4608]{1,0:T(8,128)(2,1)S(1)} fusion(bf16[128,512]{1,0:T(8,128)(2,1)} %cot.9, bf16[128,4096]{1,0:T(8,128)(2,1)} %act.9), kind=kLoop, calls=%fused_computation | loop fusion | flops 2359296 | bytes 2359296 | tf_op jit(solution)/shard_map/concatenate | solution.py:102
  2.2 3.0 %collective-permute-start = (bf16[128,1536]{1,0:T(8,128)(2,1)S(1)}, bf16[128,1536]{1,0:T(8,128)(2,1)S(1)}, u32[]{:S(2)}, u32[]{:S(2)}) collective-permute-start(bf16[128,1536]{1,0:T(8,128)(2,1)S(1)} %get-tuple-element.30), channel_id=1, source_target_pairs={{0,8},{1,9},{2,10},{3,11},{4,12},{5,13},{6,14},{7,15},{8,0},{9,1},... | collective-permute-start | bytes 1179656 | tf_op jit(solution)/shard_map/ppermute | solution.py:36
  5.2 1.5 %collective-permute-start.4 = (bf16[128,1536]{1,0:T(8,128)(2,1)S(1)}, bf16[128,1536]{1,0:T(8,128)(2,1)S(1)}, u32[]{:S(2)}, u32[]{:S(2)}) collective-permute-start(bf16[128,1536]{1,0:T(8,128)(2,1)S(1)} %get-tuple-element.37), channel_id=1, source_target_pairs={{0,16},{1,17},{2,18},{3,19},{4,20},{5,21},{6,22},{7,23},{8,24},{9,... | collective-permute-start | bytes 1179656 | tf_op jit(solution)/shard_map/ppermute | solution.py:36
  6.8 3.1 %collective-permute-start.1 = (bf16[128,512]{1,0:T(8,128)(2,1)S(1)}, bf16[128,512]{1,0:T(8,128)(2,1)S(1)}, u32[]{:S(2)}, u32[]{:S(2)}) collective-permute-start(bf16[128,512]{1,0:T(8,128)(2,1)S(1)} %own_slice.1), channel_id=1, source_target_pairs={{0,2},{1,3},{2,0},{3,1},{4,6},{5,7},{6,4},{7,5},{8,10},{9,11},{10,... | collective-permute-start | bytes 393224 | tf_op jit(solution)/shard_map/ppermute | solution.py:36
  9.9 1.6 %collective-permute-start.2 = (bf16[128,512]{1,0:T(8,128)(2,1)S(1)}, bf16[128,512]{1,0:T(8,128)(2,1)S(1)}, u32[]{:S(2)}, u32[]{:S(2)}) collective-permute-start(bf16[128,512]{1,0:T(8,128)(2,1)S(1)} %own_slice.1), channel_id=1, source_target_pairs={{0,1},{1,0},{2,3},{3,2},{4,5},{5,4},{6,7},{7,6},{8,9},{9,8},{10,11... | collective-permute-start | bytes 393224 | tf_op jit(solution)/shard_map/ppermute | solution.py:36
  11.5 4.0 %collective-permute-done.1.refs_0_ = bf16[128,512]{1,0:T(8,128)(2,1)S(1)} collective-permute-done((bf16[128,512]{1,0:T(8,128)(2,1)S(1)}, bf16[128,512]{1,0:T(8,128)(2,1)S(1)}, u32[]{:S(2)}, u32[]{:S(2)}) %collective-permute-start.1) | collective-permute-done | bytes 131104 | tf_op jit(solution)/shard_map/ppermute | solution.py:36
  15.5 0.6 %collective-permute-start.3 = (bf16[128,512]{1,0:T(8,128)(2,1)S(1)}, bf16[128,512]{1,0:T(8,128)(2,1)S(1)}, u32[]{:S(2)}, u32[]{:S(2)}) collective-permute-start(bf16[128,512]{1,0:T(8,128)(2,1)S(1)} %collective-permute-done.1.refs_0_), channel_id=1, source_target_pairs={{0,1},{1,0},{2,3},{3,2},{4,5},{5,4},{6,7},{7,6},{8,9},{9,8},{10,11... | collective-permute-start | bytes 393224 | tf_op jit(solution)/shard_map/ppermute | solution.py:36
  16.1 1.2 %own_quarter.1 = (f32[128,512]{1,0:T(8,128)S(1)}, bf16[128,4096]{1,0:T(8,128)(2,1)}) custom-call(bf16[128,4096]{1,0:T(8,128)(2,1)S(1)} %copy-done, bf16[128,512]{1,0:T(8,128)(2,1)S(1)} %copy-done.2, bf16[1024,512]{1,0:T(8,128)(2,1)S(1)} %copy-done.1), custom_call_target="tpu_custom_call" | custom-call | bytes 1024 | tf_op jit(solution)/shard_map/own_quarter/pallas_call | solution.py:136
  17.3 3.1 %collective-permute-done.3.refs_2_ = bf16[128,512]{1,0:T(8,128)(2,1)S(1)} collective-permute-done((bf16[128,512]{1,0:T(8,128)(2,1)S(1)}, bf16[128,512]{1,0:T(8,128)(2,1)S(1)}, u32[]{:S(2)}, u32[]{:S(2)}) %collective-permute-start.3) | collective-permute-done | bytes 131104 | tf_op jit(solution)/shard_map/ppermute | solution.py:36
  20.5 1.6 %collective-permute-start.7 = (bf16[384,512]{1,0:T(8,128)(2,1)S(1)}, bf16[384,512]{1,0:T(8,128)(2,1)S(1)}, u32[]{:S(2)}, u32[]{:S(2)}) collective-permute-start(bf16[384,512]{1,0:T(8,128)(2,1)S(1)} %stack.3.refs_0_), channel_id=1, source_target_pairs={{0,8},{1,9},{2,10},{3,11},{4,12},{5,13},{6,14},{7,15},{8,0},{9,1},... | collective-permute-start | bytes 1179656 | tf_op jit(solution)/shard_map/ppermute | solution.py:36
  22.1 1.5 %collective-permute-start.8 = (bf16[384,512]{1,0:T(8,128)(2,1)S(1)}, bf16[384,512]{1,0:T(8,128)(2,1)S(1)}, u32[]{:S(2)}, u32[]{:S(2)}) collective-permute-start(bf16[384,512]{1,0:T(8,128)(2,1)S(1)} %stack.3.refs_0_), channel_id=1, source_target_pairs={{0,16},{1,17},{2,18},{3,19},{4,20},{5,21},{6,22},{7,23},{8,24},{9,... | collective-permute-start | bytes 1179656 | tf_op jit(solution)/shard_map/ppermute | solution.py:36
  23.6 1.0 %collective-permute-done.4.refs_1_ = bf16[128,1536]{1,0:T(8,128)(2,1)S(1)} collective-permute-done((bf16[128,1536]{1,0:T(8,128)(2,1)S(1)}, bf16[128,1536]{1,0:T(8,128)(2,1)S(1)}, u32[]{:S(2)}, u32[]{:S(2)}) %collective-permute-start.4) | collective-permute-done | bytes 393248 | tf_op jit(solution)/shard_map/ppermute | solution.py:36
  25.6 0.6 %sums.2 = (f32[384,512]{1,0:T(8,128)S(1)}, f32[384,512]{1,0:T(8,128)S(1)}) custom-call(bf16[128,4096]{1,0:T(8,128)(2,1)S(1)} %copy-done, bf16[128,512]{1,0:T(8,128)(2,1)S(1)} %copy-done.2, bf16[128,1536]{1,0:T(8,128)(2,1)S(1)} %collective-permute-done.refs_0_, bf16[128,1536]{1,0:T(8,128)(2,1)S(1)} %collective-permute-done.4.refs_1_, ...), custom_call_target="tpu_custom_call" | custom-call | flops 23000000512 | bytes 1024 | tf_op jit(solution)/shard_map/sums/pallas_call | solution.py:45
  26.2 0.6 %collective-permute-start.13 = (f32[384,512]{1,0:T(8,128)S(1)}, f32[384,512]{1,0:T(8,128)S(1)}, u32[]{:S(2)}, u32[]{:S(2)}) collective-permute-start(f32[384,512]{1,0:T(8,128)S(1)} %get-tuple-element.48), channel_id=1, source_target_pairs={{0,4},{1,5},{2,6},{3,7},{4,0},{5,1},{6,2},{7,3},{8,12},{9,13},{10,... | collective-permute-start | bytes 2359304 | tf_op jit(solution)/shard_map/ppermute | solution.py:36
  27.3 1.6 %collective-permute-start.14 = (f16[144,512]{1,0:T(8,128)(2,1)S(1)}, f16[144,512]{1,0:T(8,128)(2,1)S(1)}, u32[]{:S(2)}, u32[]{:S(2)}) collective-permute-start(f16[144,512]{1,0:T(8,128)(2,1)S(1)} %convert_element_type.18), channel_id=1, source_target_pairs={{0,1},{1,0},{2,3},{3,2},{4,5},{5,4},{6,7},{7,6},{8,9},{9,8},{10,11... | collective-permute-start | bytes 442376 | tf_op jit(solution)/shard_map/ppermute | solution.py:36
  29.0 2.3 %collective-permute-done.7.refs_1_ = bf16[384,512]{1,0:T(8,128)(2,1)S(1)} collective-permute-done((bf16[384,512]{1,0:T(8,128)(2,1)S(1)}, bf16[384,512]{1,0:T(8,128)(2,1)S(1)}, u32[]{:S(2)}, u32[]{:S(2)}) %collective-permute-start.7) | collective-permute-done | bytes 393248 | tf_op jit(solution)/shard_map/ppermute | solution.py:36
  31.2 1.4 %collective-permute-done.8.refs_2_ = bf16[384,512]{1,0:T(8,128)(2,1)S(1)} collective-permute-done((bf16[384,512]{1,0:T(8,128)(2,1)S(1)}, bf16[384,512]{1,0:T(8,128)(2,1)S(1)}, u32[]{:S(2)}, u32[]{:S(2)}) %collective-permute-start.8) | collective-permute-done | bytes 393248 | tf_op jit(solution)/shard_map/ppermute | solution.py:36
  32.8 1.3 %collective-permute-start.10 = (bf16[192,512]{1,0:T(8,128)(2,1)S(1)}, bf16[192,512]{1,0:T(8,128)(2,1)S(1)}, u32[]{:S(2)}, u32[]{:S(2)}) collective-permute-start(bf16[192,512]{1,0:T(8,128)(2,1)S(1)} %slice.9), channel_id=1, source_target_pairs={{0,8},{1,9},{2,10},{3,11},{4,12},{5,13},{6,14},{7,15},{8,0},{9,1},... | collective-permute-start | bytes 589832 | tf_op jit(solution)/shard_map/ppermute | solution.py:36
  34.1 0.8 %collective-permute-start.11 = (bf16[192,512]{1,0:T(8,128)(2,1)S(1)}, bf16[192,512]{1,0:T(8,128)(2,1)S(1)}, u32[]{:S(2)}, u32[]{:S(2)}) collective-permute-start(bf16[192,512]{1,0:T(8,128)(2,1)S(1)} %slice.10), channel_id=1, source_target_pairs={{0,16},{1,17},{2,18},{3,19},{4,20},{5,21},{6,22},{7,23},{8,24},{9,... | collective-permute-start | bytes 589832 | tf_op jit(solution)/shard_map/ppermute | solution.py:36
  35.2 2.7 %collective-permute-start.15 = (f16[144,512]{1,0:T(8,128)(2,1)S(1)}, f16[144,512]{1,0:T(8,128)(2,1)S(1)}, u32[]{:S(2)}, u32[]{:S(2)}) collective-permute-start(f16[144,512]{1,0:T(8,128)(2,1)S(1)} %convert_element_type.20), channel_id=1, source_target_pairs={{0,2},{1,3},{2,0},{3,1},{4,6},{5,7},{6,4},{7,5},{8,10},{9,11},{10,... | collective-permute-start | bytes 442376 | tf_op jit(solution)/shard_map/ppermute | solution.py:36
  38.1 1.6 %collective-permute-start.16 = (f16[144,512]{1,0:T(8,128)(2,1)S(1)}, f16[144,512]{1,0:T(8,128)(2,1)S(1)}, u32[]{:S(2)}, u32[]{:S(2)}) collective-permute-start(f16[144,512]{1,0:T(8,128)(2,1)S(1)} %convert_element_type.22), channel_id=1, source_target_pairs={{0,1},{1,0},{2,3},{3,2},{4,5},{5,4},{6,7},{7,6},{8,9},{9,8},{10,11... | collective-permute-start | bytes 442376 | tf_op jit(solution)/shard_map/ppermute | solution.py:36
  39.8 1.8 %product.2 = (f32[128,512]{1,0:T(8,128)S(1)}, bf16[128,4096]{1,0:T(8,128)(2,1)}) custom-call(bf16[128,4096]{1,0:T(8,128)(2,1)S(1)} %copy-done, bf16[128,512]{1,0:T(8,128)(2,1)S(1)} %copy-done.2, f32[128,512]{1,0:T(8,128)S(1)} %get-tuple-element.34.acc, bf16[128,4096]{1,0:T(8,128)(2,1)} %get-tuple-element.35._, ...), custom_call_target="tpu_custom_call", output_to_operand_aliasing={{1}: (3, {})} | custom-call | bytes 1024 | tf_op jit(solution)/shard_map/product/pallas_call | solution.py:244
  42.3 2.8 %collective-permute-done.15 = f16[144,512]{1,0:T(8,128)(2,1)S(1)} collective-permute-done((f16[144,512]{1,0:T(8,128)(2,1)S(1)}, f16[144,512]{1,0:T(8,128)(2,1)S(1)}, u32[]{:S(2)}, u32[]{:S(2)}) %collective-permute-start.15) | collective-permute-done | bytes 147488 | tf_op jit(solution)/shard_map/ppermute | solution.py:36
  45.7 1.2 %product.3 = (bf16[128,512]{1,0:T(8,128)(2,1)}, bf16[128,4096]{1,0:T(8,128)(2,1)}, f32[128,512]{1,0:T(8,128)}) custom-call(bf16[128,4096]{1,0:T(8,128)(2,1)S(1)} %copy-done, bf16[128,512]{1,0:T(8,128)(2,1)S(1)} %copy-done.2, f32[128,512]{1,0:T(8,128)S(1)} %get-tuple-element.46.acc, ...), custom_call_target="tpu_custom_call", output_to_operand_aliasing={{1}: (3, {})} | custom-call | bytes 1024 | tf_op jit(solution)/shard_map/product/pallas_call | solution.py:244
  (42 shorter events, 3.5 us)
Async XLA Ops:
  0.6 6.1 %copy-start.1 = (bf16[1024,512]{1,0:T(8,128)(2,1)S(1)}, bf16[1024,512]{1,0:T(8,128)(2,1)}, u32[]{:S(2)}) copy-start(bf16[1024,512]{1,0:T(8,128)(2,1)} %w) | copy-start | bytes 3145732
  2.1 14.0 %copy-start = (bf16[128,4096]{1,0:T(8,128)(2,1)S(1)}, bf16[128,4096]{1,0:T(8,128)(2,1)}, u32[]{:S(2)}) copy-start(bf16[128,4096]{1,0:T(8,128)(2,1)} %act.9) | copy-start | bytes 3145732
  2.1 14.0 %copy-start.2 = (bf16[128,512]{1,0:T(8,128)(2,1)S(1)}, bf16[128,512]{1,0:T(8,128)(2,1)}, u32[]{:S(2)}) copy-start(bf16[128,512]{1,0:T(8,128)(2,1)} %cot.9) | copy-start | bytes 393220
  2.2 21.4 %collective-permute-start = (bf16[128,1536]{1,0:T(8,128)(2,1)S(1)}, bf16[128,1536]{1,0:T(8,128)(2,1)S(1)}, u32[]{:S(2)}, u32[]{:S(2)}) collective-permute-start(bf16[128,1536]{1,0:T(8,128)(2,1)S(1)} %get-tuple-element.30), channel_id=1, source_target_pairs={{0,8},{1,9},{2,10},{3,11},{4,12},{5,13},{6,14},{7,15},{8,0},{9,1},... | collective-permute-start | bytes 1179656 | tf_op jit(solution)/shard_map/ppermute | solution.py:36
  5.2 19.4 %collective-permute-start.4 = (bf16[128,1536]{1,0:T(8,128)(2,1)S(1)}, bf16[128,1536]{1,0:T(8,128)(2,1)S(1)}, u32[]{:S(2)}, u32[]{:S(2)}) collective-permute-start(bf16[128,1536]{1,0:T(8,128)(2,1)S(1)} %get-tuple-element.37), channel_id=1, source_target_pairs={{0,16},{1,17},{2,18},{3,19},{4,20},{5,21},{6,22},{7,23},{8,24},{9,... | collective-permute-start | bytes 1179656 | tf_op jit(solution)/shard_map/ppermute | solution.py:36
  6.7 18.4 %collective-permute-start.5 = (bf16[128,1536]{1,0:T(8,128)(2,1)S(1)}, bf16[128,1536]{1,0:T(8,128)(2,1)S(1)}, u32[]{:S(2)}, u32[]{:S(2)}) collective-permute-start(bf16[128,1536]{1,0:T(8,128)(2,1)S(1)} %get-tuple-element.38), channel_id=1, source_target_pairs={{0,24},{1,25},{2,26},{3,27},{4,28},{5,29},{6,30},{7,31},{8,16},{9,... | collective-permute-start | bytes 1179656 | tf_op jit(solution)/shard_map/ppermute | solution.py:36
  6.8 8.7 %collective-permute-start.1 = (bf16[128,512]{1,0:T(8,128)(2,1)S(1)}, bf16[128,512]{1,0:T(8,128)(2,1)S(1)}, u32[]{:S(2)}, u32[]{:S(2)}) collective-permute-start(bf16[128,512]{1,0:T(8,128)(2,1)S(1)} %own_slice.1), channel_id=1, source_target_pairs={{0,2},{1,3},{2,0},{3,1},{4,6},{5,7},{6,4},{7,5},{8,10},{9,11},{10,... | collective-permute-start | bytes 393224 | tf_op jit(solution)/shard_map/ppermute | solution.py:36
  9.9 7.4 %collective-permute-start.2 = (bf16[128,512]{1,0:T(8,128)(2,1)S(1)}, bf16[128,512]{1,0:T(8,128)(2,1)S(1)}, u32[]{:S(2)}, u32[]{:S(2)}) collective-permute-start(bf16[128,512]{1,0:T(8,128)(2,1)S(1)} %own_slice.1), channel_id=1, source_target_pairs={{0,1},{1,0},{2,3},{3,2},{4,5},{5,4},{6,7},{7,6},{8,9},{9,8},{10,11... | collective-permute-start | bytes 393224 | tf_op jit(solution)/shard_map/ppermute | solution.py:36
  15.5 5.0 %collective-permute-start.3 = (bf16[128,512]{1,0:T(8,128)(2,1)S(1)}, bf16[128,512]{1,0:T(8,128)(2,1)S(1)}, u32[]{:S(2)}, u32[]{:S(2)}) collective-permute-start(bf16[128,512]{1,0:T(8,128)(2,1)S(1)} %collective-permute-done.1.refs_0_), channel_id=1, source_target_pairs={{0,1},{1,0},{2,3},{3,2},{4,5},{5,4},{6,7},{7,6},{8,9},{9,8},{10,11... | collective-permute-start | bytes 393224 | tf_op jit(solution)/shard_map/ppermute | solution.py:36
  20.5 10.8 %collective-permute-start.7 = (bf16[384,512]{1,0:T(8,128)(2,1)S(1)}, bf16[384,512]{1,0:T(8,128)(2,1)S(1)}, u32[]{:S(2)}, u32[]{:S(2)}) collective-permute-start(bf16[384,512]{1,0:T(8,128)(2,1)S(1)} %stack.3.refs_0_), channel_id=1, source_target_pairs={{0,8},{1,9},{2,10},{3,11},{4,12},{5,13},{6,14},{7,15},{8,0},{9,1},... | collective-permute-start | bytes 1179656 | tf_op jit(solution)/shard_map/ppermute | solution.py:36
  22.1 10.6 %collective-permute-start.8 = (bf16[384,512]{1,0:T(8,128)(2,1)S(1)}, bf16[384,512]{1,0:T(8,128)(2,1)S(1)}, u32[]{:S(2)}, u32[]{:S(2)}) collective-permute-start(bf16[384,512]{1,0:T(8,128)(2,1)S(1)} %stack.3.refs_0_), channel_id=1, source_target_pairs={{0,16},{1,17},{2,18},{3,19},{4,20},{5,21},{6,22},{7,23},{8,24},{9,... | collective-permute-start | bytes 1179656 | tf_op jit(solution)/shard_map/ppermute | solution.py:36
  25.5 1.6 %collective-permute-start.6 = (f32[128,512]{1,0:T(8,128)S(1)}, f32[128,512]{1,0:T(8,128)S(1)}, u32[]{:S(2)}, u32[]{:S(2)}) collective-permute-start(f32[128,512]{1,0:T(8,128)S(1)} %get-tuple-element.41), channel_id=1, source_target_pairs={{0,4},{1,5},{2,6},{3,7},{4,0},{5,1},{6,2},{7,3},{8,12},{9,13},{10,... | collective-permute-start | bytes 786440 | tf_op jit(solution)/shard_map/ppermute | solution.py:36
  26.2 8.8 %collective-permute-start.13 = (f32[384,512]{1,0:T(8,128)S(1)}, f32[384,512]{1,0:T(8,128)S(1)}, u32[]{:S(2)}, u32[]{:S(2)}) collective-permute-start(f32[384,512]{1,0:T(8,128)S(1)} %get-tuple-element.48), channel_id=1, source_target_pairs={{0,4},{1,5},{2,6},{3,7},{4,0},{5,1},{6,2},{7,3},{8,12},{9,13},{10,... | collective-permute-start | bytes 2359304 | tf_op jit(solution)/shard_map/ppermute | solution.py:36
  27.3 7.6 %collective-permute-start.14 = (f16[144,512]{1,0:T(8,128)(2,1)S(1)}, f16[144,512]{1,0:T(8,128)(2,1)S(1)}, u32[]{:S(2)}, u32[]{:S(2)}) collective-permute-start(f16[144,512]{1,0:T(8,128)(2,1)S(1)} %convert_element_type.18), channel_id=1, source_target_pairs={{0,1},{1,0},{2,3},{3,2},{4,5},{5,4},{6,7},{7,6},{8,9},{9,8},{10,11... | collective-permute-start | bytes 442376 | tf_op jit(solution)/shard_map/ppermute | solution.py:36
  32.8 5.1 %collective-permute-start.9 = (bf16[1152,512]{1,0:T(8,128)(2,1)S(1)}, bf16[1152,512]{1,0:T(8,128)(2,1)S(1)}, u32[]{:S(2)}, u32[]{:S(2)}) collective-permute-start(bf16[1152,512]{1,0:T(8,128)(2,1)S(1)} %stack.4.mine), channel_id=1, source_target_pairs={{0,4},{1,5},{2,6},{3,7},{4,0},{5,1},{6,2},{7,3},{8,12},{9,13},{10,... | collective-permute-start | bytes 3538952 | tf_op jit(solution)/shard_map/ppermute | solution.py:36
  32.8 8.8 %collective-permute-start.10 = (bf16[192,512]{1,0:T(8,128)(2,1)S(1)}, bf16[192,512]{1,0:T(8,128)(2,1)S(1)}, u32[]{:S(2)}, u32[]{:S(2)}) collective-permute-start(bf16[192,512]{1,0:T(8,128)(2,1)S(1)} %slice.9), channel_id=1, source_target_pairs={{0,8},{1,9},{2,10},{3,11},{4,12},{5,13},{6,14},{7,15},{8,0},{9,1},... | collective-permute-start | bytes 589832 | tf_op jit(solution)/shard_map/ppermute | solution.py:36
  34.1 7.5 %collective-permute-start.11 = (bf16[192,512]{1,0:T(8,128)(2,1)S(1)}, bf16[192,512]{1,0:T(8,128)(2,1)S(1)}, u32[]{:S(2)}, u32[]{:S(2)}) collective-permute-start(bf16[192,512]{1,0:T(8,128)(2,1)S(1)} %slice.10), channel_id=1, source_target_pairs={{0,16},{1,17},{2,18},{3,19},{4,20},{5,21},{6,22},{7,23},{8,24},{9,... | collective-permute-start | bytes 589832 | tf_op jit(solution)/shard_map/ppermute | solution.py:36
  35.2 9.9 %collective-permute-start.15 = (f16[144,512]{1,0:T(8,128)(2,1)S(1)}, f16[144,512]{1,0:T(8,128)(2,1)S(1)}, u32[]{:S(2)}, u32[]{:S(2)}) collective-permute-start(f16[144,512]{1,0:T(8,128)(2,1)S(1)} %convert_element_type.20), channel_id=1, source_target_pairs={{0,2},{1,3},{2,0},{3,1},{4,6},{5,7},{6,4},{7,5},{8,10},{9,11},{10,... | collective-permute-start | bytes 442376 | tf_op jit(solution)/shard_map/ppermute | solution.py:36
  38.1 7.5 %collective-permute-start.16 = (f16[144,512]{1,0:T(8,128)(2,1)S(1)}, f16[144,512]{1,0:T(8,128)(2,1)S(1)}, u32[]{:S(2)}, u32[]{:S(2)}) collective-permute-start(f16[144,512]{1,0:T(8,128)(2,1)S(1)} %convert_element_type.22), channel_id=1, source_target_pairs={{0,1},{1,0},{2,3},{3,2},{4,5},{5,4},{6,7},{7,6},{8,9},{9,8},{10,11... | collective-permute-start | bytes 442376 | tf_op jit(solution)/shard_map/ppermute | solution.py:36
  41.6 4.0 %collective-permute-start.17 = (f32[8,128]{1,0:T(8,128)S(1)}, f32[8,128]{1,0:T(8,128)S(1)}, u32[]{:S(2)}, u32[]{:S(2)}) collective-permute-start(f32[8,128]{1,0:T(8,128)S(1)} %slice.11), channel_id=1, source_target_pairs={{0,4},{1,5},{2,6},{3,7},{4,0},{5,1},{6,2},{7,3},{8,12},{9,13},{10,... | collective-permute-start | bytes 12296 | tf_op jit(solution)/shard_map/ppermute | solution.py:36
  41.7 4.0 %collective-permute-start.12 = (bf16[384,512]{1,0:T(8,128)(2,1)S(1)}, bf16[384,512]{1,0:T(8,128)(2,1)S(1)}, u32[]{:S(2)}, u32[]{:S(2)}) collective-permute-start(bf16[384,512]{1,0:T(8,128)(2,1)S(1)} %stack.5.mine), channel_id=1, source_target_pairs={{0,4},{1,5},{2,6},{3,7},{4,0},{5,1},{6,2},{7,3},{8,12},{9,13},{10,... | collective-permute-start | bytes 1179656 | tf_op jit(solution)/shard_map/ppermute | solution.py:36
